TPU v7x, 128 devices: a whole 4x4x4 slice. The times are simulated.
128 devices in a mesh: wide: 16 (over x, y), pair: 8 (over z, core).
Axes of the slice: x: 4, y: 4, z: 4, core: 2. Of those that a mesh axis runs over, the one named last changes fastest.
Arguments:
- embeddings: float32 [65536, 1024], P(('wide', 'pair')), may hold values from -24 to 24
- cluster_ids: int32 [65536], P(('wide', 'pair')), may hold values from 0 to 15, as said below
Outputs:
- best_match: float32 [65536], P(('wide', 'pair'))
Inputs may be any that keep to these rules, and one draw needn't show every extreme that they name: `cluster_ids`: the owner of cluster c is c. Among the 512 rows of one device, at most 64 name clusters of any one owner, and on every device some owner has exactly 64.
All inputs are finite; a program needn't handle non-finite values.
Results may differ from a plain program's by a relative error of at most 0.0003.
Values may be sent and summed in bfloat16 or wider, within the bound.
No kernel may reach another device: no remote copies, remote signals or barrier semaphores. Data moves between devices by JAX's collectives and lax.ppermute only.
A program may use at most 64 MiB of HBM per device.

v0:
```python
import jax
import jax.numpy as jnp
from jax import lax
from jax.sharding import PartitionSpec as P

CL_OWN = 1


EPSILON = 1e-06


def unit_rows(values):
    return (values * lax.rsqrt(jnp.sum(values * values, axis=1, keepdims=True) + EPSILON)).astype(
        jnp.bfloat16
    )


def similar(left_rows, right_rows):
    return lax.dot_general(
        left_rows, right_rows, (((1,), (1,)), ((), ())), preferred_element_type=jnp.float32
    )


def masked(scores, left_ids, right_ids, keep_mask):
    same = (left_ids[:, None] == right_ids[None, :]) & (left_ids[:, None] >= 0) & keep_mask
    return jnp.where(same, scores, jnp.float32(-1.0))


def per_device(embeddings, cluster_ids):
    feature_width = embeddings.shape[1]
    rows_here = embeddings.shape[0]
    wide_count = lax.axis_size("wide")
    capacity = 2 * rows_here // wide_count
    owners = cluster_ids // CL_OWN
    onehot = (owners[:, None] == jnp.arange(wide_count, dtype=jnp.int32)[None, :]).astype(jnp.int32)
    member_rank = jnp.sum(jnp.cumsum(onehot, axis=0) * onehot, axis=1) - 1
    slot_index = owners * capacity + member_rank
    outgoing = (
        jnp.zeros((wide_count * capacity, feature_width), embeddings.dtype)
        .at[slot_index]
        .set(embeddings)
    )
    outgoing = outgoing.reshape(wide_count, capacity, feature_width)
    outgoing_ids = jnp.full((wide_count * capacity,), -1, jnp.int32).at[slot_index].set(cluster_ids)
    outgoing_ids = outgoing_ids.reshape(wide_count, capacity)
    arrived, arrived_ids = (
        lax.all_to_all(outgoing, "wide", split_axis=0, concat_axis=0, tiled=True),
        lax.all_to_all(outgoing_ids, "wide", split_axis=0, concat_axis=0, tiled=True),
    )
    members = unit_rows(arrived.reshape(-1, feature_width))
    member_ids = arrived_ids.reshape(-1)
    buffer_rows = members.shape[0]
    position = jnp.arange(buffer_rows, dtype=jnp.int32)
    pair_index = lax.axis_index("pair")
    floor_values = jnp.full((buffer_rows,), -1.0, jnp.float32)
    own_global = pair_index * buffer_rows + position
    tile_rows = lax.all_gather(members, "pair", axis=0, tiled=True)
    tile_ids = lax.all_gather(member_ids, "pair", axis=0, tiled=True)
    columns = jnp.arange(tile_rows.shape[0], dtype=jnp.int32)
    keep_mask = own_global[:, None] != columns[None, :]
    scores = masked(similar(members, tile_rows), member_ids, tile_ids, keep_mask)
    best_match = jnp.maximum(floor_values, jnp.max(scores, axis=1))
    back = lax.all_to_all(
        best_match.reshape(wide_count, capacity), "wide", split_axis=0, concat_axis=0, tiled=True
    )
    return back.reshape(-1)[slot_index]


def solution(mesh):
    in_specs = (P(("wide", "pair"), None), P(("wide", "pair")))
    out_specs = P(("wide", "pair"))
    return jax.shard_map(
        per_device, mesh=mesh, in_specs=in_specs, out_specs=out_specs, check_vma=False
    )
```

profile of v0, /device:TPU:0, one launch (start us, length us, event | category | flops | bytes accessed | tf_op | source)
XLA Modules:
  0.0 216.9 jit_solution(1922062307074453348)
XLA Ops:
  6.5 0.0 all-gather.2.cloned.1.call-start
  6.5 0.7 fusion.5
  7.2 1.1 reduce-window.6
  8.4 0.2 slice_reduce_fusion
  8.6 0.8 fusion.4
  9.4 0.7 compare_select_fusion
  10.1 5.4 %scatter_custom_fusion.1 = f32[1024,1024]{1,0:T(8,128)} fusion(s32[512]{0:T(512)S(1)} %compare_select_fusion, f32[512,1024]{1,0:T(8,128)} %param.2, f32[]{:T(128)} %constant.18.clone.1), kind=kCustom, calls=%fused_computation.8 | custom fusion | bytes 4194816 | tf_op jit(solution)/shard_map/scatter | solution.py:41
  15.5 57.8 %all_to_all.20 = f32[16,64,1024]{2,1,0:T(8,128)S(1)} all-to-all(f32[16,64,1024]{2,1,0:T(8,128)} %bitcast.21), channel_id=1, replica_groups=mesh['wide'=16,'pair'=8] {'wide'}, dimensions={0} | all-to-all | bytes 8388608 | tf_op jit(solution)/shard_map/all_to_all | solution.py:47
  73.4 0.0 copy-start
  73.4 1.9 copy-done
  75.3 0.3 multiply_reduce_fusion
  75.6 0.1 rsqrt.12
  75.7 3.8 %bitcast_multiply_fusion = bf16[1024,1024]{1,0:T(8,128)(2,1)} fusion(f32[16,64,1024]{2,1,0:T(8,128)} %copy-done, f32[1024]{0:T(1024)S(1)} %rsqrt.12), kind=kLoop, calls=%fused_computation.6 | loop fusion | flops 2097152 | bytes 6295552 | tf_op jit(solution)/shard_map/mul | solution.py:13
  79.5 0.0 all-gather.2.cloned.1.call-update
  79.6 2.6 %scatter_custom_fusion = s32[1024]{0:T(1024)S(1)} fusion(s32[512]{0:T(512)S(1)} %compare_select_fusion, s32[512]{0:T(512)} %param.3, s32[]{:T(128)} %constant.13.clone.1), kind=kCustom, calls=%fused_computation.24 | custom fusion | bytes 4608 | tf_op jit(solution)/shard_map/scatter | solution.py:44
  82.2 0.7 all_to_all.13
  82.8 4.2 %all-to-all-start = ((s32[16,1,64]{2,1,0:T(1,128)}), s32[16,1,64]{2,1,0:T(1,128)S(1)}, u32[]{:S(2)}, u32[]{:S(2)}) async-start(s32[16,1,64]{2,1,0:T(1,128)} %all_to_all.13), calls=%async_computation | async-start | bytes 16384 | tf_op jit(solution)/shard_map/all_to_all | solution.py:48
  87.1 7.5 %all-to-all-done = s32[16,1,64]{2,1,0:T(1,128)S(1)} async-done(((s32[16,1,64]{2,1,0:T(1,128)}), s32[16,1,64]{2,1,0:T(1,128)S(1)}, u32[]{:S(2)}, u32[]{:S(2)}) %all-to-all-start) | async-done | bytes 4128 | tf_op jit(solution)/shard_map/all_to_all | solution.py:48
  94.6 0.5 broadcast.74
  95.1 0.7 reduce.9
  95.8 0.1 eq.45
  95.9 14.2 %all_gather.6 = s32[8192]{0:T(1024)S(1)} all-gather(s32[1024]{0:T(1024)S(1)} %eq.45), channel_id=1, replica_groups=mesh['wide'=16,'pair'=8] {'pair'}, dimensions={0}, use_global_device_ids=true | all-gather | bytes 36864 | tf_op jit(solution)/shard_map/all_gather | solution.py:58
  110.1 54.5 %all-gather.2.cloned.1.call-done = bf16[8192,1024]{1,0:T(8,128)(2,1)} async-done(((bf16[1024,1024]{1,0:T(8,128)(2,1)}), bf16[8192,1024]{1,0:T(8,128)(2,1)}) %all-gather.2.cloned.1.call-update) | async-done | bytes 16777232 | tf_op jit(solution)/shard_map/all_gather | solution.py:57
  164.6 25.8 %select_reduce_fusion = f32[1024]{0:T(1024)S(1)} fusion(bf16[1024,1024]{1,0:T(8,128)(2,1)} %bitcast_multiply_fusion, bf16[8192,1024]{1,0:T(8,128)(2,1)} %all-gather.2.cloned.1.call-done, s32[1024]{0:T(1024)S(1)} %iota_add_fusion, s32[8192]{0:T(1024)S(1)} %all_gather.6, s32[1024]{0:T(1024)S(1)} %eq.45, pred[1024]{0:T(1024)(128)(4,1)S(1)} %broadcast_compare_fusion), kind=kOutput, calls=%fused_computation.3 | convolution fusion | flops 17230200832 | bytes 18920448 | tf_op jit(solution)/shard_map/dot_general | solution.py:19
  190.4 0.7 max_broadcast_in_dim.15
  191.0 6.8 %all-to-all-start.2 = ((f32[16,1,64]{2,1,0:T(1,128)}), f32[16,1,64]{2,1,0:T(1,128)S(1)}, u32[]{:S(2)}, u32[]{:S(2)}) async-start(f32[16,1,64]{2,1,0:T(1,128)} %max_broadcast_in_dim.15), calls=%async_computation.2 | async-start | bytes 16384 | tf_op jit(solution)/shard_map/all_to_all | solution.py:63
  197.9 7.5 %all-to-all-done.2 = f32[16,1,64]{2,1,0:T(1,128)S(1)} async-done(((f32[16,1,64]{2,1,0:T(1,128)}), f32[16,1,64]{2,1,0:T(1,128)S(1)}, u32[]{:S(2)}, u32[]{:S(2)}) %all-to-all-start.2) | async-done | bytes 4128 | tf_op jit(solution)/shard_map/all_to_all | solution.py:63
  205.4 0.5 broadcast.75
  205.9 0.7 reduce.10
  206.6 0.1 reshape.79
  206.7 3.4 %gather_fusion = f32[512]{0:T(512)} fusion(f32[1024]{0:T(1024)S(1)} %reshape.79, s32[1024]{0:T(1024)S(1)} %pad_clamp_fusion), kind=kCustom, calls=%fused_computation | custom fusion | bytes 6144 | tf_op jit(solution)/shard_map/gather | solution.py:66
  (7 shorter events, 0.1 us)
Async XLA Ops:
  6.5 158.0 %all-gather.2.cloned.1.call-start = ((), (), s32[]{:S(2)}) async-start(), calls=%async_computation.3 | async-start | bytes 18874368 | tf_op jit(solution)/shard_map/all_gather | solution.py:57
  73.4 1.9 copy-start
  82.8 11.8 %all-to-all-start = ((s32[16,1,64]{2,1,0:T(1,128)}), s32[16,1,64]{2,1,0:T(1,128)S(1)}, u32[]{:S(2)}, u32[]{:S(2)}) async-start(s32[16,1,64]{2,1,0:T(1,128)} %all_to_all.13), calls=%async_computation | async-start | bytes 16384 | tf_op jit(solution)/shard_map/all_to_all | solution.py:48
  191.0 14.4 %all-to-all-start.2 = ((f32[16,1,64]{2,1,0:T(1,128)}), f32[16,1,64]{2,1,0:T(1,128)S(1)}, u32[]{:S(2)}, u32[]{:S(2)}) async-start(f32[16,1,64]{2,1,0:T(1,128)} %max_broadcast_in_dim.15), calls=%async_computation.2 | async-start | bytes 16384 | tf_op jit(solution)/shard_map/all_to_all | solution.py:63
Sparse Core Ops, SparseCore 0:
  79.7 84.8 all-gather.1
where the time goes:
time: 217 us
  blocking collectives  72 us (33%)
  waiting for transfers between devices  69.6 us (32%)
  matrix products  25.8 us (12%)
  local copies, waits for them, and re-layouts  16.2 us (7%)
  between operations  13.5 us (6%)
  starting transfers between devices  11 us (5%)
  other arithmetic  8.86 us (4%)
    all_to_all x1, blocking collectives, per_device(): lax.all_to_all(outgoing, 'wide', split_axis=0, concat_axis=0, tiled=True)  57.8 us
    all_gather x1, waiting for transfers between devices, per_device(): tile_rows = lax.all_gather(members, 'pair', axis=0, tiled=True)  54.5 us
    dot_general x1, matrix products, similar(): lax.dot_general(left_rows, right_rows, (((1,), (1,)), ((), ())), preferre...  25.8 us
    all_gather x1, blocking collectives, per_device(): tile_ids = lax.all_gather(member_ids, 'pair', axis=0, tiled=True)  14.2 us
    all_to_all x1, waiting for transfers between devices, per_device(): lax.all_to_all(best_match.reshape(wide_count, capacity), 'wide', split_ax...  7.55 us
    all_to_all x1, waiting for transfers between devices, per_device(): lax.all_to_all(outgoing_ids, 'wide', split_axis=0, concat_axis=0, tiled=T...  7.55 us
    all_to_all x1, starting transfers between devices, per_device(): lax.all_to_all(best_match.reshape(wide_count, capacity), 'wide', split_ax...  6.81 us
    scatter x1, local copies, waits for them, and re-layouts, per_device(): outgoing = jnp.zeros((wide_count * capacity, feature_width), embeddings.d...  5.43 us
  transfers between devices with their start and end apart: 3, of which 3 were waited for; matrix products, arithmetic and copies ran while one was open for 2% of the time, Pallas kernels for 0%

commit v1 on v0

v1 whole, which is shorter than its diff:
```python
import functools

import jax
import jax.numpy as jnp
from jax import lax
from jax.experimental import pallas as pl
from jax.experimental.pallas import tpu as pltpu
from jax.sharding import PartitionSpec as P

EPSILON = 1e-06
OWNERS = 16
CAP = 64
HALF = CAP // 2
CHUNK = OWNERS * HALF
LOW = -1e30
MARK = 2.0
F32 = jnp.float32
BF16 = jnp.bfloat16


def params():
    return pltpu.CompilerParams(vmem_limit_bytes=40 * 1024 * 1024)


def cost(flops, bytes_accessed):
    return pl.CostEstimate(flops=flops, bytes_accessed=bytes_accessed, transcendentals=0)


def iota(shape, dim):
    return lax.broadcasted_iota(jnp.int32, shape, dim)


def prep_kernel(x_ref, ids_ref, first_ref, second_ref, meta_ref):
    rows = x_ref.shape[0]
    x = x_ref[...]
    unit = (x * lax.rsqrt(jnp.sum(x * x, axis=1, keepdims=True) + EPSILON)).astype(BF16)
    ids = ids_ref[...]
    onehot = iota((OWNERS, rows), 0) == ids
    upto = (iota((rows, rows), 0) <= iota((rows, rows), 1)).astype(BF16)
    counts = jnp.dot(onehot.astype(BF16), upto, preferred_element_type=F32)
    rank = jnp.sum(jnp.where(onehot, counts, 0.0), axis=0, keepdims=True).astype(jnp.int32) - 1
    meta_ref[...] = jnp.where(iota((8, rows), 0) == 0, ids, rank)
    ones = jnp.ones((rows, 128), BF16)
    for half, out_ref in ((0, first_ref), (1, second_ref)):
        inside = (rank >= half * HALF) & (rank < (half + 1) * HALF)
        slot = jnp.where(inside, ids * HALF + rank - half * HALF, -1)
        place = (iota((CHUNK, rows), 0) == slot).astype(BF16)
        moved = jnp.dot(place, unit, preferred_element_type=F32)
        taken = jnp.dot(place, ones, preferred_element_type=F32)
        out_ref[...] = moved.astype(BF16)
        mark = jnp.where(iota((CHUNK, 128), 1) == 0, MARK * (1.0 - taken), 0.0)
        out_ref[:, 0:128] = (moved[:, 0:128] + mark).astype(BF16)


def prep(embeddings, ids):
    rows, width = embeddings.shape
    return pl.pallas_call(
        prep_kernel,
        out_shape=(
            jax.ShapeDtypeStruct((CHUNK, width), BF16),
            jax.ShapeDtypeStruct((CHUNK, width), BF16),
            jax.ShapeDtypeStruct((8, rows), jnp.int32),
        ),
        compiler_params=params(),
        cost_estimate=cost(4 * CHUNK * rows * width, 8 * CHUNK * width),
        name="prep",
    )(embeddings, ids)


def pair_kernel(units, n_blocks, n_before, wanted, *refs):
    blocks = refs[:n_blocks]
    before = refs[n_blocks : n_blocks + n_before]
    outs = refs[n_blocks + n_before : n_blocks + n_before + len(wanted)]
    lane_bias, row_bias, over_lanes, over_rows = refs[n_blocks + n_before + len(wanted) :]
    tile = 256
    for b, block in enumerate(blocks):
        head = block[:, 0:128].astype(F32)
        bias = jnp.where(head[:, 0:1] > 1.5, LOW, 0.0)
        bias = jnp.broadcast_to(bias, head.shape)
        lane_bias[b] = bias
        row_bias[b] = jnp.transpose(bias)[0:8, :]
        over_lanes[b] = jnp.full(head.shape, LOW, F32)
        over_rows[b] = jnp.full((8, head.shape[0]), LOW, F32)
    for left, right, mode in units:
        n_left, n_right = blocks[left].shape[0], blocks[right].shape[0]

        def step(t, carry, left=left, right=right, mode=mode, n_left=n_left):
            at = pl.ds(pl.multiple_of(t * tile, tile), tile)
            scores = lax.dot_general(
                blocks[left][...], blocks[right][at, :], (((1,), (1,)), ((), ())),
                preferred_element_type=F32,
            )
            masked = scores + row_bias[right, 0:1, at]
            if mode == "self":
                same = iota(scores.shape, 0) == iota(scores.shape, 1) + t * tile
                masked = jnp.where(same, LOW, masked)
            best = masked[:, 0:128]
            for g in range(1, tile // 128):
                best = jnp.maximum(best, masked[:, g * 128 : (g + 1) * 128])
            over_lanes[left] = jnp.maximum(over_lanes[left], best)
            if mode == "both":
                bias = lane_bias[left]
                for g in range(tile // 128):
                    part = scores[:, g * 128 : (g + 1) * 128] + bias
                    part = jnp.max(part.reshape(n_left // 8, 8, 128), axis=0)
                    here = pl.ds(pl.multiple_of(t * tile + g * 128, 128), 128)
                    over_rows[right, :, here] = jnp.maximum(over_rows[right, :, here], part)
            return carry

        lax.fori_loop(0, n_right // tile, step, 0)
    for (first, second, earlier), out in zip(wanted, outs):
        parts = []
        for b in (first, second):
            if b is None:
                parts.append(jnp.full((1, CHUNK), LOW, F32))
                continue
            value = jnp.max(jnp.transpose(over_lanes[b]), axis=0, keepdims=True)
            parts.append(jnp.maximum(value, jnp.max(over_rows[b], axis=0, keepdims=True)))
        for i, part in enumerate(parts):
            at = slice(i * CHUNK, (i + 1) * CHUNK)
            if earlier is not None:
                part = jnp.maximum(part, before[earlier][:, at])
            out[:, at] = part


def pairs(units, blocks, before, wanted, name):
    n = len(blocks)
    rows, width = blocks[0].shape
    return pl.pallas_call(
        functools.partial(pair_kernel, units, n, len(before), wanted),
        out_shape=tuple(jax.ShapeDtypeStruct((1, 2 * CHUNK), F32) for _ in wanted),
        scratch_shapes=[
            pltpu.VMEM((n, rows, 128), F32),
            pltpu.VMEM((n, 8, rows), F32),
            pltpu.VMEM((n, rows, 128), F32),
            pltpu.VMEM((n, 8, rows), F32),
        ],
        compiler_params=params(),
        cost_estimate=cost(2 * len(units) * rows * rows * width, 2 * n * rows * width),
        name=name,
    )(*blocks, *before)


def join_kernel(own_ref, a_ref, b_ref, c_ref, out_ref):
    best = jnp.maximum(jnp.maximum(own_ref[...], a_ref[...]), jnp.maximum(b_ref[...], c_ref[...]))
    best = jnp.maximum(best, -1.0)
    out_ref[...] = jnp.zeros(out_ref.shape, F32)
    for source in range(OWNERS):
        for half in range(2):
            at = half * CHUNK + source * HALF
            out_ref[source * 8 : source * 8 + 1, half * HALF : (half + 1) * HALF] = best[:, at : at + HALF]


def join(own, a, b, c):
    return pl.pallas_call(
        join_kernel,
        out_shape=jax.ShapeDtypeStruct((OWNERS * 8, 128), F32),
        compiler_params=params(),
        name="join",
    )(own, a, b, c)


def pick_kernel(back_ref, meta_ref, out_ref):
    rows = meta_ref.shape[1]
    ids = meta_ref[0:1, :]
    rank = meta_ref[1:2, :]
    onehot = (iota((OWNERS, rows), 0) == ids).astype(BF16)
    at_rank = iota((128, rows), 0) == rank
    rest = jnp.concatenate([back_ref[s * 8 : s * 8 + 1, :] for s in range(OWNERS)], axis=0)
    total = jnp.zeros((1, rows), F32)
    for _ in range(3):
        part = rest.astype(BF16)
        rest = rest - part.astype(F32)
        spread = lax.dot_general(part, onehot, (((0,), (0,)), ((), ())), preferred_element_type=F32)
        total = total + jnp.sum(jnp.where(at_rank, spread, 0.0), axis=0, keepdims=True)
    out_ref[...] = total


def pick(back, meta):
    return pl.pallas_call(
        pick_kernel,
        out_shape=jax.ShapeDtypeStruct((1, meta.shape[1]), F32),
        compiler_params=params(),
        name="pick",
    )(back, meta)


def swap_cores():
    return [(2 * z + k, 2 * z + 1 - k) for z in range(4) for k in range(2)]


def from_next():
    return [(2 * ((z + 1) % 4) + k, 2 * z + k) for z in range(4) for k in range(2)]


def from_last():
    return [
        (2 * ((z + 3) % 4) + (k if z < 2 else 1 - k), 2 * z + k) for z in range(4) for k in range(2)
    ]


def inverse(perm):
    return [(b, a) for a, b in perm]


def to_owners(block):
    shape = block.shape
    block = block.reshape(OWNERS, HALF, shape[1])
    return lax.all_to_all(block, "wide", split_axis=0, concat_axis=0, tiled=True).reshape(shape)


def along_pair(block, perm):
    return lax.ppermute(block, "pair", perm)


def per_device(embeddings, cluster_ids):
    first, second, meta = prep(embeddings, cluster_ids.reshape(1, -1))
    own_a = to_owners(first)
    own_a, second = lax.optimization_barrier((own_a, second))
    sib_a = along_pair(own_a, swap_cores())
    next_a = along_pair(own_a, from_next())
    last_a = along_pair(own_a, from_last())
    own_b = to_owners(second)
    sib_b = along_pair(own_b, swap_cores())
    next_b = along_pair(own_b, from_next())
    last_b = along_pair(own_b, from_last())
    own, sib, nxt, last = pairs(
        (
            (0, 0, "self"), (0, 1, "both"), (1, 1, "self"),
            (0, 2, "left"), (0, 3, "left"), (1, 2, "left"), (1, 3, "left"),
            (0, 4, "both"), (1, 4, "both"), (2, 4, "both"), (3, 4, "both"), (5, 4, "both"),
        ),
        (own_a, own_b, sib_a, sib_b, next_a, last_a),
        (),
        ((0, 1, None), (2, 3, None), (4, None, None), (5, None, None)),
        "early",
    )
    own, sib, nxt, last = pairs(
        (
            (0, 6, "both"), (1, 6, "both"), (2, 6, "both"), (3, 6, "both"),
            (5, 6, "both"), (7, 4, "both"), (7, 6, "both"),
        ),
        (own_a, own_b, sib_a, sib_b, next_a, last_a, next_b, last_b),
        (own, sib, nxt, last),
        ((0, 1, 0), (2, 3, 1), (4, 6, 2), (5, 7, 3)),
        "late",
    )
    tiles = join(
        own,
        along_pair(sib, swap_cores()),
        along_pair(nxt, inverse(from_next())),
        along_pair(last, inverse(from_last())),
    )
    back = lax.all_to_all(tiles.reshape(OWNERS, 8, 128), "wide", split_axis=0, concat_axis=0, tiled=True)
    return pick(back.reshape(OWNERS * 8, 128), meta).reshape(-1)


def solution(mesh):
    in_specs = (P(("wide", "pair"), None), P(("wide", "pair")))
    out_specs = P(("wide", "pair"))
    return jax.shard_map(
        per_device, mesh=mesh, in_specs=in_specs, out_specs=out_specs, check_vma=False
    )
```

time: 217 us -> 115 us (0.53)
  waiting for transfers between devices: 69.6 us -> 30.1 us
  blocking collectives: 72 us -> 38.4 us
  Pallas kernels: 0 us -> 28.3 us
  matrix products: 25.8 us -> 0 us
  local copies, waits for them, and re-layouts: 16.2 us -> 2.27 us
  between operations: 13.5 us -> 0.04 us
  other arithmetic: 8.86 us -> 0 us
  starting transfers between devices: 11 us -> 15.2 us
    all_gather x1 -> x0, waiting for transfers between devices: 54.5 us -> none  [per_device(): tile_rows = lax.all_gather(members, 'pair', axis=0, tiled=True)]
    pallas_call x0 -> x5, Pallas kernels: none -> 28.3 us  [the longest x2 24.6 us: pairs(): pl.pallas_call(functools.partial(pair_kernel, units, n, len(before), want...]
    dot_general x1 -> x0, matrix products: 25.8 us -> none  [similar(): lax.dot_general(left_rows, right_rows, (((1,), (1,)), ((), ())), preferre...]
    all_to_all x1 -> x2, blocking collectives: 57.8 us -> 38.4 us  [the longest x1 23.8 us: to_owners(): lax.all_to_all(block, 'wide', split_axis=0, concat_axis=0, tiled=True)]
    ppermute x0 -> x9, waiting for transfers between devices: none -> 18.3 us  [along_pair(): return lax.ppermute(block, 'pair', perm)]
    all_gather x1 -> x0, blocking collectives: 14.2 us -> none  [per_device(): tile_ids = lax.all_gather(member_ids, 'pair', axis=0, tiled=True)]
    ppermute x0 -> x9, starting transfers between devices: none -> 11.3 us  [along_pair(): return lax.ppermute(block, 'pair', perm)]
    scatter x2 -> x0, local copies, waits for them, and re-layouts: 8.03 us -> none  [the longest x1 5.43 us: per_device(): outgoing = jnp.zeros((wide_count * capacity, feature_width), embeddings.d...]
  transfers between devices with their start and end apart: 3 -> 10, of which waited for: 3 -> 6; matrix products, arithmetic and copies ran while one was open for 2% -> 0% of each run, Pallas kernels for 0% -> 13%
where the time goes in v1:
time: 115 us; the launch traced here: 114 us
  blocking collectives  38.4 us (33%)
  waiting for transfers between devices  30.1 us (26%)
  Pallas kernels  28.3 us (25%)
  starting transfers between devices  15.2 us (13%)
  local copies, waits for them, and re-layouts  2.27 us (2%)
    pallas_call x2, Pallas kernels, pairs(): pl.pallas_call(functools.partial(pair_kernel, units, n, len(before), want...  24.6 us
    all_to_all x1, blocking collectives, to_owners(): lax.all_to_all(block, 'wide', split_axis=0, concat_axis=0, tiled=True)  23.8 us
    ppermute x9, waiting for transfers between devices, along_pair(): return lax.ppermute(block, 'pair', perm)  18.3 us
    all_to_all x1, blocking collectives, per_device(): lax.all_to_all(tiles.reshape(OWNERS, 8, 128), 'wide', split_axis=0, conca...  14.6 us
    all_to_all x1, waiting for transfers between devices, to_owners(): lax.all_to_all(block, 'wide', split_axis=0, concat_axis=0, tiled=True)  11.7 us
    ppermute x9, starting transfers between devices, along_pair(): return lax.ppermute(block, 'pair', perm)  11.3 us
    all_to_all x1, starting transfers between devices, to_owners(): lax.all_to_all(block, 'wide', split_axis=0, concat_axis=0, tiled=True)  3.84 us
    pallas_call x1, Pallas kernels, prep(): pl.pallas_call(prep_kernel, out_shape=(jax.ShapeDtypeStruct((CHUNK, width...  2.73 us
  transfers between devices with their start and end apart: 10, of which 6 were waited for; matrix products, arithmetic and copies ran while one was open for 0% of the time, Pallas kernels for 13%

profile of v1, /device:TPU:0, one launch (start us, length us, event | category | flops | bytes accessed | tf_op | source)
XLA Modules:
  0.0 114.2 jit_solution(11313257744048019850)
XLA Ops:
  0.0 0.0 copy-start
  0.0 1.6 %copy-done = f32[512,1024]{1,0:T(8,128)S(1)} copy-done((f32[512,1024]{1,0:T(8,128)S(1)}, f32[512,1024]{1,0:T(8,128)}, u32[]{:S(2)}) %copy-start) | copy-done | bytes 2097176
  1.6 0.0 copy-start.1
  1.6 0.7 copy-done.1
  2.3 2.7 %prep.1 = (bf16[512,1024]{1,0:T(8,128)(2,1)S(1)}, bf16[512,1024]{1,0:T(8,128)(2,1)}, s32[8,512]{1,0:T(8,128)S(1)}) custom-call(f32[512,1024]{1,0:T(8,128)S(1)} %copy-done, s32[1,512]{1,0:T(1,128)S(1)} %bitcast.21), custom_call_target="tpu_custom_call" | custom-call | flops 1073741824 | bytes 4194304 | tf_op jit(solution)/shard_map/prep/pallas_call | solution.py:57
  5.0 23.8 %all_to_all.15 = bf16[16,32,1024]{2,1,0:T(8,128)(2,1)S(1)} all-to-all(bf16[16,32,1024]{2,1,0:T(8,128)(2,1)S(1)} %bitcast.18), channel_id=1, replica_groups=mesh['wide'=16,'pair'=8] {'wide'}, dimensions={0} | all-to-all | bytes 2097152 | tf_op jit(solution)/shard_map/all_to_all | solution.py:209
  28.8 3.8 %all-to-all-start.1 = ((bf16[16,32,1024]{2,1,0:T(8,128)(2,1)}), bf16[16,32,1024]{2,1,0:T(8,128)(2,1)S(1)}, u32[]{:S(2)}, u32[]{:S(2)}) async-start(bf16[16,32,1024]{2,1,0:T(8,128)(2,1)} %bitcast.3), calls=%async_computation.1 | async-start | bytes 2097152 | tf_op jit(solution)/shard_map/all_to_all | solution.py:209
  32.6 2.0 %collective-permute-start.3 = (bf16[512,1024]{1,0:T(8,128)(2,1)S(1)}, bf16[512,1024]{1,0:T(8,128)(2,1)S(1)}, u32[]{:S(2)}, u32[]{:S(2)}) collective-permute-start(bf16[512,1024]{1,0:T(8,128)(2,1)S(1)} %bitcast.8), channel_id=1, source_target_pairs={{6,0},{7,1},{0,2},{1,3},{3,4},{2,5},{5,6},{4,7},{14,8},{15,9},{8,1... | collective-permute-start | bytes 3145736 | tf_op jit(solution)/shard_map/ppermute | solution.py:213
  34.6 2.2 %collective-permute-start.2 = (bf16[512,1024]{1,0:T(8,128)(2,1)S(1)}, bf16[512,1024]{1,0:T(8,128)(2,1)}, u32[]{:S(2)}, u32[]{:S(2)}) collective-permute-start(bf16[512,1024]{1,0:T(8,128)(2,1)S(1)} %bitcast.9), channel_id=1, source_target_pairs={{2,0},{3,1},{4,2},{5,3},{6,4},{7,5},{0,6},{1,7},{10,8},{11,9},{12,... | collective-permute-start | bytes 3145736 | tf_op jit(solution)/shard_map/ppermute | solution.py:213
  36.8 0.0 collective-permute-start
  36.8 11.7 %all-to-all-done.1 = bf16[16,32,1024]{2,1,0:T(8,128)(2,1)S(1)} async-done(((bf16[16,32,1024]{2,1,0:T(8,128)(2,1)}), bf16[16,32,1024]{2,1,0:T(8,128)(2,1)S(1)}, u32[]{:S(2)}, u32[]{:S(2)}) %all-to-all-start.1) | async-done | bytes 1048608 | tf_op jit(solution)/shard_map/all_to_all | solution.py:209
  48.5 0.0 collective-permute-start.1
  48.5 1.9 %collective-permute-start.5 = (bf16[512,1024]{1,0:T(8,128)(2,1)S(1)}, bf16[512,1024]{1,0:T(8,128)(2,1)S(1)}, u32[]{:S(2)}, u32[]{:S(2)}) collective-permute-start(bf16[512,1024]{1,0:T(8,128)(2,1)S(1)} %bitcast.14), channel_id=1, source_target_pairs={{6,0},{7,1},{0,2},{1,3},{3,4},{2,5},{5,6},{4,7},{14,8},{15,9},{8,1... | collective-permute-start | bytes 3145736 | tf_op jit(solution)/shard_map/ppermute | solution.py:213
  50.4 10.4 %collective-permute-done.3.refs_5_ = bf16[512,1024]{1,0:T(8,128)(2,1)S(1)} collective-permute-done((bf16[512,1024]{1,0:T(8,128)(2,1)S(1)}, bf16[512,1024]{1,0:T(8,128)(2,1)S(1)}, u32[]{:S(2)}, u32[]{:S(2)}) %collective-permute-start.3) | collective-permute-done | bytes 1048608 | tf_op jit(solution)/shard_map/ppermute | solution.py:213
  60.8 1.4 %collective-permute-start.4 = (bf16[512,1024]{1,0:T(8,128)(2,1)S(1)}, bf16[512,1024]{1,0:T(8,128)(2,1)S(1)}, u32[]{:S(2)}, u32[]{:S(2)}) collective-permute-start(bf16[512,1024]{1,0:T(8,128)(2,1)S(1)} %bitcast.15), channel_id=1, source_target_pairs={{2,0},{3,1},{4,2},{5,3},{6,4},{7,5},{0,6},{1,7},{10,8},{11,9},{12,... | collective-permute-start | bytes 3145736 | tf_op jit(solution)/shard_map/ppermute | solution.py:213
  62.2 0.0 collective-permute-done.2.refs_4_
  62.2 0.0 collective-permute-done.refs_2_
  62.2 0.0 collective-permute-done.1.refs_3_
  62.2 14.5 %early.1 = (f32[1,1024]{1,0:T(1,128)S(1)}, f32[1,1024]{1,0:T(1,128)S(1)}, f32[1,1024]{1,0:T(1,128)S(1)}, f32[1,1024]{1,0:T(1,128)S(1)}) custom-call(bf16[512,1024]{1,0:T(8,128)(2,1)S(1)} %bitcast.11, bf16[512,1024]{1,0:T(8,128)(2,1)S(1)} %bitcast.16, bf16[512,1024]{1,0:T(8,128)(2,1)} %collective-permute-done.refs_2_, ...), custom_call_target="tpu_custom_call" | custom-call | flops 6442450944 | bytes 6291456 | tf_op jit(solution)/shard_map/early/pallas_call | solution.py:129
  76.7 4.3 %collective-permute-done.5.refs_7_ = bf16[512,1024]{1,0:T(8,128)(2,1)S(1)} collective-permute-done((bf16[512,1024]{1,0:T(8,128)(2,1)S(1)}, bf16[512,1024]{1,0:T(8,128)(2,1)S(1)}, u32[]{:S(2)}, u32[]{:S(2)}) %collective-permute-start.5) | collective-permute-done | bytes 1048608 | tf_op jit(solution)/shard_map/ppermute | solution.py:213
  80.9 2.1 %collective-permute-done.4.refs_6_ = bf16[512,1024]{1,0:T(8,128)(2,1)S(1)} collective-permute-done((bf16[512,1024]{1,0:T(8,128)(2,1)S(1)}, bf16[512,1024]{1,0:T(8,128)(2,1)S(1)}, u32[]{:S(2)}, u32[]{:S(2)}) %collective-permute-start.4) | collective-permute-done | bytes 1048608 | tf_op jit(solution)/shard_map/ppermute | solution.py:213
  83.0 10.2 %late.1 = (f32[1,1024]{1,0:T(1,128)S(1)}, f32[1,1024]{1,0:T(1,128)S(1)}, f32[1,1024]{1,0:T(1,128)S(1)}, f32[1,1024]{1,0:T(1,128)S(1)}) custom-call(bf16[512,1024]{1,0:T(8,128)(2,1)S(1)} %bitcast.12, bf16[512,1024]{1,0:T(8,128)(2,1)S(1)} %bitcast.17, bf16[512,1024]{1,0:T(8,128)(2,1)} %collective-permute-done.refs_2_, ...), custom_call_target="tpu_custom_call" | custom-call | flops 3758096384 | bytes 8388608 | tf_op jit(solution)/shard_map/late/pallas_call | solution.py:129
  93.1 0.1 collective-permute-start.6
  93.2 1.8 %collective-permute-start.7 = (f32[1,1024]{1,0:T(1,128)S(1)}, f32[1,1024]{1,0:T(1,128)S(1)}, u32[]{:S(2)}, u32[]{:S(2)}) collective-permute-start(f32[1,1024]{1,0:T(1,128)S(1)} %get-tuple-element.28), channel_id=1, source_target_pairs={{0,2},{1,3},{2,4},{3,5},{4,6},{5,7},{6,0},{7,1},{8,10},{9,11},{10,... | collective-permute-start | bytes 12296 | tf_op jit(solution)/shard_map/ppermute | solution.py:213
  95.0 1.9 %collective-permute-start.8 = (f32[1,1024]{1,0:T(1,128)S(1)}, f32[1,1024]{1,0:T(1,128)S(1)}, u32[]{:S(2)}, u32[]{:S(2)}) collective-permute-start(f32[1,1024]{1,0:T(1,128)S(1)} %get-tuple-element.29), channel_id=1, source_target_pairs={{0,6},{1,7},{2,0},{3,1},{4,3},{5,2},{6,5},{7,4},{8,14},{9,15},{10,... | collective-permute-start | bytes 12296 | tf_op jit(solution)/shard_map/ppermute | solution.py:213
  97.0 0.0 collective-permute-done.6.a_ref
  97.0 1.5 %collective-permute-done.7.b_ref = f32[1,1024]{1,0:T(1,128)S(1)} collective-permute-done((f32[1,1024]{1,0:T(1,128)S(1)}, f32[1,1024]{1,0:T(1,128)S(1)}, u32[]{:S(2)}, u32[]{:S(2)}) %collective-permute-start.7) | collective-permute-done | bytes 4128 | tf_op jit(solution)/shard_map/ppermute | solution.py:213
  98.5 0.2 collective-permute-done.8.c_ref
  98.6 0.1 join.1
  98.7 14.6 %all_to_all.16 = f32[16,8,128]{2,1,0:T(8,128)S(1)} all-to-all(f32[16,8,128]{2,1,0:T(8,128)S(1)} %bitcast.19), channel_id=1, replica_groups=mesh['wide'=16,'pair'=8] {'wide'}, dimensions={0} | all-to-all | bytes 131072 | tf_op jit(solution)/shard_map/all_to_all | solution.py:254
  113.3 0.9 pick.1
Async XLA Ops:
  0.0 1.6 %copy-start = (f32[512,1024]{1,0:T(8,128)S(1)}, f32[512,1024]{1,0:T(8,128)}, u32[]{:S(2)}) copy-start(f32[512,1024]{1,0:T(8,128)} %x_ref.1) | copy-start | bytes 6291460
  1.6 0.7 copy-start.1
  28.8 19.8 %all-to-all-start.1 = ((bf16[16,32,1024]{2,1,0:T(8,128)(2,1)}), bf16[16,32,1024]{2,1,0:T(8,128)(2,1)S(1)}, u32[]{:S(2)}, u32[]{:S(2)}) async-start(bf16[16,32,1024]{2,1,0:T(8,128)(2,1)} %bitcast.3), calls=%async_computation.1 | async-start | bytes 2097152 | tf_op jit(solution)/shard_map/all_to_all | solution.py:209
  32.6 28.2 %collective-permute-start.3 = (bf16[512,1024]{1,0:T(8,128)(2,1)S(1)}, bf16[512,1024]{1,0:T(8,128)(2,1)S(1)}, u32[]{:S(2)}, u32[]{:S(2)}) collective-permute-start(bf16[512,1024]{1,0:T(8,128)(2,1)S(1)} %bitcast.8), channel_id=1, source_target_pairs={{6,0},{7,1},{0,2},{1,3},{3,4},{2,5},{5,6},{4,7},{14,8},{15,9},{8,1... | collective-permute-start | bytes 3145736 | tf_op jit(solution)/shard_map/ppermute | solution.py:213
  34.6 27.6 %collective-permute-start.2 = (bf16[512,1024]{1,0:T(8,128)(2,1)S(1)}, bf16[512,1024]{1,0:T(8,128)(2,1)}, u32[]{:S(2)}, u32[]{:S(2)}) collective-permute-start(bf16[512,1024]{1,0:T(8,128)(2,1)S(1)} %bitcast.9), channel_id=1, source_target_pairs={{2,0},{3,1},{4,2},{5,3},{6,4},{7,5},{0,6},{1,7},{10,8},{11,9},{12,... | collective-permute-start | bytes 3145736 | tf_op jit(solution)/shard_map/ppermute | solution.py:213
  36.8 25.4 %collective-permute-start = (bf16[512,1024]{1,0:T(8,128)(2,1)S(1)}, bf16[512,1024]{1,0:T(8,128)(2,1)}, u32[]{:S(2)}, u32[]{:S(2)}) collective-permute-start(bf16[512,1024]{1,0:T(8,128)(2,1)S(1)} %bitcast.10), channel_id=1, source_target_pairs={{0,1},{1,0},{2,3},{3,2},{4,5},{5,4},{6,7},{7,6},{8,9},{9,8},{10,11... | collective-permute-start | bytes 3145736 | tf_op jit(solution)/shard_map/ppermute | solution.py:213
  48.5 13.7 %collective-permute-start.1 = (bf16[512,1024]{1,0:T(8,128)(2,1)S(1)}, bf16[512,1024]{1,0:T(8,128)(2,1)S(1)}, u32[]{:S(2)}, u32[]{:S(2)}) collective-permute-start(bf16[512,1024]{1,0:T(8,128)(2,1)S(1)} %bitcast.13), channel_id=1, source_target_pairs={{0,1},{1,0},{2,3},{3,2},{4,5},{5,4},{6,7},{7,6},{8,9},{9,8},{10,11... | collective-permute-start | bytes 3145736 | tf_op jit(solution)/shard_map/ppermute | solution.py:213
  48.5 32.4 %collective-permute-start.5 = (bf16[512,1024]{1,0:T(8,128)(2,1)S(1)}, bf16[512,1024]{1,0:T(8,128)(2,1)S(1)}, u32[]{:S(2)}, u32[]{:S(2)}) collective-permute-start(bf16[512,1024]{1,0:T(8,128)(2,1)S(1)} %bitcast.14), channel_id=1, source_target_pairs={{6,0},{7,1},{0,2},{1,3},{3,4},{2,5},{5,6},{4,7},{14,8},{15,9},{8,1... | collective-permute-start | bytes 3145736 | tf_op jit(solution)/shard_map/ppermute | solution.py:213
  60.8 22.2 %collective-permute-start.4 = (bf16[512,1024]{1,0:T(8,128)(2,1)S(1)}, bf16[512,1024]{1,0:T(8,128)(2,1)S(1)}, u32[]{:S(2)}, u32[]{:S(2)}) collective-permute-start(bf16[512,1024]{1,0:T(8,128)(2,1)S(1)} %bitcast.15), channel_id=1, source_target_pairs={{2,0},{3,1},{4,2},{5,3},{6,4},{7,5},{0,6},{1,7},{10,8},{11,9},{12,... | collective-permute-start | bytes 3145736 | tf_op jit(solution)/shard_map/ppermute | solution.py:213
  93.1 3.9 %collective-permute-start.6 = (f32[1,1024]{1,0:T(1,128)S(1)}, f32[1,1024]{1,0:T(1,128)S(1)}, u32[]{:S(2)}, u32[]{:S(2)}) collective-permute-start(f32[1,1024]{1,0:T(1,128)S(1)} %get-tuple-element.27), channel_id=1, source_target_pairs={{0,1},{1,0},{2,3},{3,2},{4,5},{5,4},{6,7},{7,6},{8,9},{9,8},{10,11... | collective-permute-start | bytes 12296 | tf_op jit(solution)/shard_map/ppermute | solution.py:213
  93.2 5.3 %collective-permute-start.7 = (f32[1,1024]{1,0:T(1,128)S(1)}, f32[1,1024]{1,0:T(1,128)S(1)}, u32[]{:S(2)}, u32[]{:S(2)}) collective-permute-start(f32[1,1024]{1,0:T(1,128)S(1)} %get-tuple-element.28), channel_id=1, source_target_pairs={{0,2},{1,3},{2,4},{3,5},{4,6},{5,7},{6,0},{7,1},{8,10},{9,11},{10,... | collective-permute-start | bytes 12296 | tf_op jit(solution)/shard_map/ppermute | solution.py:213
  95.0 3.6 %collective-permute-start.8 = (f32[1,1024]{1,0:T(1,128)S(1)}, f32[1,1024]{1,0:T(1,128)S(1)}, u32[]{:S(2)}, u32[]{:S(2)}) collective-permute-start(f32[1,1024]{1,0:T(1,128)S(1)} %get-tuple-element.29), channel_id=1, source_target_pairs={{0,6},{1,7},{2,0},{3,1},{4,3},{5,2},{6,5},{7,4},{8,14},{9,15},{10,... | collective-permute-start | bytes 12296 | tf_op jit(solution)/shard_map/ppermute | solution.py:213

commit v2 on v1

v2 whole, which is shorter than its diff:
```python
import functools

import jax
import jax.numpy as jnp
from jax import lax
from jax.experimental import pallas as pl
from jax.experimental.pallas import tpu as pltpu
from jax.sharding import PartitionSpec as P

EPSILON = 1e-06
OWNERS = 16
CAP = 64
HALF = CAP // 2
CHUNK = OWNERS * HALF
SHORT = 256
LOW = -1e30
MARK = 2.0
F32 = jnp.float32
BF16 = jnp.bfloat16


def params():
    return pltpu.CompilerParams(vmem_limit_bytes=40 * 1024 * 1024)


def cost(flops, bytes_accessed):
    return pl.CostEstimate(flops=flops, bytes_accessed=bytes_accessed, transcendentals=0)


def iota(shape, dim):
    return lax.broadcasted_iota(jnp.int32, shape, dim)


def marked(head):
    return head.astype(F32)[:, 0:1] > 1.5


def place(half, unit, ids, rank, out_ref):
    rows = unit.shape[0]
    inside = (rank >= half * HALF) & (rank < (half + 1) * HALF)
    slot = jnp.where(inside, ids * HALF + rank - half * HALF, -1)
    onehot = (iota((CHUNK, rows), 0) == slot).astype(BF16)
    moved = jnp.dot(onehot, unit, preferred_element_type=F32)
    taken = jnp.dot(onehot, jnp.ones((rows, 128), BF16), preferred_element_type=F32)
    out_ref[...] = moved.astype(BF16)
    mark = jnp.where(iota((CHUNK, 128), 1) == 0, MARK * (1.0 - taken), 0.0)
    out_ref[:, 0:128] = (moved[:, 0:128] + mark).astype(BF16)


def prep_kernel(x_hbm, ids_hbm, first_ref, unit_ref, meta_ref, x_ref, ids_ref, sems):
    rows = x_ref.shape[0]
    parts = 4
    step = rows // parts
    copies = [pltpu.make_async_copy(ids_hbm, ids_ref, sems.at[parts])]
    for i in range(parts):
        at = pl.ds(i * step, step)
        copies.append(pltpu.make_async_copy(x_hbm.at[at], x_ref.at[at], sems.at[i]))
    for copy in copies:
        copy.start()
    copies[0].wait()
    ids = ids_ref[...]
    onehot = iota((OWNERS, rows), 0) == ids
    upto = (iota((rows, rows), 0) <= iota((rows, rows), 1)).astype(BF16)
    counts = jnp.dot(onehot.astype(BF16), upto, preferred_element_type=F32)
    rank = jnp.sum(jnp.where(onehot, counts, 0.0), axis=0, keepdims=True).astype(jnp.int32) - 1
    meta_ref[...] = jnp.where(iota((8, rows), 0) == 0, ids, rank)
    for i in range(parts):
        copies[i + 1].wait()
        at = pl.ds(i * step, step)
        x = x_ref[at, :]
        scale = lax.rsqrt(jnp.sum(x * x, axis=1, keepdims=True) + EPSILON)
        unit_ref[at, :] = (x * scale).astype(BF16)
    place(0, unit_ref[...], ids, rank, first_ref)


def prep(embeddings, ids):
    rows, width = embeddings.shape
    return pl.pallas_call(
        prep_kernel,
        in_specs=[pl.BlockSpec(memory_space=pltpu.HBM)] * 2,
        out_shape=(
            jax.ShapeDtypeStruct((CHUNK, width), BF16),
            jax.ShapeDtypeStruct((rows, width), BF16),
            jax.ShapeDtypeStruct((8, rows), jnp.int32),
        ),
        scratch_shapes=[
            pltpu.VMEM((rows, width), F32),
            pltpu.VMEM((1, rows), jnp.int32),
            pltpu.SemaphoreType.DMA((5,)),
        ],
        compiler_params=params(),
        cost_estimate=cost(2 * CHUNK * rows * width, 8 * rows * width),
        name="prep",
    )(embeddings, ids)


def rest_kernel(unit_ref, meta_ref, second_ref):
    place(1, unit_ref[...], meta_ref[0:1, :], meta_ref[1:2, :], second_ref)


def rest(unit, meta):
    rows, width = unit.shape
    return pl.pallas_call(
        rest_kernel,
        out_shape=jax.ShapeDtypeStruct((CHUNK, width), BF16),
        compiler_params=params(),
        cost_estimate=cost(2 * CHUNK * rows * width, 4 * rows * width),
        name="rest",
    )(unit, meta)


def pack_kernel(block_ref, packed_ref, spot_ref):
    rows = block_ref.shape[0]
    full = jnp.where(marked(block_ref[:, 0:128]), 0.0, 1.0)
    full = jnp.transpose(jnp.broadcast_to(full, (rows, 128)))[0:8, :]
    upto = (iota((rows, rows), 0) <= iota((rows, rows), 1)).astype(BF16)
    count = jnp.dot(full.astype(BF16), upto, preferred_element_type=F32)
    spot = jnp.where(full > 0.5, count - 1.0, -1.0).astype(jnp.int32)
    spot_ref[...] = spot
    onehot = (iota((SHORT, rows), 0) == spot[0:1, :]).astype(BF16)
    moved = jnp.dot(onehot, block_ref[...], preferred_element_type=F32)
    taken = jnp.dot(onehot, jnp.ones((rows, 128), BF16), preferred_element_type=F32)
    packed_ref[...] = moved.astype(BF16)
    mark = jnp.where(iota((SHORT, 128), 1) == 0, MARK * (1.0 - taken), 0.0)
    packed_ref[:, 0:128] = (moved[:, 0:128] + mark).astype(BF16)


def pack(block):
    rows, width = block.shape
    return pl.pallas_call(
        pack_kernel,
        out_shape=(
            jax.ShapeDtypeStruct((SHORT, width), BF16),
            jax.ShapeDtypeStruct((8, rows), jnp.int32),
        ),
        compiler_params=params(),
        cost_estimate=cost(2 * SHORT * rows * width, 4 * rows * width),
        name="pack",
    )(block)


def pair_kernel(units, n_blocks, n_before, wanted, tails, *refs):
    blocks = refs[:n_blocks]
    before = refs[n_blocks : n_blocks + n_before]
    outs = refs[n_blocks + n_before : n_blocks + n_before + len(wanted)]
    lane_bias, row_bias, over_lanes, over_rows = refs[n_blocks + n_before + len(wanted) :]
    for b, block in enumerate(blocks):
        rows = block.shape[0]
        bias = jnp.where(marked(block[:, 0:128]), LOW, 0.0)
        bias = jnp.broadcast_to(bias, (rows, 128))
        lane_bias[b, 0:rows] = bias
        row_bias[b, :, 0:rows] = jnp.transpose(bias)[0:8, :]
        over_lanes[b, 0:rows] = jnp.full((rows, 128), LOW, F32)
        over_rows[b, :, 0:rows] = jnp.full((8, rows), LOW, F32)
    for left, right, mode in units:
        n_left, n_right = blocks[left].shape[0], blocks[right].shape[0]
        scores = lax.dot_general(
            blocks[left][...], blocks[right][...], (((1,), (1,)), ((), ())), preferred_element_type=F32
        )
        valid = scores + row_bias[right, 0:1, 0:n_right]
        if mode == "self":
            valid = jnp.where(iota(scores.shape, 0) == iota(scores.shape, 1), LOW, valid)
        best = over_lanes[left, 0:n_left]
        for g in range(0, n_right, 128):
            best = jnp.maximum(best, valid[:, g : g + 128])
        over_lanes[left, 0:n_left] = best
        if mode == "both":
            bias = lane_bias[left, 0:n_left]
            for g in range(0, n_right, 128):
                part = (scores[:, g : g + 128] + bias).reshape(n_left // 8, 8, 128)
                part = jnp.max(part, axis=0)
                over_rows[right, :, g : g + 128] = jnp.maximum(over_rows[right, :, g : g + 128], part)
    flag = jnp.zeros((1, 128), F32)
    for b in tails:
        end = blocks[b].shape[0]
        last = blocks[b][end - 16 : end, 0:128].astype(F32)[15:16, 0:1]
        flag = jnp.maximum(flag, jnp.where(last > 1.5, 0.0, 1.0))
    for (first, second, earlier), out in zip(wanted, outs):
        for b, at, n in ((first, 0, CHUNK), (second, CHUNK, out.shape[1] - CHUNK - 128)):
            part = jnp.full((1, n), LOW, F32)
            if b is not None:
                part = jnp.max(jnp.transpose(over_lanes[b, 0:n]), axis=0, keepdims=True)
                part = jnp.maximum(part, jnp.max(over_rows[b, :, 0:n], axis=0, keepdims=True))
            if earlier is not None:
                part = jnp.maximum(part, before[earlier][:, at : at + n])
            out[:, at : at + n] = part
        out[:, out.shape[1] - 128 :] = flag


def pairs(units, blocks, before, wanted, tails, width, name):
    n = len(blocks)
    rows, depth = blocks[0].shape
    work = sum(blocks[a].shape[0] * blocks[b].shape[0] for a, b, _ in units)
    return pl.pallas_call(
        functools.partial(pair_kernel, units, n, len(before), wanted, tails),
        out_shape=tuple(jax.ShapeDtypeStruct((1, width + 128), F32) for _ in wanted),
        scratch_shapes=[
            pltpu.VMEM((n, rows, 128), F32),
            pltpu.VMEM((n, 8, rows), F32),
            pltpu.VMEM((n, rows, 128), F32),
            pltpu.VMEM((n, 8, rows), F32),
        ],
        compiler_params=params(),
        cost_estimate=cost(2 * work * depth, 2 * n * rows * depth),
        name=name,
    )(*blocks, *before)


def spread_exact(value, onehot, contract):
    total = None
    for _ in range(3):
        part = value.astype(BF16)
        value = value - part.astype(F32)
        moved = lax.dot_general(part, onehot, ((contract, ((0,))), ((), ())), preferred_element_type=F32)
        total = moved if total is None else total + moved
    return total


def join_kernel(packed, own_ref, a_ref, b_ref, c_ref, *rest):
    best = jnp.maximum(jnp.maximum(own_ref[...], a_ref[...]), jnp.maximum(b_ref[...], c_ref[...]))
    best = jnp.maximum(best, -1.0)
    out_ref = rest[-1]
    second = best[:, CHUNK:-128]
    if packed:
        spot = rest[0][0:1, :]
        onehot = (iota((SHORT, CHUNK), 0) == spot).astype(BF16)
        second = spread_exact(jnp.broadcast_to(second, (8, SHORT)), onehot, (1,))[0:1, :]
    out_ref[...] = jnp.zeros(out_ref.shape, F32)
    for source in range(OWNERS):
        at = source * HALF
        row = slice(source * 8, source * 8 + 1)
        out_ref[row, 0:HALF] = best[:, at : at + HALF]
        out_ref[row, HALF:CAP] = second[:, at : at + HALF]
        out_ref[row, CAP:128] = best[:, -CAP:]


def join(own, a, b, c, *spot):
    return pl.pallas_call(
        functools.partial(join_kernel, bool(spot)),
        out_shape=jax.ShapeDtypeStruct((OWNERS * 8, 128), F32),
        compiler_params=params(),
        name="join",
    )(own, a, b, c, *spot)


def pick_kernel(back_ref, meta_ref, out_ref, flag_ref):
    rows = meta_ref.shape[1]
    ids = meta_ref[0:1, :]
    rank = meta_ref[1:2, :]
    onehot = (iota((OWNERS, rows), 0) == ids).astype(BF16)
    tiles = jnp.concatenate([back_ref[s * 8 : s * 8 + 1, :] for s in range(OWNERS)], axis=0)
    moved = spread_exact(tiles, onehot, (0,))
    out_ref[...] = jnp.sum(jnp.where(iota((128, rows), 0) == rank, moved, 0.0), axis=0, keepdims=True)
    flag_ref[...] = jnp.max(tiles, axis=0, keepdims=True)


def pick(back, meta):
    return pl.pallas_call(
        pick_kernel,
        out_shape=(
            jax.ShapeDtypeStruct((1, meta.shape[1]), F32),
            jax.ShapeDtypeStruct((1, 128), F32),
        ),
        compiler_params=params(),
        name="pick",
    )(back, meta)


def swap_cores():
    return [(2 * z + k, 2 * z + 1 - k) for z in range(4) for k in range(2)]


def from_next():
    return [(2 * ((z + 1) % 4) + k, 2 * z + k) for z in range(4) for k in range(2)]


def from_last():
    return [
        (2 * ((z + 3) % 4) + (k if z < 2 else 1 - k), 2 * z + k) for z in range(4) for k in range(2)
    ]


def inverse(perm):
    return [(b, a) for a, b in perm]


def to_owners(block):
    shape = block.shape
    block = block.reshape(OWNERS, HALF, shape[1])
    return lax.all_to_all(block, "wide", split_axis=0, concat_axis=0, tiled=True).reshape(shape)


def along_pair(block, perm):
    return lax.ppermute(block, "pair", perm)


def give_back(own, sib, nxt, last, meta, *spot):
    tiles = join(
        own,
        along_pair(sib, swap_cores()),
        along_pair(nxt, inverse(from_next())),
        along_pair(last, inverse(from_last())),
        *spot,
    )
    back = lax.all_to_all(tiles.reshape(OWNERS, 8, 128), "wide", split_axis=0, concat_axis=0, tiled=True)
    return pick(back.reshape(OWNERS * 8, 128), meta)


EARLY = (
    (0, 0, "self"), (0, 2, "left"), (0, 4, "both"), (2, 4, "both"), (5, 4, "both"),
    (0, 1, "both"), (1, 1, "self"), (0, 3, "left"), (1, 2, "left"), (1, 3, "left"),
    (1, 4, "both"), (3, 4, "both"),
)
LATE = (
    (0, 6, "both"), (1, 6, "both"), (2, 6, "both"), (3, 6, "both"),
    (5, 6, "both"), (7, 4, "both"), (7, 6, "both"),
)


def match(a, second, tails):
    own_a, sib_a, next_a, last_a = a
    own_b, sib_b, next_b, last_b = second
    width = CHUNK + own_b.shape[0]
    before = pairs(
        EARLY,
        (own_a, own_b, sib_a, sib_b, next_a, last_a),
        (),
        ((0, 1, None), (2, 3, None), (4, None, None), (5, None, None)),
        (),
        width,
        "early",
    )
    return pairs(
        LATE,
        (own_a, own_b, sib_a, sib_b, next_a, last_a, next_b, last_b),
        before,
        ((0, 1, 0), (2, 3, 1), (4, 6, 2), (5, 7, 3)),
        tails,
        width,
        "late",
    )


def neighbours(block):
    return (
        block,
        along_pair(block, swap_cores()),
        along_pair(block, from_next()),
        along_pair(block, from_last()),
    )


def exchange(embeddings, ids):
    first, unit, meta = prep(embeddings, ids)
    own_a = to_owners(first)
    own_a, unit = lax.optimization_barrier((own_a, unit))
    a = neighbours(own_a)
    own_b = to_owners(rest(unit, meta))
    own_b, *a = lax.optimization_barrier((own_b, *a))
    return tuple(a), own_b, meta


def whole(embeddings, ids):
    a, own_b, meta = exchange(embeddings, ids)
    best = match(a, neighbours(own_b), ())
    return give_back(*best, meta)[0]


def per_device(embeddings, cluster_ids):
    ids = cluster_ids.reshape(1, -1)
    a, own_b, meta = exchange(embeddings, ids)
    packed, spot = pack(own_b)
    best = match(a, neighbours(packed), (1, 3, 6, 7))
    value, flag = give_back(*best, meta, spot)
    return lax.cond(
        flag[0, CAP] > 0.5, lambda: whole(embeddings, ids), lambda: value
    ).reshape(-1)


def solution(mesh):
    in_specs = (P(("wide", "pair"), None), P(("wide", "pair")))
    out_specs = P(("wide", "pair"))
    return jax.shard_map(
        per_device, mesh=mesh, in_specs=in_specs, out_specs=out_specs, check_vma=False
    )
```

time: 115 us -> 92 us (0.80)
  Pallas kernels: 28.3 us -> 12.6 us
  waiting for transfers between devices: 30.1 us -> 17.6 us
  blocking collectives: 38.4 us -> 45.2 us
  local copies, waits for them, and re-layouts: 2.27 us -> 0.58 us
    all_to_all x1 -> x2, blocking collectives: 23.8 us -> 45.2 us  [to_owners(): lax.all_to_all(block, 'wide', split_axis=0, concat_axis=0, tiled=True)]
    pallas_call x2, Pallas kernels: 24.6 us -> 6.66 us  [pairs(): pl.pallas_call(functools.partial(pair_kernel, units, n, len(before), want...]
    all_to_all x1 -> x0, blocking collectives: 14.6 us -> none  [per_device(): lax.all_to_all(tiles.reshape(OWNERS, 8, 128), 'wide', split_axis=0, conca...]
    ppermute x9, waiting for transfers between devices: 18.3 us -> 9.97 us  [along_pair(): return lax.ppermute(block, 'pair', perm)]
    all_to_all x1, waiting for transfers between devices: 11.7 us -> 7.67 us  [give_back(): lax.all_to_all(tiles.reshape(OWNERS, 8, 128), 'wide', split_axis=0, conca...]
    unnamed x4, local copies, waits for them, and re-layouts: 2.27 us -> 0.01 us
    pallas_call x3 -> x5, Pallas kernels: 3.7 us -> 5.9 us  [the longest x1 2.46 us: prep(): pl.pallas_call(prep_kernel, in_specs=[pl.BlockSpec(memory_space=pltpu.HBM...]
  transfers between devices with their start and end apart: 10 -> 10, of which waited for: 6 -> 4; matrix products, arithmetic and copies ran while one was open for 0% -> 0% of each run, Pallas kernels for 13% -> 6%
where the time goes in v2:
time: 92 us; the launch traced here: 91.7 us
  blocking collectives  45.2 us (49%)
  waiting for transfers between devices  17.6 us (19%)
  starting transfers between devices  14.6 us (16%)
  Pallas kernels  12.6 us (14%)
    all_to_all x2, blocking collectives, to_owners(): lax.all_to_all(block, 'wide', split_axis=0, concat_axis=0, tiled=True)  45.2 us
    ppermute x9, starting transfers between devices, along_pair(): return lax.ppermute(block, 'pair', perm)  10.8 us
    ppermute x9, waiting for transfers between devices, along_pair(): return lax.ppermute(block, 'pair', perm)  9.97 us
    all_to_all x1, waiting for transfers between devices, give_back(): lax.all_to_all(tiles.reshape(OWNERS, 8, 128), 'wide', split_axis=0, conca...  7.67 us
    pallas_call x2, Pallas kernels, pairs(): pl.pallas_call(functools.partial(pair_kernel, units, n, len(before), want...  6.66 us
    all_to_all x1, starting transfers between devices, give_back(): lax.all_to_all(tiles.reshape(OWNERS, 8, 128), 'wide', split_axis=0, conca...  3.83 us
    pallas_call x1, Pallas kernels, prep(): pl.pallas_call(prep_kernel, in_specs=[pl.BlockSpec(memory_space=pltpu.HBM...  2.46 us
  transfers between devices with their start and end apart: 10, of which 4 were waited for; matrix products, arithmetic and copies ran while one was open for 0% of the time, Pallas kernels for 6%

profile of v2, /device:TPU:0, one launch (start us, length us, event | category | flops | bytes accessed | tf_op | source)
XLA Modules:
  0.0 91.7 jit_solution(5333016844695907629)
XLA Ops:
  0.0 2.5 %prep.3 = (bf16[512,1024]{1,0:T(8,128)(2,1)S(1)}, bf16[512,1024]{1,0:T(8,128)(2,1)S(1)}, s32[8,512]{1,0:T(8,128)S(1)}) custom-call(f32[512,1024]{1,0:T(8,128)} %x_hbm.1, s32[1,512]{1,0:T(1,128)} %bitcast.39), custom_call_target="tpu_custom_call" | custom-call | flops 536870912 | bytes 4194304 | tf_op jit(solution)/shard_map/prep/pallas_call | solution.py:78
  2.5 23.8 %all_to_all.30 = bf16[16,32,1024]{2,1,0:T(8,128)(2,1)S(1)} all-to-all(bf16[16,32,1024]{2,1,0:T(8,128)(2,1)S(1)} %bitcast.34), channel_id=1, replica_groups=mesh['wide'=16,'pair'=8] {'wide'}, dimensions={0} | all-to-all | bytes 2097152 | tf_op jit(solution)/shard_map/all_to_all | solution.py:290
  26.2 1.9 %collective-permute-start.11 = (bf16[512,1024]{1,0:T(8,128)(2,1)S(1)}, bf16[512,1024]{1,0:T(8,128)(2,1)S(1)}, u32[]{:S(2)}, u32[]{:S(2)}) collective-permute-start(bf16[512,1024]{1,0:T(8,128)(2,1)S(1)} %bitcast.16), channel_id=1, source_target_pairs={{6,0},{7,1},{0,2},{1,3},{3,4},{2,5},{5,6},{4,7},{14,8},{15,9},{8,1... | collective-permute-start | bytes 3145736 | tf_op jit(solution)/shard_map/ppermute | solution.py:294
  28.1 2.1 %collective-permute-start.10 = (bf16[512,1024]{1,0:T(8,128)(2,1)S(1)}, bf16[512,1024]{1,0:T(8,128)(2,1)S(1)}, u32[]{:S(2)}, u32[]{:S(2)}) collective-permute-start(bf16[512,1024]{1,0:T(8,128)(2,1)S(1)} %bitcast.17), channel_id=1, source_target_pairs={{2,0},{3,1},{4,2},{5,3},{6,4},{7,5},{0,6},{1,7},{10,8},{11,9},{12,... | collective-permute-start | bytes 3145736 | tf_op jit(solution)/shard_map/ppermute | solution.py:294
  30.3 0.0 collective-permute-start.9
  30.3 0.8 rest.3
  31.1 21.4 %all_to_all.31 = bf16[16,32,1024]{2,1,0:T(8,128)(2,1)S(1)} all-to-all(bf16[16,32,1024]{2,1,0:T(8,128)(2,1)S(1)} %bitcast.22), channel_id=1, replica_groups=mesh['wide'=16,'pair'=8] {'wide'}, dimensions={0} | all-to-all | bytes 2097152 | tf_op jit(solution)/shard_map/all_to_all | solution.py:290
  52.5 0.0 collective-permute-done.11.refs_5_
  52.5 0.9 %collective-permute-done.10.refs_4_ = bf16[512,1024]{1,0:T(8,128)(2,1)S(1)} collective-permute-done((bf16[512,1024]{1,0:T(8,128)(2,1)S(1)}, bf16[512,1024]{1,0:T(8,128)(2,1)S(1)}, u32[]{:S(2)}, u32[]{:S(2)}) %collective-permute-start.10) | collective-permute-done | bytes 1048608 | tf_op jit(solution)/shard_map/ppermute | solution.py:294
  53.5 0.0 collective-permute-done.9.refs_2_
  53.5 0.8 pack.1
  54.3 0.1 collective-permute-start.12
  54.4 0.6 collective-permute-start.14
  54.9 2.7 %collective-permute-start.13 = (bf16[256,1024]{1,0:T(8,128)(2,1)S(1)}, bf16[256,1024]{1,0:T(8,128)(2,1)S(1)}, u32[]{:S(2)}, u32[]{:S(2)}) collective-permute-start(bf16[256,1024]{1,0:T(8,128)(2,1)S(1)} %get-tuple-element.65.refs_1_), channel_id=1, source_target_pairs={{2,0},{3,1},{4,2},{5,3},{6,4},{7,5},{0,6},{1,7},{10,8},{11,9},{12,... | collective-permute-start | bytes 1572872 | tf_op jit(solution)/shard_map/ppermute | solution.py:294
  57.7 0.0 collective-permute-done.12.refs_3_
  57.7 4.8 %early.3 = (f32[1,896]{1,0:T(1,128)S(1)}, f32[1,896]{1,0:T(1,128)S(1)}, f32[1,896]{1,0:T(1,128)S(1)}, f32[1,896]{1,0:T(1,128)S(1)}) custom-call(bf16[512,1024]{1,0:T(8,128)(2,1)S(1)} %bitcast.19, bf16[256,1024]{1,0:T(8,128)(2,1)S(1)} %get-tuple-element.65.refs_1_, bf16[512,1024]{1,0:T(8,128)(2,1)S(1)} %collective-permute-done.9.refs_2_, ...), custom_call_target="tpu_custom_call" | custom-call | flops 4294967296 | bytes 6291456 | tf_op jit(solution)/shard_map/early/pallas_call | solution.py:194
  62.5 7.4 %collective-permute-done.14.refs_7_ = bf16[256,1024]{1,0:T(8,128)(2,1)S(1)} collective-permute-done((bf16[256,1024]{1,0:T(8,128)(2,1)S(1)}, bf16[256,1024]{1,0:T(8,128)(2,1)S(1)}, u32[]{:S(2)}, u32[]{:S(2)}) %collective-permute-start.14) | collective-permute-done | bytes 524320 | tf_op jit(solution)/shard_map/ppermute | solution.py:294
  69.9 0.0 collective-permute-done.13.refs_6_
  69.9 0.0 copy-start
  69.9 0.0 copy-start.1
  69.9 1.9 %late.3 = (f32[1,896]{1,0:T(1,128)S(1)}, f32[1,896]{1,0:T(1,128)S(1)}, f32[1,896]{1,0:T(1,128)S(1)}, f32[1,896]{1,0:T(1,128)S(1)}) custom-call(bf16[512,1024]{1,0:T(8,128)(2,1)S(1)} %bitcast.20, bf16[256,1024]{1,0:T(8,128)(2,1)S(1)} %get-tuple-element.65.refs_1_, bf16[512,1024]{1,0:T(8,128)(2,1)S(1)} %collective-permute-done.9.refs_2_, ...), custom_call_target="tpu_custom_call" | custom-call | flops 1476395008 | bytes 8388608 | tf_op jit(solution)/shard_map/late/pallas_call | solution.py:194
  71.8 0.1 collective-permute-start.15
  71.9 0.9 collective-permute-start.16
  72.7 2.4 %collective-permute-start.17 = (f32[1,896]{1,0:T(1,128)S(1)}, f32[1,896]{1,0:T(1,128)S(1)}, u32[]{:S(2)}, u32[]{:S(2)}) collective-permute-start(f32[1,896]{1,0:T(1,128)S(1)} %get-tuple-element.76), channel_id=1, source_target_pairs={{0,6},{1,7},{2,0},{3,1},{4,3},{5,2},{6,5},{7,4},{8,14},{9,15},{10,... | collective-permute-start | bytes 10760 | tf_op jit(solution)/shard_map/ppermute | solution.py:294
  75.2 0.0 collective-permute-done.15.a_ref
  75.2 1.6 %collective-permute-done.16.b_ref = f32[1,896]{1,0:T(1,128)S(1)} collective-permute-done((f32[1,896]{1,0:T(1,128)S(1)}, f32[1,896]{1,0:T(1,128)S(1)}, u32[]{:S(2)}, u32[]{:S(2)}) %collective-permute-start.16) | collective-permute-done | bytes 3616 | tf_op jit(solution)/shard_map/ppermute | solution.py:294
  76.8 0.0 collective-permute-done.17.c_ref
  76.8 0.9 %join.3 = f32[128,128]{1,0:T(8,128)} custom-call(f32[1,896]{1,0:T(1,128)S(1)} %get-tuple-element.73.own_ref, f32[1,896]{1,0:T(1,128)S(1)} %collective-permute-done.15.a_ref, f32[1,896]{1,0:T(1,128)S(1)} %collective-permute-done.16.b_ref, f32[1,896]{1,0:T(1,128)S(1)} %collective-permute-done.17.c_ref, s32[8,512]{1,0:T(8,128)S(1)} %get-tuple-element.77.rest_0_), custom_call_target="tpu_custom_call" | custom-call | tf_op jit(solution)/shard_map/join/pallas_call | solution.py:238
  77.7 3.8 %all-to-all-start.5 = ((f32[16,8,128]{2,1,0:T(8,128)}), f32[16,8,128]{2,1,0:T(8,128)S(1)}, u32[]{:S(2)}, u32[]{:S(2)}) async-start(f32[16,8,128]{2,1,0:T(8,128)} %bitcast.13), calls=%async_computation.5 | async-start | bytes 131072 | tf_op jit(solution)/shard_map/all_to_all | solution.py:305
  81.5 7.7 %all-to-all-done.5 = f32[16,8,128]{2,1,0:T(8,128)S(1)} async-done(((f32[16,8,128]{2,1,0:T(8,128)}), f32[16,8,128]{2,1,0:T(8,128)S(1)}, u32[]{:S(2)}, u32[]{:S(2)}) %all-to-all-start.5) | async-done | bytes 65568 | tf_op jit(solution)/shard_map/all_to_all | solution.py:305
  89.2 0.9 pick.3
  90.1 0.6 slice.3
  91.2 0.0 copy-done
  91.3 0.0 copy-done.1
  91.3 0.3 conditional.1
Async XLA Ops:
  26.2 26.3 %collective-permute-start.11 = (bf16[512,1024]{1,0:T(8,128)(2,1)S(1)}, bf16[512,1024]{1,0:T(8,128)(2,1)S(1)}, u32[]{:S(2)}, u32[]{:S(2)}) collective-permute-start(bf16[512,1024]{1,0:T(8,128)(2,1)S(1)} %bitcast.16), channel_id=1, source_target_pairs={{6,0},{7,1},{0,2},{1,3},{3,4},{2,5},{5,6},{4,7},{14,8},{15,9},{8,1... | collective-permute-start | bytes 3145736 | tf_op jit(solution)/shard_map/ppermute | solution.py:294
  28.1 25.4 %collective-permute-start.10 = (bf16[512,1024]{1,0:T(8,128)(2,1)S(1)}, bf16[512,1024]{1,0:T(8,128)(2,1)S(1)}, u32[]{:S(2)}, u32[]{:S(2)}) collective-permute-start(bf16[512,1024]{1,0:T(8,128)(2,1)S(1)} %bitcast.17), channel_id=1, source_target_pairs={{2,0},{3,1},{4,2},{5,3},{6,4},{7,5},{0,6},{1,7},{10,8},{11,9},{12,... | collective-permute-start | bytes 3145736 | tf_op jit(solution)/shard_map/ppermute | solution.py:294
  30.3 23.2 %collective-permute-start.9 = (bf16[512,1024]{1,0:T(8,128)(2,1)S(1)}, bf16[512,1024]{1,0:T(8,128)(2,1)S(1)}, u32[]{:S(2)}, u32[]{:S(2)}) collective-permute-start(bf16[512,1024]{1,0:T(8,128)(2,1)S(1)} %bitcast.18), channel_id=1, source_target_pairs={{0,1},{1,0},{2,3},{3,2},{4,5},{5,4},{6,7},{7,6},{8,9},{9,8},{10,11... | collective-permute-start | bytes 3145736 | tf_op jit(solution)/shard_map/ppermute | solution.py:294
  54.3 3.4 %collective-permute-start.12 = (bf16[256,1024]{1,0:T(8,128)(2,1)S(1)}, bf16[256,1024]{1,0:T(8,128)(2,1)S(1)}, u32[]{:S(2)}, u32[]{:S(2)}) collective-permute-start(bf16[256,1024]{1,0:T(8,128)(2,1)S(1)} %get-tuple-element.65.refs_1_), channel_id=1, source_target_pairs={{0,1},{1,0},{2,3},{3,2},{4,5},{5,4},{6,7},{7,6},{8,9},{9,8},{10,11... | collective-permute-start | bytes 1572872 | tf_op jit(solution)/shard_map/ppermute | solution.py:294
  54.4 15.6 %collective-permute-start.14 = (bf16[256,1024]{1,0:T(8,128)(2,1)S(1)}, bf16[256,1024]{1,0:T(8,128)(2,1)S(1)}, u32[]{:S(2)}, u32[]{:S(2)}) collective-permute-start(bf16[256,1024]{1,0:T(8,128)(2,1)S(1)} %get-tuple-element.65.refs_1_), channel_id=1, source_target_pairs={{6,0},{7,1},{0,2},{1,3},{3,4},{2,5},{5,6},{4,7},{14,8},{15,9},{8,1... | collective-permute-start | bytes 1572872 | tf_op jit(solution)/shard_map/ppermute | solution.py:294
  54.9 15.0 %collective-permute-start.13 = (bf16[256,1024]{1,0:T(8,128)(2,1)S(1)}, bf16[256,1024]{1,0:T(8,128)(2,1)S(1)}, u32[]{:S(2)}, u32[]{:S(2)}) collective-permute-start(bf16[256,1024]{1,0:T(8,128)(2,1)S(1)} %get-tuple-element.65.refs_1_), channel_id=1, source_target_pairs={{2,0},{3,1},{4,2},{5,3},{6,4},{7,5},{0,6},{1,7},{10,8},{11,9},{12,... | collective-permute-start | bytes 1572872 | tf_op jit(solution)/shard_map/ppermute | solution.py:294
  69.9 21.3 %copy-start = (f32[512,1024]{1,0:T(8,128)S(1)}, f32[512,1024]{1,0:T(8,128)}, u32[]{:S(2)}) copy-start(f32[512,1024]{1,0:T(8,128)} %x_hbm.1) | copy-start | bytes 6291460
  69.9 21.3 %copy-start.1 = (s32[512]{0:T(512)S(1)}, s32[512]{0:T(512)}, u32[]{:S(2)}) copy-start(s32[512]{0:T(512)} %param.5) | copy-start | bytes 6148
  71.8 3.4 %collective-permute-start.15 = (f32[1,896]{1,0:T(1,128)S(1)}, f32[1,896]{1,0:T(1,128)S(1)}, u32[]{:S(2)}, u32[]{:S(2)}) collective-permute-start(f32[1,896]{1,0:T(1,128)S(1)} %get-tuple-element.74), channel_id=1, source_target_pairs={{0,1},{1,0},{2,3},{3,2},{4,5},{5,4},{6,7},{7,6},{8,9},{9,8},{10,11... | collective-permute-start | bytes 10760 | tf_op jit(solution)/shard_map/ppermute | solution.py:294
  71.9 4.9 %collective-permute-start.16 = (f32[1,896]{1,0:T(1,128)S(1)}, f32[1,896]{1,0:T(1,128)S(1)}, u32[]{:S(2)}, u32[]{:S(2)}) collective-permute-start(f32[1,896]{1,0:T(1,128)S(1)} %get-tuple-element.75), channel_id=1, source_target_pairs={{0,2},{1,3},{2,4},{3,5},{4,6},{5,7},{6,0},{7,1},{8,10},{9,11},{10,... | collective-permute-start | bytes 10760 | tf_op jit(solution)/shard_map/ppermute | solution.py:294
  72.7 4.0 %collective-permute-start.17 = (f32[1,896]{1,0:T(1,128)S(1)}, f32[1,896]{1,0:T(1,128)S(1)}, u32[]{:S(2)}, u32[]{:S(2)}) collective-permute-start(f32[1,896]{1,0:T(1,128)S(1)} %get-tuple-element.76), channel_id=1, source_target_pairs={{0,6},{1,7},{2,0},{3,1},{4,3},{5,2},{6,5},{7,4},{8,14},{9,15},{10,... | collective-permute-start | bytes 10760 | tf_op jit(solution)/shard_map/ppermute | solution.py:294
  77.7 11.5 %all-to-all-start.5 = ((f32[16,8,128]{2,1,0:T(8,128)}), f32[16,8,128]{2,1,0:T(8,128)S(1)}, u32[]{:S(2)}, u32[]{:S(2)}) async-start(f32[16,8,128]{2,1,0:T(8,128)} %bitcast.13), calls=%async_computation.5 | async-start | bytes 131072 | tf_op jit(solution)/shard_map/all_to_all | solution.py:305

commit v3 on v2

--- a/solution.py
+++ b/solution.py
@@ -12,7 +12,7 @@
 CAP = 64
 HALF = CAP // 2
 CHUNK = OWNERS * HALF
-SHORT = 256
+SHORT = 208
 LOW = -1e30
 MARK = 2.0
 F32 = jnp.float32
@@ -109,15 +109,15 @@
     )(unit, meta)
 
 
-def pack_kernel(block_ref, packed_ref, spot_ref):
+def pack_kernel(block_ref, packed_ref, onehot_ref):
     rows = block_ref.shape[0]
     full = jnp.where(marked(block_ref[:, 0:128]), 0.0, 1.0)
     full = jnp.transpose(jnp.broadcast_to(full, (rows, 128)))[0:8, :]
     upto = (iota((rows, rows), 0) <= iota((rows, rows), 1)).astype(BF16)
     count = jnp.dot(full.astype(BF16), upto, preferred_element_type=F32)
     spot = jnp.where(full > 0.5, count - 1.0, -1.0).astype(jnp.int32)
-    spot_ref[...] = spot
     onehot = (iota((SHORT, rows), 0) == spot[0:1, :]).astype(BF16)
+    onehot_ref[...] = onehot
     moved = jnp.dot(onehot, block_ref[...], preferred_element_type=F32)
     taken = jnp.dot(onehot, jnp.ones((rows, 128), BF16), preferred_element_type=F32)
     packed_ref[...] = moved.astype(BF16)
@@ -131,12 +131,16 @@
         pack_kernel,
         out_shape=(
             jax.ShapeDtypeStruct((SHORT, width), BF16),
-            jax.ShapeDtypeStruct((8, rows), jnp.int32),
+            jax.ShapeDtypeStruct((SHORT, rows), BF16),
         ),
         compiler_params=params(),
         cost_estimate=cost(2 * SHORT * rows * width, 4 * rows * width),
         name="pack",
     )(block)
+
+
+def lanes(rows):
+    return -(-rows // 128) * 128
 
 
 def pair_kernel(units, n_blocks, n_before, wanted, tails, *refs):
@@ -147,11 +151,10 @@
     for b, block in enumerate(blocks):
         rows = block.shape[0]
         bias = jnp.where(marked(block[:, 0:128]), LOW, 0.0)
-        bias = jnp.broadcast_to(bias, (rows, 128))
-        lane_bias[b, 0:rows] = bias
-        row_bias[b, :, 0:rows] = jnp.transpose(bias)[0:8, :]
-        over_lanes[b, 0:rows] = jnp.full((rows, 128), LOW, F32)
-        over_rows[b, :, 0:rows] = jnp.full((8, rows), LOW, F32)
+        lane_bias[b, 0:rows] = jnp.broadcast_to(bias, (rows, 128))
+        row_bias[b, :, 0 : lanes(rows)] = jnp.transpose(lane_bias[b, 0 : lanes(rows)])[0:8, :]
+        over_lanes[b, 0 : lanes(rows)] = jnp.full((lanes(rows), 128), LOW, F32)
+        over_rows[b, :, 0 : lanes(rows)] = jnp.full((8, lanes(rows)), LOW, F32)
     for left, right, mode in units:
         n_left, n_right = blocks[left].shape[0], blocks[right].shape[0]
         scores = lax.dot_general(
@@ -161,15 +164,21 @@
         if mode == "self":
             valid = jnp.where(iota(scores.shape, 0) == iota(scores.shape, 1), LOW, valid)
         best = over_lanes[left, 0:n_left]
-        for g in range(0, n_right, 128):
+        whole_groups = n_right // 128 * 128
+        for g in range(0, whole_groups, 128):
             best = jnp.maximum(best, valid[:, g : g + 128])
         over_lanes[left, 0:n_left] = best
+        if whole_groups < n_right:
+            some = n_right - whole_groups
+            best = jnp.maximum(over_lanes[left, 0:n_left, 0:some], valid[:, whole_groups:])
+            over_lanes[left, 0:n_left, 0:some] = best
         if mode == "both":
             bias = lane_bias[left, 0:n_left]
             for g in range(0, n_right, 128):
-                part = (scores[:, g : g + 128] + bias).reshape(n_left // 8, 8, 128)
-                part = jnp.max(part, axis=0)
-                over_rows[right, :, g : g + 128] = jnp.maximum(over_rows[right, :, g : g + 128], part)
+                end = min(g + 128, n_right)
+                part = scores[:, g:end] + bias[:, 0 : end - g]
+                part = jnp.max(part.reshape(n_left // 8, 8, end - g), axis=0)
+                over_rows[right, :, g:end] = jnp.maximum(over_rows[right, :, g:end], part)
     flag = jnp.zeros((1, 128), F32)
     for b in tails:
         end = blocks[b].shape[0]
@@ -206,14 +215,13 @@
     )(*blocks, *before)
 
 
-def spread_exact(value, onehot, contract):
-    total = None
+def three_parts(value):
+    parts = []
     for _ in range(3):
-        part = value.astype(BF16)
-        value = value - part.astype(F32)
-        moved = lax.dot_general(part, onehot, ((contract, ((0,))), ((), ())), preferred_element_type=F32)
-        total = moved if total is None else total + moved
-    return total
+        part = value.astype(BF16).astype(F32)
+        value = value - part
+        parts.append(part)
+    return jnp.concatenate(parts, axis=0).astype(BF16)
 
 
 def join_kernel(packed, own_ref, a_ref, b_ref, c_ref, *rest):
@@ -222,36 +230,37 @@
     out_ref = rest[-1]
     second = best[:, CHUNK:-128]
     if packed:
-        spot = rest[0][0:1, :]
-        onehot = (iota((SHORT, CHUNK), 0) == spot).astype(BF16)
-        second = spread_exact(jnp.broadcast_to(second, (8, SHORT)), onehot, (1,))[0:1, :]
-    out_ref[...] = jnp.zeros(out_ref.shape, F32)
+        parts = three_parts(jnp.broadcast_to(second[:, 0:SHORT], (8, SHORT)))
+        moved = jnp.dot(parts, rest[0][...], preferred_element_type=F32)
+        second = moved[0:1, :] + moved[8:9, :] + moved[16:17, :]
     for source in range(OWNERS):
         at = source * HALF
-        row = slice(source * 8, source * 8 + 1)
+        row = slice(source, source + 1)
         out_ref[row, 0:HALF] = best[:, at : at + HALF]
         out_ref[row, HALF:CAP] = second[:, at : at + HALF]
         out_ref[row, CAP:128] = best[:, -CAP:]
 
 
-def join(own, a, b, c, *spot):
-    return pl.pallas_call(
-        functools.partial(join_kernel, bool(spot)),
-        out_shape=jax.ShapeDtypeStruct((OWNERS * 8, 128), F32),
+def join(own, a, b, c, *onehot):
+    return pl.pallas_call(
+        functools.partial(join_kernel, bool(onehot)),
+        out_shape=jax.ShapeDtypeStruct((OWNERS, 128), F32),
         compiler_params=params(),
         name="join",
-    )(own, a, b, c, *spot)
+    )(own, a, b, c, *onehot)
 
 
 def pick_kernel(back_ref, meta_ref, out_ref, flag_ref):
     rows = meta_ref.shape[1]
     ids = meta_ref[0:1, :]
     rank = meta_ref[1:2, :]
-    onehot = (iota((OWNERS, rows), 0) == ids).astype(BF16)
-    tiles = jnp.concatenate([back_ref[s * 8 : s * 8 + 1, :] for s in range(OWNERS)], axis=0)
-    moved = spread_exact(tiles, onehot, (0,))
-    out_ref[...] = jnp.sum(jnp.where(iota((128, rows), 0) == rank, moved, 0.0), axis=0, keepdims=True)
-    flag_ref[...] = jnp.max(tiles, axis=0, keepdims=True)
+    flag_ref[...] = jnp.max(jnp.max(back_ref[:, CAP:], axis=0, keepdims=True), axis=1, keepdims=True)
+    onehot = ((iota((3 * OWNERS, rows), 0) & (OWNERS - 1)) == ids).astype(BF16)
+    tiles = back_ref[...]
+    moved = lax.dot_general(
+        three_parts(tiles), onehot, (((0,), (0,)), ((), ())), preferred_element_type=F32
+    )[0:CAP, :]
+    out_ref[...] = jnp.sum(jnp.where(iota((CAP, rows), 0) == rank, moved, 0.0), axis=0, keepdims=True)
 
 
 def pick(back, meta):
@@ -259,7 +268,7 @@
         pick_kernel,
         out_shape=(
             jax.ShapeDtypeStruct((1, meta.shape[1]), F32),
-            jax.ShapeDtypeStruct((1, 128), F32),
+            jax.ShapeDtypeStruct((1, 1), F32),
         ),
         compiler_params=params(),
         name="pick",
@@ -294,16 +303,16 @@
     return lax.ppermute(block, "pair", perm)
 
 
-def give_back(own, sib, nxt, last, meta, *spot):
+def give_back(own, sib, nxt, last, meta, *onehot):
     tiles = join(
         own,
         along_pair(sib, swap_cores()),
         along_pair(nxt, inverse(from_next())),
         along_pair(last, inverse(from_last())),
-        *spot,
-    )
-    back = lax.all_to_all(tiles.reshape(OWNERS, 8, 128), "wide", split_axis=0, concat_axis=0, tiled=True)
-    return pick(back.reshape(OWNERS * 8, 128), meta)
+        *onehot,
+    )
+    back = lax.all_to_all(tiles.reshape(OWNERS, 1, 128), "wide", split_axis=0, concat_axis=0, tiled=True)
+    return pick(back.reshape(OWNERS, 128), meta)
 
 
 EARLY = (
@@ -320,7 +329,7 @@
 def match(a, second, tails):
     own_a, sib_a, next_a, last_a = a
     own_b, sib_b, next_b, last_b = second
-    width = CHUNK + own_b.shape[0]
+    width = CHUNK + lanes(own_b.shape[0])
     before = pairs(
         EARLY,
         (own_a, own_b, sib_a, sib_b, next_a, last_a),
@@ -369,11 +378,11 @@
 def per_device(embeddings, cluster_ids):
     ids = cluster_ids.reshape(1, -1)
     a, own_b, meta = exchange(embeddings, ids)
-    packed, spot = pack(own_b)
+    packed, onehot = pack(own_b)
     best = match(a, neighbours(packed), (1, 3, 6, 7))
-    value, flag = give_back(*best, meta, spot)
+    value, flag = give_back(*best, meta, onehot)
     return lax.cond(
-        flag[0, CAP] > 0.5, lambda: whole(embeddings, ids), lambda: value
+        flag.reshape(()) > 0.5, lambda: whole(embeddings, ids), lambda: value
     ).reshape(-1)
 
 

time: 92 us -> 88.7 us (0.964)
  waiting for transfers between devices: 17.6 us -> 15.3 us
    ppermute x9, waiting for transfers between devices: 9.97 us -> 7.75 us  [along_pair(): return lax.ppermute(block, 'pair', perm)]
  transfers between devices with their start and end apart: 10 -> 10, of which waited for: 4 -> 4; matrix products, arithmetic and copies ran while one was open for 0% -> 0% of each run, Pallas kernels for 6% -> 7%
where the time goes in v3:
time: 88.7 us; the launch traced here: 88.5 us
  blocking collectives  45.2 us (51%)
  waiting for transfers between devices  15.3 us (17%)
  starting transfers between devices  14.6 us (16%)
  Pallas kernels  12.5 us (14%)
    all_to_all x2, blocking collectives, to_owners(): lax.all_to_all(block, 'wide', split_axis=0, concat_axis=0, tiled=True)  45.2 us
    ppermute x9, starting transfers between devices, along_pair(): return lax.ppermute(block, 'pair', perm)  10.8 us
    ppermute x9, waiting for transfers between devices, along_pair(): return lax.ppermute(block, 'pair', perm)  7.75 us
    all_to_all x1, waiting for transfers between devices, give_back(): lax.all_to_all(tiles.reshape(OWNERS, 1, 128), 'wide', split_axis=0, conca...  7.56 us
    pallas_call x2, Pallas kernels, pairs(): pl.pallas_call(functools.partial(pair_kernel, units, n, len(before), want...  6.87 us
    all_to_all x1, starting transfers between devices, give_back(): lax.all_to_all(tiles.reshape(OWNERS, 1, 128), 'wide', split_axis=0, conca...  3.83 us
    pallas_call x1, Pallas kernels, prep(): pl.pallas_call(prep_kernel, in_specs=[pl.BlockSpec(memory_space=pltpu.HBM...  2.46 us
  transfers between devices with their start and end apart: 10, of which 4 were waited for; matrix products, arithmetic and copies ran while one was open for 0% of the time, Pallas kernels for 7%

profile of v3, /device:TPU:0, one launch (start us, length us, event | category | flops | bytes accessed | tf_op | source)
XLA Modules:
  0.0 88.5 jit_solution(13457802636939218353)
XLA Ops:
  0.0 2.5 %prep.3 = (bf16[512,1024]{1,0:T(8,128)(2,1)S(1)}, bf16[512,1024]{1,0:T(8,128)(2,1)S(1)}, s32[8,512]{1,0:T(8,128)S(1)}) custom-call(f32[512,1024]{1,0:T(8,128)} %x_hbm.1, s32[1,512]{1,0:T(1,128)} %bitcast.43), custom_call_target="tpu_custom_call" | custom-call | flops 536870912 | bytes 4194304 | tf_op jit(solution)/shard_map/prep/pallas_call | solution.py:78
  2.5 23.8 %all_to_all.30 = bf16[16,32,1024]{2,1,0:T(8,128)(2,1)S(1)} all-to-all(bf16[16,32,1024]{2,1,0:T(8,128)(2,1)S(1)} %bitcast.38), channel_id=1, replica_groups=mesh['wide'=16,'pair'=8] {'wide'}, dimensions={0} | all-to-all | bytes 2097152 | tf_op jit(solution)/shard_map/all_to_all | solution.py:299
  26.2 1.9 %collective-permute-start.11 = (bf16[512,1024]{1,0:T(8,128)(2,1)S(1)}, bf16[512,1024]{1,0:T(8,128)(2,1)S(1)}, u32[]{:S(2)}, u32[]{:S(2)}) collective-permute-start(bf16[512,1024]{1,0:T(8,128)(2,1)S(1)} %bitcast.23), channel_id=1, source_target_pairs={{6,0},{7,1},{0,2},{1,3},{3,4},{2,5},{5,6},{4,7},{14,8},{15,9},{8,1... | collective-permute-start | bytes 3145736 | tf_op jit(solution)/shard_map/ppermute | solution.py:303
  28.1 2.1 %collective-permute-start.10 = (bf16[512,1024]{1,0:T(8,128)(2,1)S(1)}, bf16[512,1024]{1,0:T(8,128)(2,1)S(1)}, u32[]{:S(2)}, u32[]{:S(2)}) collective-permute-start(bf16[512,1024]{1,0:T(8,128)(2,1)S(1)} %bitcast.24), channel_id=1, source_target_pairs={{2,0},{3,1},{4,2},{5,3},{6,4},{7,5},{0,6},{1,7},{10,8},{11,9},{12,... | collective-permute-start | bytes 3145736 | tf_op jit(solution)/shard_map/ppermute | solution.py:303
  30.3 0.0 collective-permute-start.9
  30.3 0.8 rest.3
  31.1 21.4 %all_to_all.31 = bf16[16,32,1024]{2,1,0:T(8,128)(2,1)S(1)} all-to-all(bf16[16,32,1024]{2,1,0:T(8,128)(2,1)S(1)} %bitcast.21), channel_id=1, replica_groups=mesh['wide'=16,'pair'=8] {'wide'}, dimensions={0} | all-to-all | bytes 2097152 | tf_op jit(solution)/shard_map/all_to_all | solution.py:299
  52.5 0.0 collective-permute-done.11.refs_5_
  52.5 0.9 %collective-permute-done.10.refs_4_ = bf16[512,1024]{1,0:T(8,128)(2,1)S(1)} collective-permute-done((bf16[512,1024]{1,0:T(8,128)(2,1)S(1)}, bf16[512,1024]{1,0:T(8,128)(2,1)S(1)}, u32[]{:S(2)}, u32[]{:S(2)}) %collective-permute-start.10) | collective-permute-done | bytes 1048608 | tf_op jit(solution)/shard_map/ppermute | solution.py:303
  53.5 0.0 collective-permute-done.9.refs_2_
  53.5 0.7 pack.1
  54.2 0.1 collective-permute-start.12
  54.3 0.6 collective-permute-start.14
  54.9 2.7 %collective-permute-start.13 = (bf16[208,1024]{1,0:T(8,128)(2,1)S(1)}, bf16[208,1024]{1,0:T(8,128)(2,1)S(1)}, u32[]{:S(2)}, u32[]{:S(2)}) collective-permute-start(bf16[208,1024]{1,0:T(8,128)(2,1)S(1)} %get-tuple-element.65.refs_1_), channel_id=1, source_target_pairs={{2,0},{3,1},{4,2},{5,3},{6,4},{7,5},{0,6},{1,7},{10,8},{11,9},{12,... | collective-permute-start | bytes 1277960 | tf_op jit(solution)/shard_map/ppermute | solution.py:303
  57.6 0.0 collective-permute-done.12.refs_3_
  57.6 4.9 %early.3 = (f32[1,896]{1,0:T(1,128)S(1)}, f32[1,896]{1,0:T(1,128)S(1)}, f32[1,896]{1,0:T(1,128)S(1)}, f32[1,896]{1,0:T(1,128)S(1)}) custom-call(bf16[512,1024]{1,0:T(8,128)(2,1)S(1)} %bitcast.26, bf16[208,1024]{1,0:T(8,128)(2,1)S(1)} %get-tuple-element.65.refs_1_, bf16[512,1024]{1,0:T(8,128)(2,1)S(1)} %collective-permute-done.9.refs_2_, ...), custom_call_target="tpu_custom_call" | custom-call | flops 3952082944 | bytes 6291456 | tf_op jit(solution)/shard_map/early/pallas_call | solution.py:203
  62.5 5.2 %collective-permute-done.14.refs_7_ = bf16[208,1024]{1,0:T(8,128)(2,1)S(1)} collective-permute-done((bf16[208,1024]{1,0:T(8,128)(2,1)S(1)}, bf16[208,1024]{1,0:T(8,128)(2,1)S(1)}, u32[]{:S(2)}, u32[]{:S(2)}) %collective-permute-start.14) | collective-permute-done | bytes 426016 | tf_op jit(solution)/shard_map/ppermute | solution.py:303
  67.8 0.0 collective-permute-done.13.refs_6_
  67.8 0.0 copy-start
  67.8 0.0 copy-start.1
  67.8 2.0 %late.3 = (f32[1,896]{1,0:T(1,128)S(1)}, f32[1,896]{1,0:T(1,128)S(1)}, f32[1,896]{1,0:T(1,128)S(1)}, f32[1,896]{1,0:T(1,128)S(1)}) custom-call(bf16[512,1024]{1,0:T(8,128)(2,1)S(1)} %bitcast.27, bf16[208,1024]{1,0:T(8,128)(2,1)S(1)} %get-tuple-element.65.refs_1_, bf16[512,1024]{1,0:T(8,128)(2,1)S(1)} %collective-permute-done.9.refs_2_, ...), custom_call_target="tpu_custom_call" | custom-call | flops 1138229248 | bytes 8388608 | tf_op jit(solution)/shard_map/late/pallas_call | solution.py:203
  69.7 0.1 collective-permute-start.15
  69.8 0.9 collective-permute-start.16
  70.7 2.4 %collective-permute-start.17 = (f32[1,896]{1,0:T(1,128)S(1)}, f32[1,896]{1,0:T(1,128)S(1)}, u32[]{:S(2)}, u32[]{:S(2)}) collective-permute-start(f32[1,896]{1,0:T(1,128)S(1)} %get-tuple-element.76), channel_id=1, source_target_pairs={{0,6},{1,7},{2,0},{3,1},{4,3},{5,2},{6,5},{7,4},{8,14},{9,15},{10,... | collective-permute-start | bytes 10760 | tf_op jit(solution)/shard_map/ppermute | solution.py:303
  73.1 0.0 collective-permute-done.15.a_ref
  73.1 1.6 %collective-permute-done.16.b_ref = f32[1,896]{1,0:T(1,128)S(1)} collective-permute-done((f32[1,896]{1,0:T(1,128)S(1)}, f32[1,896]{1,0:T(1,128)S(1)}, u32[]{:S(2)}, u32[]{:S(2)}) %collective-permute-start.16) | collective-permute-done | bytes 3616 | tf_op jit(solution)/shard_map/ppermute | solution.py:303
  74.7 0.0 collective-permute-done.17.c_ref
  74.7 0.8 join.3
  75.5 3.8 %all-to-all-start.5 = ((f32[16,1,128]{2,1,0:T(1,128)}), f32[16,1,128]{2,1,0:T(1,128)S(1)}, u32[]{:S(2)}, u32[]{:S(2)}) async-start(f32[16,1,128]{2,1,0:T(1,128)} %bitcast.16), calls=%async_computation.5 | async-start | bytes 16384 | tf_op jit(solution)/shard_map/all_to_all | solution.py:314
  79.4 7.6 %all-to-all-done.5 = f32[16,1,128]{2,1,0:T(1,128)S(1)} async-done(((f32[16,1,128]{2,1,0:T(1,128)}), f32[16,1,128]{2,1,0:T(1,128)S(1)}, u32[]{:S(2)}, u32[]{:S(2)}) %all-to-all-start.5) | async-done | bytes 8224 | tf_op jit(solution)/shard_map/all_to_all | solution.py:314
  86.9 0.8 pick.3
  88.3 0.0 copy-done
  88.3 0.0 copy-done.1
  (1 shorter events, 0.0 us)
Async XLA Ops:
  26.2 26.3 %collective-permute-start.11 = (bf16[512,1024]{1,0:T(8,128)(2,1)S(1)}, bf16[512,1024]{1,0:T(8,128)(2,1)S(1)}, u32[]{:S(2)}, u32[]{:S(2)}) collective-permute-start(bf16[512,1024]{1,0:T(8,128)(2,1)S(1)} %bitcast.23), channel_id=1, source_target_pairs={{6,0},{7,1},{0,2},{1,3},{3,4},{2,5},{5,6},{4,7},{14,8},{15,9},{8,1... | collective-permute-start | bytes 3145736 | tf_op jit(solution)/shard_map/ppermute | solution.py:303
  28.1 25.4 %collective-permute-start.10 = (bf16[512,1024]{1,0:T(8,128)(2,1)S(1)}, bf16[512,1024]{1,0:T(8,128)(2,1)S(1)}, u32[]{:S(2)}, u32[]{:S(2)}) collective-permute-start(bf16[512,1024]{1,0:T(8,128)(2,1)S(1)} %bitcast.24), channel_id=1, source_target_pairs={{2,0},{3,1},{4,2},{5,3},{6,4},{7,5},{0,6},{1,7},{10,8},{11,9},{12,... | collective-permute-start | bytes 3145736 | tf_op jit(solution)/shard_map/ppermute | solution.py:303
  30.3 23.2 %collective-permute-start.9 = (bf16[512,1024]{1,0:T(8,128)(2,1)S(1)}, bf16[512,1024]{1,0:T(8,128)(2,1)S(1)}, u32[]{:S(2)}, u32[]{:S(2)}) collective-permute-start(bf16[512,1024]{1,0:T(8,128)(2,1)S(1)} %bitcast.25), channel_id=1, source_target_pairs={{0,1},{1,0},{2,3},{3,2},{4,5},{5,4},{6,7},{7,6},{8,9},{9,8},{10,11... | collective-permute-start | bytes 3145736 | tf_op jit(solution)/shard_map/ppermute | solution.py:303
  54.2 3.4 %collective-permute-start.12 = (bf16[208,1024]{1,0:T(8,128)(2,1)S(1)}, bf16[208,1024]{1,0:T(8,128)(2,1)S(1)}, u32[]{:S(2)}, u32[]{:S(2)}) collective-permute-start(bf16[208,1024]{1,0:T(8,128)(2,1)S(1)} %get-tuple-element.65.refs_1_), channel_id=1, source_target_pairs={{0,1},{1,0},{2,3},{3,2},{4,5},{5,4},{6,7},{7,6},{8,9},{9,8},{10,11... | collective-permute-start | bytes 1277960 | tf_op jit(solution)/shard_map/ppermute | solution.py:303
  54.3 13.4 %collective-permute-start.14 = (bf16[208,1024]{1,0:T(8,128)(2,1)S(1)}, bf16[208,1024]{1,0:T(8,128)(2,1)S(1)}, u32[]{:S(2)}, u32[]{:S(2)}) collective-permute-start(bf16[208,1024]{1,0:T(8,128)(2,1)S(1)} %get-tuple-element.65.refs_1_), channel_id=1, source_target_pairs={{6,0},{7,1},{0,2},{1,3},{3,4},{2,5},{5,6},{4,7},{14,8},{15,9},{8,1... | collective-permute-start | bytes 1277960 | tf_op jit(solution)/shard_map/ppermute | solution.py:303
  54.9 12.9 %collective-permute-start.13 = (bf16[208,1024]{1,0:T(8,128)(2,1)S(1)}, bf16[208,1024]{1,0:T(8,128)(2,1)S(1)}, u32[]{:S(2)}, u32[]{:S(2)}) collective-permute-start(bf16[208,1024]{1,0:T(8,128)(2,1)S(1)} %get-tuple-element.65.refs_1_), channel_id=1, source_target_pairs={{2,0},{3,1},{4,2},{5,3},{6,4},{7,5},{0,6},{1,7},{10,8},{11,9},{12,... | collective-permute-start | bytes 1277960 | tf_op jit(solution)/shard_map/ppermute | solution.py:303
  67.8 20.5 %copy-start = (f32[512,1024]{1,0:T(8,128)S(1)}, f32[512,1024]{1,0:T(8,128)}, u32[]{:S(2)}) copy-start(f32[512,1024]{1,0:T(8,128)} %x_hbm.1) | copy-start | bytes 6291460
  67.8 20.5 %copy-start.1 = (s32[512]{0:T(512)S(1)}, s32[512]{0:T(512)}, u32[]{:S(2)}) copy-start(s32[512]{0:T(512)} %param.5) | copy-start | bytes 6148
  69.7 3.4 %collective-permute-start.15 = (f32[1,896]{1,0:T(1,128)S(1)}, f32[1,896]{1,0:T(1,128)S(1)}, u32[]{:S(2)}, u32[]{:S(2)}) collective-permute-start(f32[1,896]{1,0:T(1,128)S(1)} %get-tuple-element.74), channel_id=1, source_target_pairs={{0,1},{1,0},{2,3},{3,2},{4,5},{5,4},{6,7},{7,6},{8,9},{9,8},{10,11... | collective-permute-start | bytes 10760 | tf_op jit(solution)/shard_map/ppermute | solution.py:303
  69.8 4.9 %collective-permute-start.16 = (f32[1,896]{1,0:T(1,128)S(1)}, f32[1,896]{1,0:T(1,128)S(1)}, u32[]{:S(2)}, u32[]{:S(2)}) collective-permute-start(f32[1,896]{1,0:T(1,128)S(1)} %get-tuple-element.75), channel_id=1, source_target_pairs={{0,2},{1,3},{2,4},{3,5},{4,6},{5,7},{6,0},{7,1},{8,10},{9,11},{10,... | collective-permute-start | bytes 10760 | tf_op jit(solution)/shard_map/ppermute | solution.py:303
  70.7 4.0 %collective-permute-start.17 = (f32[1,896]{1,0:T(1,128)S(1)}, f32[1,896]{1,0:T(1,128)S(1)}, u32[]{:S(2)}, u32[]{:S(2)}) collective-permute-start(f32[1,896]{1,0:T(1,128)S(1)} %get-tuple-element.76), channel_id=1, source_target_pairs={{0,6},{1,7},{2,0},{3,1},{4,3},{5,2},{6,5},{7,4},{8,14},{9,15},{10,... | collective-permute-start | bytes 10760 | tf_op jit(solution)/shard_map/ppermute | solution.py:303
  75.5 11.4 %all-to-all-start.5 = ((f32[16,1,128]{2,1,0:T(1,128)}), f32[16,1,128]{2,1,0:T(1,128)S(1)}, u32[]{:S(2)}, u32[]{:S(2)}) async-start(f32[16,1,128]{2,1,0:T(1,128)} %bitcast.16), calls=%async_computation.5 | async-start | bytes 16384 | tf_op jit(solution)/shard_map/all_to_all | solution.py:314

commit v4 on v3

--- a/solution.py
+++ b/solution.py
@@ -20,7 +20,7 @@
 
 
 def params():
-    return pltpu.CompilerParams(vmem_limit_bytes=40 * 1024 * 1024)
+    return pltpu.CompilerParams(vmem_limit_bytes=24 * 1024 * 1024)
 
 
 def cost(flops, bytes_accessed):
@@ -148,13 +148,19 @@
     before = refs[n_blocks : n_blocks + n_before]
     outs = refs[n_blocks + n_before : n_blocks + n_before + len(wanted)]
     lane_bias, row_bias, over_lanes, over_rows = refs[n_blocks + n_before + len(wanted) :]
-    for b, block in enumerate(blocks):
-        rows = block.shape[0]
-        bias = jnp.where(marked(block[:, 0:128]), LOW, 0.0)
+    lefts = sorted({left for left, _, _ in units})
+    rights = sorted({right for _, right, mode in units if mode == "both"})
+    for b in sorted({b for unit in units for b in unit[0:2]}):
+        rows = blocks[b].shape[0]
+        bias = jnp.where(marked(blocks[b][:, 0:128]), LOW, 0.0)
         lane_bias[b, 0:rows] = jnp.broadcast_to(bias, (rows, 128))
-        row_bias[b, :, 0 : lanes(rows)] = jnp.transpose(lane_bias[b, 0 : lanes(rows)])[0:8, :]
-        over_lanes[b, 0 : lanes(rows)] = jnp.full((lanes(rows), 128), LOW, F32)
-        over_rows[b, :, 0 : lanes(rows)] = jnp.full((8, lanes(rows)), LOW, F32)
+        if any(b == right for _, right, _ in units):
+            turned = jnp.transpose(lane_bias[b, 0 : lanes(rows)])
+            row_bias[b, :, 0 : lanes(rows)] = turned[0:8, :]
+        if b in lefts:
+            over_lanes[b, 0 : lanes(rows)] = jnp.full((lanes(rows), 128), LOW, F32)
+        if b in rights:
+            over_rows[b, :, 0 : lanes(rows)] = jnp.full((8, lanes(rows)), LOW, F32)
     for left, right, mode in units:
         n_left, n_right = blocks[left].shape[0], blocks[right].shape[0]
         scores = lax.dot_general(
@@ -187,8 +193,9 @@
     for (first, second, earlier), out in zip(wanted, outs):
         for b, at, n in ((first, 0, CHUNK), (second, CHUNK, out.shape[1] - CHUNK - 128)):
             part = jnp.full((1, n), LOW, F32)
-            if b is not None:
+            if b in lefts:
                 part = jnp.max(jnp.transpose(over_lanes[b, 0:n]), axis=0, keepdims=True)
+            if b in rights:
                 part = jnp.maximum(part, jnp.max(over_rows[b, :, 0:n], axis=0, keepdims=True))
             if earlier is not None:
                 part = jnp.maximum(part, before[earlier][:, at : at + n])
@@ -318,12 +325,9 @@
 EARLY = (
     (0, 0, "self"), (0, 2, "left"), (0, 4, "both"), (2, 4, "both"), (5, 4, "both"),
     (0, 1, "both"), (1, 1, "self"), (0, 3, "left"), (1, 2, "left"), (1, 3, "left"),
-    (1, 4, "both"), (3, 4, "both"),
+    (1, 4, "both"), (3, 4, "both"), (1, 5, "both"), (3, 5, "both"),
 )
-LATE = (
-    (0, 6, "both"), (1, 6, "both"), (2, 6, "both"), (3, 6, "both"),
-    (5, 6, "both"), (7, 4, "both"), (7, 6, "both"),
-)
+LATE = ((5, 6, "both"), (7, 4, "both"), (1, 6, "both"), (3, 6, "both"), (7, 6, "both"))
 
 
 def match(a, second, tails):
@@ -364,13 +368,12 @@
     own_a = to_owners(first)
     own_a, unit = lax.optimization_barrier((own_a, unit))
     a = neighbours(own_a)
-    own_b = to_owners(rest(unit, meta))
-    own_b, *a = lax.optimization_barrier((own_b, *a))
-    return tuple(a), own_b, meta
+    return a, to_owners(rest(unit, meta)), meta
 
 
 def whole(embeddings, ids):
     a, own_b, meta = exchange(embeddings, ids)
+    own_b, *a = lax.optimization_barrier((own_b, *a))
     best = match(a, neighbours(own_b), ())
     return give_back(*best, meta)[0]
 
@@ -379,6 +382,7 @@
     ids = cluster_ids.reshape(1, -1)
     a, own_b, meta = exchange(embeddings, ids)
     packed, onehot = pack(own_b)
+    packed, *a = lax.optimization_barrier((packed, *a))
     best = match(a, neighbours(packed), (1, 3, 6, 7))
     value, flag = give_back(*best, meta, onehot)
     return lax.cond(

time: 88.7 us -> 87.3 us (0.984)
  waiting for transfers between devices: 15.3 us -> 13.9 us
    ppermute x9, waiting for transfers between devices: 7.75 us -> 6.37 us  [along_pair(): return lax.ppermute(block, 'pair', perm)]
  transfers between devices with their start and end apart: 10 -> 10, of which waited for: 4 -> 4; matrix products, arithmetic and copies ran while one was open for 0% -> 0% of each run, Pallas kernels for 7% -> 8%
where the time goes in v4:
time: 87.3 us; the launch traced here: 87 us
  blocking collectives  45.2 us (52%)
  starting transfers between devices  14.5 us (17%)
  waiting for transfers between devices  13.9 us (16%)
  Pallas kernels  12.6 us (14%)
    all_to_all x2, blocking collectives, to_owners(): lax.all_to_all(block, 'wide', split_axis=0, concat_axis=0, tiled=True)  45.2 us
    ppermute x9, starting transfers between devices, along_pair(): return lax.ppermute(block, 'pair', perm)  10.7 us
    all_to_all x1, waiting for transfers between devices, give_back(): lax.all_to_all(tiles.reshape(OWNERS, 1, 128), 'wide', split_axis=0, conca...  7.56 us
    pallas_call x2, Pallas kernels, pairs(): pl.pallas_call(functools.partial(pair_kernel, units, n, len(before), want...  6.96 us
    ppermute x9, waiting for transfers between devices, along_pair(): return lax.ppermute(block, 'pair', perm)  6.37 us
    all_to_all x1, starting transfers between devices, give_back(): lax.all_to_all(tiles.reshape(OWNERS, 1, 128), 'wide', split_axis=0, conca...  3.83 us
    pallas_call x1, Pallas kernels, prep(): pl.pallas_call(prep_kernel, in_specs=[pl.BlockSpec(memory_space=pltpu.HBM...  2.46 us
  transfers between devices with their start and end apart: 10, of which 4 were waited for; matrix products, arithmetic and copies ran while one was open for 0% of the time, Pallas kernels for 8%

profile of v4, /device:TPU:0, one launch (start us, length us, event | category | flops | bytes accessed | tf_op | source)
XLA Modules:
  0.0 87.0 jit_solution(7489451459873313948)
XLA Ops:
  0.0 2.5 %prep.3 = (bf16[512,1024]{1,0:T(8,128)(2,1)S(1)}, bf16[512,1024]{1,0:T(8,128)(2,1)S(1)}, s32[8,512]{1,0:T(8,128)S(1)}) custom-call(f32[512,1024]{1,0:T(8,128)} %x_hbm.1, s32[1,512]{1,0:T(1,128)} %bitcast.43), custom_call_target="tpu_custom_call" | custom-call | flops 536870912 | bytes 4194304 | tf_op jit(solution)/shard_map/prep/pallas_call | solution.py:78
  2.5 23.8 %all_to_all.30 = bf16[16,32,1024]{2,1,0:T(8,128)(2,1)S(1)} all-to-all(bf16[16,32,1024]{2,1,0:T(8,128)(2,1)S(1)} %bitcast.38), channel_id=1, replica_groups=mesh['wide'=16,'pair'=8] {'wide'}, dimensions={0} | all-to-all | bytes 2097152 | tf_op jit(solution)/shard_map/all_to_all | solution.py:306
  26.2 1.9 %collective-permute-start.11 = (bf16[512,1024]{1,0:T(8,128)(2,1)S(1)}, bf16[512,1024]{1,0:T(8,128)(2,1)S(1)}, u32[]{:S(2)}, u32[]{:S(2)}) collective-permute-start(bf16[512,1024]{1,0:T(8,128)(2,1)S(1)} %bitcast.23), channel_id=1, source_target_pairs={{6,0},{7,1},{0,2},{1,3},{3,4},{2,5},{5,6},{4,7},{14,8},{15,9},{8,1... | collective-permute-start | bytes 3145736 | tf_op jit(solution)/shard_map/ppermute | solution.py:310
  28.1 2.1 %collective-permute-start.10 = (bf16[512,1024]{1,0:T(8,128)(2,1)S(1)}, bf16[512,1024]{1,0:T(8,128)(2,1)S(1)}, u32[]{:S(2)}, u32[]{:S(2)}) collective-permute-start(bf16[512,1024]{1,0:T(8,128)(2,1)S(1)} %bitcast.24), channel_id=1, source_target_pairs={{2,0},{3,1},{4,2},{5,3},{6,4},{7,5},{0,6},{1,7},{10,8},{11,9},{12,... | collective-permute-start | bytes 3145736 | tf_op jit(solution)/shard_map/ppermute | solution.py:310
  30.3 0.0 collective-permute-start.9
  30.3 0.8 rest.3
  31.1 21.4 %all_to_all.31 = bf16[16,32,1024]{2,1,0:T(8,128)(2,1)S(1)} all-to-all(bf16[16,32,1024]{2,1,0:T(8,128)(2,1)S(1)} %bitcast.21), channel_id=1, replica_groups=mesh['wide'=16,'pair'=8] {'wide'}, dimensions={0} | all-to-all | bytes 2097152 | tf_op jit(solution)/shard_map/all_to_all | solution.py:306
  52.5 0.7 pack.1
  53.3 0.0 collective-permute-done.11.refs_5_
  53.3 0.2 collective-permute-done.10.refs_4_
  53.5 0.0 collective-permute-done.9.refs_2_
  53.5 0.0 collective-permute-start.12
  53.5 0.6 collective-permute-start.14
  54.1 2.7 %collective-permute-start.13 = (bf16[208,1024]{1,0:T(8,128)(2,1)S(1)}, bf16[208,1024]{1,0:T(8,128)(2,1)S(1)}, u32[]{:S(2)}, u32[]{:S(2)}) collective-permute-start(bf16[208,1024]{1,0:T(8,128)(2,1)S(1)} %get-tuple-element.65.refs_1_), channel_id=1, source_target_pairs={{2,0},{3,1},{4,2},{5,3},{6,4},{7,5},{0,6},{1,7},{10,8},{11,9},{12,... | collective-permute-start | bytes 1277960 | tf_op jit(solution)/shard_map/ppermute | solution.py:310
  56.8 0.0 collective-permute-done.12.refs_3_
  56.8 5.6 %early.3 = (f32[1,896]{1,0:T(1,128)S(1)}, f32[1,896]{1,0:T(1,128)S(1)}, f32[1,896]{1,0:T(1,128)S(1)}, f32[1,896]{1,0:T(1,128)S(1)}) custom-call(bf16[512,1024]{1,0:T(8,128)(2,1)S(1)} %bitcast.26, bf16[208,1024]{1,0:T(8,128)(2,1)S(1)} %get-tuple-element.65.refs_1_, bf16[512,1024]{1,0:T(8,128)(2,1)S(1)} %collective-permute-done.9.refs_2_, ...), custom_call_target="tpu_custom_call" | custom-call | flops 4388290560 | bytes 6291456 | tf_op jit(solution)/shard_map/early/pallas_call | solution.py:210
  62.4 4.6 %collective-permute-done.14.refs_7_ = bf16[208,1024]{1,0:T(8,128)(2,1)S(1)} collective-permute-done((bf16[208,1024]{1,0:T(8,128)(2,1)S(1)}, bf16[208,1024]{1,0:T(8,128)(2,1)S(1)}, u32[]{:S(2)}, u32[]{:S(2)}) %collective-permute-start.14) | collective-permute-done | bytes 426016 | tf_op jit(solution)/shard_map/ppermute | solution.py:310
  66.9 0.0 collective-permute-done.13.refs_6_
  66.9 0.0 copy-start
  66.9 0.0 copy-start.1
  66.9 1.4 %late.3 = (f32[1,896]{1,0:T(1,128)S(1)}, f32[1,896]{1,0:T(1,128)S(1)}, f32[1,896]{1,0:T(1,128)S(1)}, f32[1,896]{1,0:T(1,128)S(1)}) custom-call(bf16[512,1024]{1,0:T(8,128)(2,1)S(1)} %bitcast.27, bf16[208,1024]{1,0:T(8,128)(2,1)S(1)} %get-tuple-element.65.refs_1_, bf16[512,1024]{1,0:T(8,128)(2,1)S(1)} %collective-permute-done.9.refs_2_, ...), custom_call_target="tpu_custom_call" | custom-call | flops 702021632 | bytes 8388608 | tf_op jit(solution)/shard_map/late/pallas_call | solution.py:210
  68.3 0.1 collective-permute-start.15
  68.4 0.9 %collective-permute-start.16 = (f32[1,896]{1,0:T(1,128)S(1)}, f32[1,896]{1,0:T(1,128)S(1)}, u32[]{:S(2)}, u32[]{:S(2)}) collective-permute-start(f32[1,896]{1,0:T(1,128)S(1)} %get-tuple-element.75), channel_id=1, source_target_pairs={{0,2},{1,3},{2,4},{3,5},{4,6},{5,7},{6,0},{7,1},{8,10},{9,11},{10,... | collective-permute-start | bytes 10760 | tf_op jit(solution)/shard_map/ppermute | solution.py:310
  69.3 2.4 %collective-permute-start.17 = (f32[1,896]{1,0:T(1,128)S(1)}, f32[1,896]{1,0:T(1,128)S(1)}, u32[]{:S(2)}, u32[]{:S(2)}) collective-permute-start(f32[1,896]{1,0:T(1,128)S(1)} %get-tuple-element.76), channel_id=1, source_target_pairs={{0,6},{1,7},{2,0},{3,1},{4,3},{5,2},{6,5},{7,4},{8,14},{9,15},{10,... | collective-permute-start | bytes 10760 | tf_op jit(solution)/shard_map/ppermute | solution.py:310
  71.7 0.0 collective-permute-done.15.a_ref
  71.7 1.6 %collective-permute-done.16.b_ref = f32[1,896]{1,0:T(1,128)S(1)} collective-permute-done((f32[1,896]{1,0:T(1,128)S(1)}, f32[1,896]{1,0:T(1,128)S(1)}, u32[]{:S(2)}, u32[]{:S(2)}) %collective-permute-start.16) | collective-permute-done | bytes 3616 | tf_op jit(solution)/shard_map/ppermute | solution.py:310
  73.3 0.0 collective-permute-done.17.c_ref
  73.3 0.8 join.3
  74.1 3.8 %all-to-all-start.5 = ((f32[16,1,128]{2,1,0:T(1,128)}), f32[16,1,128]{2,1,0:T(1,128)S(1)}, u32[]{:S(2)}, u32[]{:S(2)}) async-start(f32[16,1,128]{2,1,0:T(1,128)} %bitcast.16), calls=%async_computation.5 | async-start | bytes 16384 | tf_op jit(solution)/shard_map/all_to_all | solution.py:321
  77.9 7.6 %all-to-all-done.5 = f32[16,1,128]{2,1,0:T(1,128)S(1)} async-done(((f32[16,1,128]{2,1,0:T(1,128)}), f32[16,1,128]{2,1,0:T(1,128)S(1)}, u32[]{:S(2)}, u32[]{:S(2)}) %all-to-all-start.5) | async-done | bytes 8224 | tf_op jit(solution)/shard_map/all_to_all | solution.py:321
  85.5 0.8 pick.3
  86.9 0.0 copy-done
  86.9 0.0 copy-done.1
  (1 shorter events, 0.0 us)
Async XLA Ops:
  26.2 27.0 %collective-permute-start.11 = (bf16[512,1024]{1,0:T(8,128)(2,1)S(1)}, bf16[512,1024]{1,0:T(8,128)(2,1)S(1)}, u32[]{:S(2)}, u32[]{:S(2)}) collective-permute-start(bf16[512,1024]{1,0:T(8,128)(2,1)S(1)} %bitcast.23), channel_id=1, source_target_pairs={{6,0},{7,1},{0,2},{1,3},{3,4},{2,5},{5,6},{4,7},{14,8},{15,9},{8,1... | collective-permute-start | bytes 3145736 | tf_op jit(solution)/shard_map/ppermute | solution.py:310
  28.1 25.4 %collective-permute-start.10 = (bf16[512,1024]{1,0:T(8,128)(2,1)S(1)}, bf16[512,1024]{1,0:T(8,128)(2,1)S(1)}, u32[]{:S(2)}, u32[]{:S(2)}) collective-permute-start(bf16[512,1024]{1,0:T(8,128)(2,1)S(1)} %bitcast.24), channel_id=1, source_target_pairs={{2,0},{3,1},{4,2},{5,3},{6,4},{7,5},{0,6},{1,7},{10,8},{11,9},{12,... | collective-permute-start | bytes 3145736 | tf_op jit(solution)/shard_map/ppermute | solution.py:310
  30.3 23.2 %collective-permute-start.9 = (bf16[512,1024]{1,0:T(8,128)(2,1)S(1)}, bf16[512,1024]{1,0:T(8,128)(2,1)S(1)}, u32[]{:S(2)}, u32[]{:S(2)}) collective-permute-start(bf16[512,1024]{1,0:T(8,128)(2,1)S(1)} %bitcast.25), channel_id=1, source_target_pairs={{0,1},{1,0},{2,3},{3,2},{4,5},{5,4},{6,7},{7,6},{8,9},{9,8},{10,11... | collective-permute-start | bytes 3145736 | tf_op jit(solution)/shard_map/ppermute | solution.py:310
  53.5 3.3 %collective-permute-start.12 = (bf16[208,1024]{1,0:T(8,128)(2,1)S(1)}, bf16[208,1024]{1,0:T(8,128)(2,1)S(1)}, u32[]{:S(2)}, u32[]{:S(2)}) collective-permute-start(bf16[208,1024]{1,0:T(8,128)(2,1)S(1)} %get-tuple-element.65.refs_1_), channel_id=1, source_target_pairs={{0,1},{1,0},{2,3},{3,2},{4,5},{5,4},{6,7},{7,6},{8,9},{9,8},{10,11... | collective-permute-start | bytes 1277960 | tf_op jit(solution)/shard_map/ppermute | solution.py:310
  53.5 13.4 %collective-permute-start.14 = (bf16[208,1024]{1,0:T(8,128)(2,1)S(1)}, bf16[208,1024]{1,0:T(8,128)(2,1)S(1)}, u32[]{:S(2)}, u32[]{:S(2)}) collective-permute-start(bf16[208,1024]{1,0:T(8,128)(2,1)S(1)} %get-tuple-element.65.refs_1_), channel_id=1, source_target_pairs={{6,0},{7,1},{0,2},{1,3},{3,4},{2,5},{5,6},{4,7},{14,8},{15,9},{8,1... | collective-permute-start | bytes 1277960 | tf_op jit(solution)/shard_map/ppermute | solution.py:310
  54.1 12.8 %collective-permute-start.13 = (bf16[208,1024]{1,0:T(8,128)(2,1)S(1)}, bf16[208,1024]{1,0:T(8,128)(2,1)S(1)}, u32[]{:S(2)}, u32[]{:S(2)}) collective-permute-start(bf16[208,1024]{1,0:T(8,128)(2,1)S(1)} %get-tuple-element.65.refs_1_), channel_id=1, source_target_pairs={{2,0},{3,1},{4,2},{5,3},{6,4},{7,5},{0,6},{1,7},{10,8},{11,9},{12,... | collective-permute-start | bytes 1277960 | tf_op jit(solution)/shard_map/ppermute | solution.py:310
  66.9 19.9 %copy-start = (f32[512,1024]{1,0:T(8,128)S(1)}, f32[512,1024]{1,0:T(8,128)}, u32[]{:S(2)}) copy-start(f32[512,1024]{1,0:T(8,128)} %x_hbm.1) | copy-start | bytes 6291460
  66.9 19.9 %copy-start.1 = (s32[512]{0:T(512)S(1)}, s32[512]{0:T(512)}, u32[]{:S(2)}) copy-start(s32[512]{0:T(512)} %param.5) | copy-start | bytes 6148
  68.3 3.4 %collective-permute-start.15 = (f32[1,896]{1,0:T(1,128)S(1)}, f32[1,896]{1,0:T(1,128)S(1)}, u32[]{:S(2)}, u32[]{:S(2)}) collective-permute-start(f32[1,896]{1,0:T(1,128)S(1)} %get-tuple-element.74), channel_id=1, source_target_pairs={{0,1},{1,0},{2,3},{3,2},{4,5},{5,4},{6,7},{7,6},{8,9},{9,8},{10,11... | collective-permute-start | bytes 10760 | tf_op jit(solution)/shard_map/ppermute | solution.py:310
  68.4 4.9 %collective-permute-start.16 = (f32[1,896]{1,0:T(1,128)S(1)}, f32[1,896]{1,0:T(1,128)S(1)}, u32[]{:S(2)}, u32[]{:S(2)}) collective-permute-start(f32[1,896]{1,0:T(1,128)S(1)} %get-tuple-element.75), channel_id=1, source_target_pairs={{0,2},{1,3},{2,4},{3,5},{4,6},{5,7},{6,0},{7,1},{8,10},{9,11},{10,... | collective-permute-start | bytes 10760 | tf_op jit(solution)/shard_map/ppermute | solution.py:310
  69.3 4.0 %collective-permute-start.17 = (f32[1,896]{1,0:T(1,128)S(1)}, f32[1,896]{1,0:T(1,128)S(1)}, u32[]{:S(2)}, u32[]{:S(2)}) collective-permute-start(f32[1,896]{1,0:T(1,128)S(1)} %get-tuple-element.76), channel_id=1, source_target_pairs={{0,6},{1,7},{2,0},{3,1},{4,3},{5,2},{6,5},{7,4},{8,14},{9,15},{10,... | collective-permute-start | bytes 10760 | tf_op jit(solution)/shard_map/ppermute | solution.py:310
  74.1 11.4 %all-to-all-start.5 = ((f32[16,1,128]{2,1,0:T(1,128)}), f32[16,1,128]{2,1,0:T(1,128)S(1)}, u32[]{:S(2)}, u32[]{:S(2)}) async-start(f32[16,1,128]{2,1,0:T(1,128)} %bitcast.16), calls=%async_computation.5 | async-start | bytes 16384 | tf_op jit(solution)/shard_map/all_to_all | solution.py:321

commit v5 on v4

--- a/solution.py
+++ b/solution.py
@@ -197,8 +197,8 @@
                 part = jnp.max(jnp.transpose(over_lanes[b, 0:n]), axis=0, keepdims=True)
             if b in rights:
                 part = jnp.maximum(part, jnp.max(over_rows[b, :, 0:n], axis=0, keepdims=True))
-            if earlier is not None:
-                part = jnp.maximum(part, before[earlier][:, at : at + n])
+            for e in earlier:
+                part = jnp.maximum(part, before[e][:, at : at + n])
             out[:, at : at + n] = part
         out[:, out.shape[1] - 128 :] = flag
 
@@ -231,9 +231,8 @@
     return jnp.concatenate(parts, axis=0).astype(BF16)
 
 
-def join_kernel(packed, own_ref, a_ref, b_ref, c_ref, *rest):
-    best = jnp.maximum(jnp.maximum(own_ref[...], a_ref[...]), jnp.maximum(b_ref[...], c_ref[...]))
-    best = jnp.maximum(best, -1.0)
+def join_kernel(packed, own_ref, a_ref, b_ref, *rest):
+    best = jnp.maximum(jnp.maximum(own_ref[...], a_ref[...]), jnp.maximum(b_ref[...], -1.0))
     out_ref = rest[-1]
     second = best[:, CHUNK:-128]
     if packed:
@@ -248,13 +247,13 @@
         out_ref[row, CAP:128] = best[:, -CAP:]
 
 
-def join(own, a, b, c, *onehot):
+def join(own, a, b, *onehot):
     return pl.pallas_call(
         functools.partial(join_kernel, bool(onehot)),
         out_shape=jax.ShapeDtypeStruct((OWNERS, 128), F32),
         compiler_params=params(),
         name="join",
-    )(own, a, b, c, *onehot)
+    )(own, a, b, *onehot)
 
 
 def pick_kernel(back_ref, meta_ref, out_ref, flag_ref):
@@ -286,14 +285,19 @@
     return [(2 * z + k, 2 * z + 1 - k) for z in range(4) for k in range(2)]
 
 
+LAST_CROSS = (0, 1, 1, 1)
+
+
 def from_next():
-    return [(2 * ((z + 1) % 4) + k, 2 * z + k) for z in range(4) for k in range(2)]
+    return [
+        (2 * ((z + 1) % 4) + (k ^ 1 ^ LAST_CROSS[(z + 1) % 4]), 2 * z + k)
+        for z in range(4)
+        for k in range(2)
+    ]
 
 
 def from_last():
-    return [
-        (2 * ((z + 3) % 4) + (k if z < 2 else 1 - k), 2 * z + k) for z in range(4) for k in range(2)
-    ]
+    return [(2 * ((z + 3) % 4) + (k ^ LAST_CROSS[z]), 2 * z + k) for z in range(4) for k in range(2)]
 
 
 def inverse(perm):
@@ -310,10 +314,9 @@
     return lax.ppermute(block, "pair", perm)
 
 
-def give_back(own, sib, nxt, last, meta, *onehot):
+def give_back(own, nxt, last, meta, *onehot):
     tiles = join(
         own,
-        along_pair(sib, swap_cores()),
         along_pair(nxt, inverse(from_next())),
         along_pair(last, inverse(from_last())),
         *onehot,
@@ -323,31 +326,32 @@
 
 
 EARLY = (
-    (0, 0, "self"), (0, 2, "left"), (0, 4, "both"), (2, 4, "both"), (5, 4, "both"),
+    (0, 0, "self"), (0, 2, "left"), (0, 4, "both"), (0, 5, "both"), (5, 4, "both"),
     (0, 1, "both"), (1, 1, "self"), (0, 3, "left"), (1, 2, "left"), (1, 3, "left"),
-    (1, 4, "both"), (3, 4, "both"), (1, 5, "both"), (3, 5, "both"),
+    (1, 4, "both"), (1, 5, "both"), (3, 4, "both"), (3, 5, "both"),
 )
-LATE = ((5, 6, "both"), (7, 4, "both"), (1, 6, "both"), (3, 6, "both"), (7, 6, "both"))
+LATE = ((5, 6, "both"), (7, 4, "both"), (1, 6, "both"), (1, 7, "both"), (7, 6, "both"))
 
 
 def match(a, second, tails):
     own_a, sib_a, next_a, last_a = a
     own_b, sib_b, next_b, last_b = second
     width = CHUNK + lanes(own_b.shape[0])
-    before = pairs(
+    own, sib, nxt, last = pairs(
         EARLY,
         (own_a, own_b, sib_a, sib_b, next_a, last_a),
         (),
-        ((0, 1, None), (2, 3, None), (4, None, None), (5, None, None)),
+        ((0, 1, ()), (2, 3, ()), (4, None, ()), (5, None, ())),
         (),
         width,
         "early",
     )
+    sib = along_pair(sib, swap_cores())
     return pairs(
         LATE,
         (own_a, own_b, sib_a, sib_b, next_a, last_a, next_b, last_b),
-        before,
-        ((0, 1, 0), (2, 3, 1), (4, 6, 2), (5, 7, 3)),
+        (own, sib, nxt, last),
+        ((0, 1, (0, 1)), (4, 6, (2,)), (5, 7, (3,))),
         tails,
         width,
         "late",

time: 87.3 us -> 86.3 us (0.989)
  no operation moved by 1% of the time
where the time goes in v5:
time: 86.3 us; the launch traced here: 86 us
  blocking collectives  44.4 us (51%)
  starting transfers between devices  14.8 us (17%)
  waiting for transfers between devices  13.3 us (15%)
  Pallas kernels  12.7 us (15%)
    all_to_all x2, blocking collectives, to_owners(): lax.all_to_all(block, 'wide', split_axis=0, concat_axis=0, tiled=True)  44.4 us
    ppermute x9, starting transfers between devices, along_pair(): return lax.ppermute(block, 'pair', perm)  10.9 us
    all_to_all x1, waiting for transfers between devices, give_back(): lax.all_to_all(tiles.reshape(OWNERS, 1, 128), 'wide', split_axis=0, conca...  7.56 us
    pallas_call x2, Pallas kernels, pairs(): pl.pallas_call(functools.partial(pair_kernel, units, n, len(before), want...  7.05 us
    ppermute x9, waiting for transfers between devices, along_pair(): return lax.ppermute(block, 'pair', perm)  5.71 us
    all_to_all x1, starting transfers between devices, give_back(): lax.all_to_all(tiles.reshape(OWNERS, 1, 128), 'wide', split_axis=0, conca...  3.84 us
    pallas_call x1, Pallas kernels, prep(): pl.pallas_call(prep_kernel, in_specs=[pl.BlockSpec(memory_space=pltpu.HBM...  2.46 us
  transfers between devices with their start and end apart: 10, of which 4 were waited for; matrix products, arithmetic and copies ran while one was open for 0% of the time, Pallas kernels for 8%

profile of v5, /device:TPU:0, one launch (start us, length us, event | category | flops | bytes accessed | tf_op | source)
XLA Modules:
  0.0 86.0 jit_solution(11643637216992567357)
XLA Ops:
  0.0 2.5 %prep.3 = (bf16[512,1024]{1,0:T(8,128)(2,1)S(1)}, bf16[512,1024]{1,0:T(8,128)(2,1)S(1)}, s32[8,512]{1,0:T(8,128)S(1)}) custom-call(f32[512,1024]{1,0:T(8,128)} %x_hbm.1, s32[1,512]{1,0:T(1,128)} %bitcast.43), custom_call_target="tpu_custom_call" | custom-call | flops 536870912 | bytes 4194304 | tf_op jit(solution)/shard_map/prep/pallas_call | solution.py:78
  2.5 23.8 %all_to_all.30 = bf16[16,32,1024]{2,1,0:T(8,128)(2,1)S(1)} all-to-all(bf16[16,32,1024]{2,1,0:T(8,128)(2,1)S(1)} %bitcast.38), channel_id=1, replica_groups=mesh['wide'=16,'pair'=8] {'wide'}, dimensions={0} | all-to-all | bytes 2097152 | tf_op jit(solution)/shard_map/all_to_all | solution.py:310
  26.2 0.1 collective-permute-start.11
  26.3 2.1 %collective-permute-start.10 = (bf16[512,1024]{1,0:T(8,128)(2,1)S(1)}, bf16[512,1024]{1,0:T(8,128)(2,1)S(1)}, u32[]{:S(2)}, u32[]{:S(2)}) collective-permute-start(bf16[512,1024]{1,0:T(8,128)(2,1)S(1)} %bitcast.24), channel_id=1, source_target_pairs={{2,0},{3,1},{4,2},{5,3},{6,4},{7,5},{1,6},{0,7},{10,8},{11,9},{12,... | collective-permute-start | bytes 3145736 | tf_op jit(solution)/shard_map/ppermute | solution.py:314
  28.4 1.9 %collective-permute-start.9 = (bf16[512,1024]{1,0:T(8,128)(2,1)S(1)}, bf16[512,1024]{1,0:T(8,128)(2,1)S(1)}, u32[]{:S(2)}, u32[]{:S(2)}) collective-permute-start(bf16[512,1024]{1,0:T(8,128)(2,1)S(1)} %bitcast.25), channel_id=1, source_target_pairs={{0,1},{1,0},{2,3},{3,2},{4,5},{5,4},{6,7},{7,6},{8,9},{9,8},{10,11... | collective-permute-start | bytes 3145736 | tf_op jit(solution)/shard_map/ppermute | solution.py:314
  30.4 0.9 rest.3
  31.2 20.7 %all_to_all.31 = bf16[16,32,1024]{2,1,0:T(8,128)(2,1)S(1)} all-to-all(bf16[16,32,1024]{2,1,0:T(8,128)(2,1)S(1)} %bitcast.21), channel_id=1, replica_groups=mesh['wide'=16,'pair'=8] {'wide'}, dimensions={0} | all-to-all | bytes 2097152 | tf_op jit(solution)/shard_map/all_to_all | solution.py:310
  51.9 0.7 pack.1
  52.6 0.0 collective-permute-done.11.refs_5_
  52.6 0.0 collective-permute-done.10.refs_4_
  52.6 0.0 collective-permute-done.9.refs_2_
  52.7 0.1 collective-permute-start.12
  52.7 1.0 %collective-permute-start.14 = (bf16[208,1024]{1,0:T(8,128)(2,1)S(1)}, bf16[208,1024]{1,0:T(8,128)(2,1)S(1)}, u32[]{:S(2)}, u32[]{:S(2)}) collective-permute-start(bf16[208,1024]{1,0:T(8,128)(2,1)S(1)} %get-tuple-element.63.refs_1_), channel_id=1, source_target_pairs={{6,0},{7,1},{1,2},{0,3},{3,4},{2,5},{5,6},{4,7},{14,8},{15,9},{9,1... | collective-permute-start | bytes 1277960 | tf_op jit(solution)/shard_map/ppermute | solution.py:314
  53.7 2.1 %collective-permute-start.13 = (bf16[208,1024]{1,0:T(8,128)(2,1)S(1)}, bf16[208,1024]{1,0:T(8,128)(2,1)S(1)}, u32[]{:S(2)}, u32[]{:S(2)}) collective-permute-start(bf16[208,1024]{1,0:T(8,128)(2,1)S(1)} %get-tuple-element.63.refs_1_), channel_id=1, source_target_pairs={{2,0},{3,1},{4,2},{5,3},{6,4},{7,5},{1,6},{0,7},{10,8},{11,9},{12,... | collective-permute-start | bytes 1277960 | tf_op jit(solution)/shard_map/ppermute | solution.py:314
  55.8 0.0 collective-permute-done.12.refs_3_
  55.8 5.7 %early.3 = (f32[1,896]{1,0:T(1,128)S(1)}, f32[1,896]{1,0:T(1,128)S(1)}, f32[1,896]{1,0:T(1,128)S(1)}, f32[1,896]{1,0:T(1,128)S(1)}) custom-call(bf16[512,1024]{1,0:T(8,128)(2,1)S(1)} %bitcast.26, bf16[208,1024]{1,0:T(8,128)(2,1)S(1)} %get-tuple-element.63.refs_1_, bf16[512,1024]{1,0:T(8,128)(2,1)S(1)} %collective-permute-done.9.refs_2_, ...), custom_call_target="tpu_custom_call" | custom-call | flops 4388290560 | bytes 6291456 | tf_op jit(solution)/shard_map/early/pallas_call | solution.py:210
  61.5 0.4 collective-permute-start.15
  61.9 4.3 %collective-permute-done.14.refs_7_ = bf16[208,1024]{1,0:T(8,128)(2,1)S(1)} collective-permute-done((bf16[208,1024]{1,0:T(8,128)(2,1)S(1)}, bf16[208,1024]{1,0:T(8,128)(2,1)S(1)}, u32[]{:S(2)}, u32[]{:S(2)}) %collective-permute-start.14) | collective-permute-done | bytes 426016 | tf_op jit(solution)/shard_map/ppermute | solution.py:314
  66.2 0.0 collective-permute-done.13.refs_6_
  66.2 0.0 collective-permute-done.15.refs_9_
  66.2 0.0 copy-start
  66.2 0.0 copy-start.1
  66.2 1.4 %late.3 = (f32[1,896]{1,0:T(1,128)S(1)}, f32[1,896]{1,0:T(1,128)S(1)}, f32[1,896]{1,0:T(1,128)S(1)}) custom-call(bf16[512,1024]{1,0:T(8,128)(2,1)S(1)} %bitcast.27, bf16[208,1024]{1,0:T(8,128)(2,1)S(1)} %get-tuple-element.63.refs_1_, bf16[512,1024]{1,0:T(8,128)(2,1)S(1)} %collective-permute-done.9.refs_2_, ...), custom_call_target="tpu_custom_call" | custom-call | flops 702021632 | bytes 8388608 | tf_op jit(solution)/shard_map/late/pallas_call | solution.py:210
  67.6 1.6 %collective-permute-start.16 = (f32[1,896]{1,0:T(1,128)S(1)}, f32[1,896]{1,0:T(1,128)S(1)}, u32[]{:S(2)}, u32[]{:S(2)}) collective-permute-start(f32[1,896]{1,0:T(1,128)S(1)} %get-tuple-element.72), channel_id=1, source_target_pairs={{0,2},{1,3},{2,4},{3,5},{4,6},{5,7},{6,1},{7,0},{8,10},{9,11},{10,... | collective-permute-start | bytes 10760 | tf_op jit(solution)/shard_map/ppermute | solution.py:314
  69.2 1.6 %collective-permute-start.17 = (f32[1,896]{1,0:T(1,128)S(1)}, f32[1,896]{1,0:T(1,128)S(1)}, u32[]{:S(2)}, u32[]{:S(2)}) collective-permute-start(f32[1,896]{1,0:T(1,128)S(1)} %get-tuple-element.73), channel_id=1, source_target_pairs={{0,6},{1,7},{2,1},{3,0},{4,3},{5,2},{6,5},{7,4},{8,14},{9,15},{10,... | collective-permute-start | bytes 10760 | tf_op jit(solution)/shard_map/ppermute | solution.py:314
  70.8 1.1 %collective-permute-done.16.a_ref = f32[1,896]{1,0:T(1,128)S(1)} collective-permute-done((f32[1,896]{1,0:T(1,128)S(1)}, f32[1,896]{1,0:T(1,128)S(1)}, u32[]{:S(2)}, u32[]{:S(2)}) %collective-permute-start.16) | collective-permute-done | bytes 3616 | tf_op jit(solution)/shard_map/ppermute | solution.py:314
  71.9 0.3 collective-permute-done.17.b_ref
  72.2 0.8 join.3
  73.0 3.8 %all-to-all-start.5 = ((f32[16,1,128]{2,1,0:T(1,128)}), f32[16,1,128]{2,1,0:T(1,128)S(1)}, u32[]{:S(2)}, u32[]{:S(2)}) async-start(f32[16,1,128]{2,1,0:T(1,128)} %bitcast.16), calls=%async_computation.5 | async-start | bytes 16384 | tf_op jit(solution)/shard_map/all_to_all | solution.py:324
  76.9 7.6 %all-to-all-done.5 = f32[16,1,128]{2,1,0:T(1,128)S(1)} async-done(((f32[16,1,128]{2,1,0:T(1,128)}), f32[16,1,128]{2,1,0:T(1,128)S(1)}, u32[]{:S(2)}, u32[]{:S(2)}) %all-to-all-start.5) | async-done | bytes 8224 | tf_op jit(solution)/shard_map/all_to_all | solution.py:324
  84.5 0.8 pick.3
  85.8 0.0 copy-done
  85.8 0.0 copy-done.1
  (1 shorter events, 0.0 us)
Async XLA Ops:
  26.2 26.4 %collective-permute-start.11 = (bf16[512,1024]{1,0:T(8,128)(2,1)S(1)}, bf16[512,1024]{1,0:T(8,128)(2,1)S(1)}, u32[]{:S(2)}, u32[]{:S(2)}) collective-permute-start(bf16[512,1024]{1,0:T(8,128)(2,1)S(1)} %bitcast.23), channel_id=1, source_target_pairs={{6,0},{7,1},{1,2},{0,3},{3,4},{2,5},{5,6},{4,7},{14,8},{15,9},{9,1... | collective-permute-start | bytes 3145736 | tf_op jit(solution)/shard_map/ppermute | solution.py:314
  26.3 26.3 %collective-permute-start.10 = (bf16[512,1024]{1,0:T(8,128)(2,1)S(1)}, bf16[512,1024]{1,0:T(8,128)(2,1)S(1)}, u32[]{:S(2)}, u32[]{:S(2)}) collective-permute-start(bf16[512,1024]{1,0:T(8,128)(2,1)S(1)} %bitcast.24), channel_id=1, source_target_pairs={{2,0},{3,1},{4,2},{5,3},{6,4},{7,5},{1,6},{0,7},{10,8},{11,9},{12,... | collective-permute-start | bytes 3145736 | tf_op jit(solution)/shard_map/ppermute | solution.py:314
  28.4 24.2 %collective-permute-start.9 = (bf16[512,1024]{1,0:T(8,128)(2,1)S(1)}, bf16[512,1024]{1,0:T(8,128)(2,1)S(1)}, u32[]{:S(2)}, u32[]{:S(2)}) collective-permute-start(bf16[512,1024]{1,0:T(8,128)(2,1)S(1)} %bitcast.25), channel_id=1, source_target_pairs={{0,1},{1,0},{2,3},{3,2},{4,5},{5,4},{6,7},{7,6},{8,9},{9,8},{10,11... | collective-permute-start | bytes 3145736 | tf_op jit(solution)/shard_map/ppermute | solution.py:314
  52.7 3.2 %collective-permute-start.12 = (bf16[208,1024]{1,0:T(8,128)(2,1)S(1)}, bf16[208,1024]{1,0:T(8,128)(2,1)S(1)}, u32[]{:S(2)}, u32[]{:S(2)}) collective-permute-start(bf16[208,1024]{1,0:T(8,128)(2,1)S(1)} %get-tuple-element.63.refs_1_), channel_id=1, source_target_pairs={{0,1},{1,0},{2,3},{3,2},{4,5},{5,4},{6,7},{7,6},{8,9},{9,8},{10,11... | collective-permute-start | bytes 1277960 | tf_op jit(solution)/shard_map/ppermute | solution.py:314
  52.7 13.4 %collective-permute-start.14 = (bf16[208,1024]{1,0:T(8,128)(2,1)S(1)}, bf16[208,1024]{1,0:T(8,128)(2,1)S(1)}, u32[]{:S(2)}, u32[]{:S(2)}) collective-permute-start(bf16[208,1024]{1,0:T(8,128)(2,1)S(1)} %get-tuple-element.63.refs_1_), channel_id=1, source_target_pairs={{6,0},{7,1},{1,2},{0,3},{3,4},{2,5},{5,6},{4,7},{14,8},{15,9},{9,1... | collective-permute-start | bytes 1277960 | tf_op jit(solution)/shard_map/ppermute | solution.py:314
  53.7 12.5 %collective-permute-start.13 = (bf16[208,1024]{1,0:T(8,128)(2,1)S(1)}, bf16[208,1024]{1,0:T(8,128)(2,1)S(1)}, u32[]{:S(2)}, u32[]{:S(2)}) collective-permute-start(bf16[208,1024]{1,0:T(8,128)(2,1)S(1)} %get-tuple-element.63.refs_1_), channel_id=1, source_target_pairs={{2,0},{3,1},{4,2},{5,3},{6,4},{7,5},{1,6},{0,7},{10,8},{11,9},{12,... | collective-permute-start | bytes 1277960 | tf_op jit(solution)/shard_map/ppermute | solution.py:314
  61.5 4.7 %collective-permute-start.15 = (f32[1,896]{1,0:T(1,128)S(1)}, f32[1,896]{1,0:T(1,128)S(1)}, u32[]{:S(2)}, u32[]{:S(2)}) collective-permute-start(f32[1,896]{1,0:T(1,128)S(1)} %get-tuple-element.68), channel_id=1, source_target_pairs={{0,1},{1,0},{2,3},{3,2},{4,5},{5,4},{6,7},{7,6},{8,9},{9,8},{10,11... | collective-permute-start | bytes 10760 | tf_op jit(solution)/shard_map/ppermute | solution.py:314
  66.2 19.6 %copy-start = (f32[512,1024]{1,0:T(8,128)S(1)}, f32[512,1024]{1,0:T(8,128)}, u32[]{:S(2)}) copy-start(f32[512,1024]{1,0:T(8,128)} %x_hbm.1) | copy-start | bytes 6291460
  66.2 19.6 %copy-start.1 = (s32[512]{0:T(512)S(1)}, s32[512]{0:T(512)}, u32[]{:S(2)}) copy-start(s32[512]{0:T(512)} %param.5) | copy-start | bytes 6148
  67.6 4.3 %collective-permute-start.16 = (f32[1,896]{1,0:T(1,128)S(1)}, f32[1,896]{1,0:T(1,128)S(1)}, u32[]{:S(2)}, u32[]{:S(2)}) collective-permute-start(f32[1,896]{1,0:T(1,128)S(1)} %get-tuple-element.72), channel_id=1, source_target_pairs={{0,2},{1,3},{2,4},{3,5},{4,6},{5,7},{6,1},{7,0},{8,10},{9,11},{10,... | collective-permute-start | bytes 10760 | tf_op jit(solution)/shard_map/ppermute | solution.py:314
  69.2 3.0 %collective-permute-start.17 = (f32[1,896]{1,0:T(1,128)S(1)}, f32[1,896]{1,0:T(1,128)S(1)}, u32[]{:S(2)}, u32[]{:S(2)}) collective-permute-start(f32[1,896]{1,0:T(1,128)S(1)} %get-tuple-element.73), channel_id=1, source_target_pairs={{0,6},{1,7},{2,1},{3,0},{4,3},{5,2},{6,5},{7,4},{8,14},{9,15},{10,... | collective-permute-start | bytes 10760 | tf_op jit(solution)/shard_map/ppermute | solution.py:314
  73.0 11.4 %all-to-all-start.5 = ((f32[16,1,128]{2,1,0:T(1,128)}), f32[16,1,128]{2,1,0:T(1,128)S(1)}, u32[]{:S(2)}, u32[]{:S(2)}) async-start(f32[16,1,128]{2,1,0:T(1,128)} %bitcast.16), calls=%async_computation.5 | async-start | bytes 16384 | tf_op jit(solution)/shard_map/all_to_all | solution.py:324

commit v6 on v5

--- a/solution.py
+++ b/solution.py
@@ -94,7 +94,8 @@
     )(embeddings, ids)
 
 
-def rest_kernel(unit_ref, meta_ref, second_ref):
+def rest_kernel(unit_ref, meta_ref, second_ref, ranks_ref):
+    ranks_ref[...] = (iota(ranks_ref.shape, 0) == meta_ref[1:2, :]).astype(BF16)
     place(1, unit_ref[...], meta_ref[0:1, :], meta_ref[1:2, :], second_ref)
 
 
@@ -102,22 +103,31 @@
     rows, width = unit.shape
     return pl.pallas_call(
         rest_kernel,
-        out_shape=jax.ShapeDtypeStruct((CHUNK, width), BF16),
+        out_shape=(
+            jax.ShapeDtypeStruct((CHUNK, width), BF16),
+            jax.ShapeDtypeStruct((128, rows), BF16),
+        ),
         compiler_params=params(),
         cost_estimate=cost(2 * CHUNK * rows * width, 4 * rows * width),
         name="rest",
     )(unit, meta)
 
 
-def pack_kernel(block_ref, packed_ref, onehot_ref):
+def pack_kernel(block_ref, packed_ref, source_ref, spread_ref):
     rows = block_ref.shape[0]
     full = jnp.where(marked(block_ref[:, 0:128]), 0.0, 1.0)
     full = jnp.transpose(jnp.broadcast_to(full, (rows, 128)))[0:8, :]
     upto = (iota((rows, rows), 0) <= iota((rows, rows), 1)).astype(BF16)
     count = jnp.dot(full.astype(BF16), upto, preferred_element_type=F32)
     spot = jnp.where(full > 0.5, count - 1.0, -1.0).astype(jnp.int32)
-    onehot = (iota((SHORT, rows), 0) == spot[0:1, :]).astype(BF16)
-    onehot_ref[...] = onehot
+    wide = (iota((lanes(SHORT), rows), 0) == spot[0:1, :]).astype(BF16)
+    source = (iota((OWNERS, rows), 1) // HALF == iota((OWNERS, rows), 0)).astype(BF16)
+    source_ref[...] = lax.dot_general(
+        source, wide, (((1,), (1,)), ((), ())), preferred_element_type=F32
+    )
+    lane = (iota((rows, 128), 0) % HALF + HALF == iota((rows, 128), 1)).astype(BF16)
+    spread_ref[...] = jnp.dot(wide, lane, preferred_element_type=F32).astype(BF16)
+    onehot = wide[0:SHORT, :]
     moved = jnp.dot(onehot, block_ref[...], preferred_element_type=F32)
     taken = jnp.dot(onehot, jnp.ones((rows, 128), BF16), preferred_element_type=F32)
     packed_ref[...] = moved.astype(BF16)
@@ -131,7 +141,8 @@
         pack_kernel,
         out_shape=(
             jax.ShapeDtypeStruct((SHORT, width), BF16),
-            jax.ShapeDtypeStruct((SHORT, rows), BF16),
+            jax.ShapeDtypeStruct((OWNERS, lanes(SHORT)), F32),
+            jax.ShapeDtypeStruct((lanes(SHORT), 128), BF16),
         ),
         compiler_params=params(),
         cost_estimate=cost(2 * SHORT * rows * width, 4 * rows * width),
@@ -236,49 +247,52 @@
     out_ref = rest[-1]
     second = best[:, CHUNK:-128]
     if packed:
-        parts = three_parts(jnp.broadcast_to(second[:, 0:SHORT], (8, SHORT)))
-        moved = jnp.dot(parts, rest[0][...], preferred_element_type=F32)
-        second = moved[0:1, :] + moved[8:9, :] + moved[16:17, :]
+        source_ref, spread_ref = rest[:2]
+        value = jnp.where(source_ref[...] > 0.5, second, 0.0)
+        moved = jnp.dot(three_parts(value), spread_ref[...], preferred_element_type=F32)
+        out_ref[...] = moved[0:OWNERS] + moved[OWNERS : 2 * OWNERS] + moved[2 * OWNERS :]
     for source in range(OWNERS):
         at = source * HALF
         row = slice(source, source + 1)
         out_ref[row, 0:HALF] = best[:, at : at + HALF]
-        out_ref[row, HALF:CAP] = second[:, at : at + HALF]
+        if not packed:
+            out_ref[row, HALF:CAP] = second[:, at : at + HALF]
         out_ref[row, CAP:128] = best[:, -CAP:]
 
 
-def join(own, a, b, *onehot):
-    return pl.pallas_call(
-        functools.partial(join_kernel, bool(onehot)),
-        out_shape=jax.ShapeDtypeStruct((OWNERS, 128), F32),
+def join(own, a, b, *moves):
+    return pl.pallas_call(
+        functools.partial(join_kernel, bool(moves)),
+        out_shape=pltpu.VMEM((OWNERS, 128), F32),
         compiler_params=params(),
         name="join",
-    )(own, a, b, *onehot)
-
-
-def pick_kernel(back_ref, meta_ref, out_ref, flag_ref):
+    )(own, a, b, *moves)
+
+
+def pick_kernel(back_ref, meta_ref, ranks_ref, out_ref, flag_ref):
     rows = meta_ref.shape[1]
-    ids = meta_ref[0:1, :]
-    rank = meta_ref[1:2, :]
-    flag_ref[...] = jnp.max(jnp.max(back_ref[:, CAP:], axis=0, keepdims=True), axis=1, keepdims=True)
-    onehot = ((iota((3 * OWNERS, rows), 0) & (OWNERS - 1)) == ids).astype(BF16)
     tiles = back_ref[...]
-    moved = lax.dot_general(
-        three_parts(tiles), onehot, (((0,), (0,)), ((), ())), preferred_element_type=F32
-    )[0:CAP, :]
-    out_ref[...] = jnp.sum(jnp.where(iota((CAP, rows), 0) == rank, moved, 0.0), axis=0, keepdims=True)
-
-
-def pick(back, meta):
+    moved = jnp.dot(three_parts(tiles), ranks_ref[...], preferred_element_type=F32)
+    moved = moved[0:OWNERS] + moved[OWNERS : 2 * OWNERS] + moved[2 * OWNERS :]
+    mine = iota((OWNERS, rows), 0) == meta_ref[0:1, :]
+    out_ref[...] = jnp.sum(jnp.where(mine, moved, 0.0), axis=0, keepdims=True)
+    flag_ref[0, 0] = (jnp.max(tiles[:, CAP:]) > 0.5).astype(jnp.int32)
+
+
+def pick(back, meta, ranks):
     return pl.pallas_call(
         pick_kernel,
         out_shape=(
             jax.ShapeDtypeStruct((1, meta.shape[1]), F32),
-            jax.ShapeDtypeStruct((1, 1), F32),
+            pltpu.SMEM((1, 1), jnp.int32),
         ),
+        out_specs=(
+            pl.BlockSpec(memory_space=pltpu.VMEM),
+            pl.BlockSpec(memory_space=pltpu.SMEM),
+        ),
         compiler_params=params(),
         name="pick",
-    )(back, meta)
+    )(back, meta, ranks)
 
 
 def swap_cores():
@@ -314,15 +328,15 @@
     return lax.ppermute(block, "pair", perm)
 
 
-def give_back(own, nxt, last, meta, *onehot):
+def give_back(own, nxt, last, own_rows, *moves):
     tiles = join(
         own,
         along_pair(nxt, inverse(from_next())),
         along_pair(last, inverse(from_last())),
-        *onehot,
+        *moves,
     )
     back = lax.all_to_all(tiles.reshape(OWNERS, 1, 128), "wide", split_axis=0, concat_axis=0, tiled=True)
-    return pick(back.reshape(OWNERS, 128), meta)
+    return pick(back.reshape(OWNERS, 128), *own_rows)
 
 
 EARLY = (
@@ -372,25 +386,26 @@
     own_a = to_owners(first)
     own_a, unit = lax.optimization_barrier((own_a, unit))
     a = neighbours(own_a)
-    return a, to_owners(rest(unit, meta)), meta
-
-
-def whole(embeddings, ids):
-    a, own_b, meta = exchange(embeddings, ids)
-    own_b, *a = lax.optimization_barrier((own_b, *a))
+    second, ranks = rest(unit, meta)
+    return a, to_owners(second), (meta, ranks)
+
+
+def whole(embeddings, ids, a, own_b):
+    _, unit, meta = prep(embeddings, ids)
+    _, ranks = rest(unit, meta)
     best = match(a, neighbours(own_b), ())
-    return give_back(*best, meta)[0]
+    return give_back(*best, (meta, ranks))[0]
 
 
 def per_device(embeddings, cluster_ids):
     ids = cluster_ids.reshape(1, -1)
-    a, own_b, meta = exchange(embeddings, ids)
-    packed, onehot = pack(own_b)
+    a, own_b, own_rows = exchange(embeddings, ids)
+    packed, *moves = pack(own_b)
     packed, *a = lax.optimization_barrier((packed, *a))
     best = match(a, neighbours(packed), (1, 3, 6, 7))
-    value, flag = give_back(*best, meta, onehot)
+    value, flag = give_back(*best, own_rows, *moves)
     return lax.cond(
-        flag.reshape(()) > 0.5, lambda: whole(embeddings, ids), lambda: value
+        flag.reshape(()) != 0, lambda: whole(embeddings, ids, a, own_b), lambda: value
     ).reshape(-1)
 
 

time: 86.3 us -> 85.5 us (level)
  transfers between devices with their start and end apart: 10 -> 10, of which waited for: 4 -> 4; matrix products, arithmetic and copies ran while one was open for 0% -> 0% of each run, Pallas kernels for 8% -> 9%
where the time goes in v6:
time: 85.5 us; the launch traced here: 85.2 us
  blocking collectives  44.4 us (52%)
  starting transfers between devices  14.8 us (17%)
  waiting for transfers between devices  13.3 us (16%)
  Pallas kernels  12.6 us (15%)
    all_to_all x2, blocking collectives, to_owners(): lax.all_to_all(block, 'wide', split_axis=0, concat_axis=0, tiled=True)  44.4 us
    ppermute x9, starting transfers between devices, along_pair(): return lax.ppermute(block, 'pair', perm)  10.9 us
    all_to_all x1, waiting for transfers between devices, give_back(): lax.all_to_all(tiles.reshape(OWNERS, 1, 128), 'wide', split_axis=0, conca...  7.56 us
    pallas_call x2, Pallas kernels, pairs(): pl.pallas_call(functools.partial(pair_kernel, units, n, len(before), want...  6.96 us
    ppermute x9, waiting for transfers between devices, along_pair(): return lax.ppermute(block, 'pair', perm)  5.72 us
    all_to_all x1, starting transfers between devices, give_back(): lax.all_to_all(tiles.reshape(OWNERS, 1, 128), 'wide', split_axis=0, conca...  3.84 us
    pallas_call x1, Pallas kernels, prep(): pl.pallas_call(prep_kernel, in_specs=[pl.BlockSpec(memory_space=pltpu.HBM...  2.46 us
  transfers between devices with their start and end apart: 10, of which 4 were waited for; matrix products, arithmetic and copies ran while one was open for 0% of the time, Pallas kernels for 9%

profile of v6, /device:TPU:0, one launch (start us, length us, event | category | flops | bytes accessed | tf_op | source)
XLA Modules:
  0.0 85.2 jit_solution(16186730559147676065)
XLA Ops:
  0.0 2.5 %prep.3 = (bf16[512,1024]{1,0:T(8,128)(2,1)S(1)}, bf16[512,1024]{1,0:T(8,128)(2,1)S(1)}, s32[8,512]{1,0:T(8,128)S(1)}) custom-call(f32[512,1024]{1,0:T(8,128)} %x_hbm.1, s32[1,512]{1,0:T(1,128)} %bitcast.28), custom_call_target="tpu_custom_call" | custom-call | flops 536870912 | bytes 4194304 | tf_op jit(solution)/shard_map/prep/pallas_call | solution.py:78
  2.5 23.8 %all_to_all.19 = bf16[16,32,1024]{2,1,0:T(8,128)(2,1)S(1)} all-to-all(bf16[16,32,1024]{2,1,0:T(8,128)(2,1)S(1)} %bitcast.16), channel_id=1, replica_groups=mesh['wide'=16,'pair'=8] {'wide'}, dimensions={0} | all-to-all | bytes 2097152 | tf_op jit(solution)/shard_map/all_to_all | solution.py:324
  26.2 0.0 copy-start.1
  26.2 0.1 collective-permute-start.8
  26.3 2.1 %collective-permute-start.7 = (bf16[512,1024]{1,0:T(8,128)(2,1)S(1)}, bf16[512,1024]{1,0:T(8,128)(2,1)S(1)}, u32[]{:S(2)}, u32[]{:S(2)}) collective-permute-start(bf16[512,1024]{1,0:T(8,128)(2,1)S(1)} %bitcast.23), channel_id=1, source_target_pairs={{2,0},{3,1},{4,2},{5,3},{6,4},{7,5},{1,6},{0,7},{10,8},{11,9},{12,... | collective-permute-start | bytes 3145736 | tf_op jit(solution)/shard_map/ppermute | solution.py:328
  28.4 1.9 %collective-permute-start.6 = (bf16[512,1024]{1,0:T(8,128)(2,1)S(1)}, bf16[512,1024]{1,0:T(8,128)(2,1)S(1)}, u32[]{:S(2)}, u32[]{:S(2)}) collective-permute-start(bf16[512,1024]{1,0:T(8,128)(2,1)S(1)} %bitcast.24), channel_id=1, source_target_pairs={{0,1},{1,0},{2,3},{3,2},{4,5},{5,4},{6,7},{7,6},{8,9},{9,8},{10,11... | collective-permute-start | bytes 3145736 | tf_op jit(solution)/shard_map/ppermute | solution.py:328
  30.4 0.9 %rest.3 = (bf16[512,1024]{1,0:T(8,128)(2,1)S(1)}, bf16[128,512]{1,0:T(8,128)(2,1)S(1)}) custom-call(bf16[512,1024]{1,0:T(8,128)(2,1)S(1)} %get-tuple-element.69.unit_ref, s32[8,512]{1,0:T(8,128)S(1)} %get-tuple-element.70.meta_ref), custom_call_target="tpu_custom_call" | custom-call | flops 536870912 | bytes 2097152 | tf_op jit(solution)/shard_map/rest/pallas_call | solution.py:104
  31.3 20.7 %all_to_all.20 = bf16[16,32,1024]{2,1,0:T(8,128)(2,1)S(1)} all-to-all(bf16[16,32,1024]{2,1,0:T(8,128)(2,1)S(1)} %bitcast.17), channel_id=1, replica_groups=mesh['wide'=16,'pair'=8] {'wide'}, dimensions={0} | all-to-all | bytes 2097152 | tf_op jit(solution)/shard_map/all_to_all | solution.py:324
  51.9 0.8 pack.1
  52.8 0.0 collective-permute-done.8.refs_5_
  52.8 0.0 copy-start.3
  52.8 0.0 collective-permute-done.7.refs_4_
  52.8 0.0 copy-start.5
  52.8 0.0 collective-permute-done.6.refs_2_
  52.8 0.0 copy-start.7
  52.8 0.1 collective-permute-start.9
  52.9 1.0 %collective-permute-start.11 = (bf16[208,1024]{1,0:T(8,128)(2,1)S(1)}, bf16[208,1024]{1,0:T(8,128)(2,1)S(1)}, u32[]{:S(2)}, u32[]{:S(2)}) collective-permute-start(bf16[208,1024]{1,0:T(8,128)(2,1)S(1)} %get-tuple-element.75.refs_1_), channel_id=1, source_target_pairs={{6,0},{7,1},{1,2},{0,3},{3,4},{2,5},{5,6},{4,7},{14,8},{15,9},{9,1... | collective-permute-start | bytes 1277960 | tf_op jit(solution)/shard_map/ppermute | solution.py:328
  53.9 2.1 %collective-permute-start.10 = (bf16[208,1024]{1,0:T(8,128)(2,1)S(1)}, bf16[208,1024]{1,0:T(8,128)(2,1)S(1)}, u32[]{:S(2)}, u32[]{:S(2)}) collective-permute-start(bf16[208,1024]{1,0:T(8,128)(2,1)S(1)} %get-tuple-element.75.refs_1_), channel_id=1, source_target_pairs={{2,0},{3,1},{4,2},{5,3},{6,4},{7,5},{1,6},{0,7},{10,8},{11,9},{12,... | collective-permute-start | bytes 1277960 | tf_op jit(solution)/shard_map/ppermute | solution.py:328
  56.0 0.0 collective-permute-done.9.refs_3_
  56.0 5.6 %early.3 = (f32[1,896]{1,0:T(1,128)S(1)}, f32[1,896]{1,0:T(1,128)S(1)}, f32[1,896]{1,0:T(1,128)S(1)}, f32[1,896]{1,0:T(1,128)S(1)}) custom-call(bf16[512,1024]{1,0:T(8,128)(2,1)S(1)} %bitcast.25, bf16[208,1024]{1,0:T(8,128)(2,1)S(1)} %get-tuple-element.75.refs_1_, bf16[512,1024]{1,0:T(8,128)(2,1)S(1)} %collective-permute-done.6.refs_2_, ...), custom_call_target="tpu_custom_call" | custom-call | flops 4388290560 | bytes 6291456 | tf_op jit(solution)/shard_map/early/pallas_call | solution.py:221
  61.6 0.4 collective-permute-start.12
  62.0 4.3 %collective-permute-done.11.refs_7_ = bf16[208,1024]{1,0:T(8,128)(2,1)S(1)} collective-permute-done((bf16[208,1024]{1,0:T(8,128)(2,1)S(1)}, bf16[208,1024]{1,0:T(8,128)(2,1)S(1)}, u32[]{:S(2)}, u32[]{:S(2)}) %collective-permute-start.11) | collective-permute-done | bytes 426016 | tf_op jit(solution)/shard_map/ppermute | solution.py:328
  66.4 0.0 collective-permute-done.10.refs_6_
  66.4 0.0 collective-permute-done.12.refs_9_
  66.4 0.0 copy-done.1
  66.4 0.0 copy-done.3
  66.4 0.0 copy-done.5
  66.4 0.0 copy-done.7
  66.4 0.0 copy-start
  66.4 0.0 copy-start.9
  66.4 1.4 %late.3 = (f32[1,896]{1,0:T(1,128)S(1)}, f32[1,896]{1,0:T(1,128)S(1)}, f32[1,896]{1,0:T(1,128)S(1)}) custom-call(bf16[512,1024]{1,0:T(8,128)(2,1)S(1)} %bitcast.26, bf16[208,1024]{1,0:T(8,128)(2,1)S(1)} %get-tuple-element.75.refs_1_, bf16[512,1024]{1,0:T(8,128)(2,1)S(1)} %collective-permute-done.6.refs_2_, ...), custom_call_target="tpu_custom_call" | custom-call | flops 702021632 | bytes 8388608 | tf_op jit(solution)/shard_map/late/pallas_call | solution.py:221
  67.8 1.6 %collective-permute-start.13 = (f32[1,896]{1,0:T(1,128)S(1)}, f32[1,896]{1,0:T(1,128)S(1)}, u32[]{:S(2)}, u32[]{:S(2)}) collective-permute-start(f32[1,896]{1,0:T(1,128)S(1)} %get-tuple-element.84), channel_id=1, source_target_pairs={{0,2},{1,3},{2,4},{3,5},{4,6},{5,7},{6,1},{7,0},{8,10},{9,11},{10,... | collective-permute-start | bytes 10760 | tf_op jit(solution)/shard_map/ppermute | solution.py:328
  69.3 1.6 %collective-permute-start.14 = (f32[1,896]{1,0:T(1,128)S(1)}, f32[1,896]{1,0:T(1,128)S(1)}, u32[]{:S(2)}, u32[]{:S(2)}) collective-permute-start(f32[1,896]{1,0:T(1,128)S(1)} %get-tuple-element.85), channel_id=1, source_target_pairs={{0,6},{1,7},{2,1},{3,0},{4,3},{5,2},{6,5},{7,4},{8,14},{9,15},{10,... | collective-permute-start | bytes 10760 | tf_op jit(solution)/shard_map/ppermute | solution.py:328
  71.0 1.1 %collective-permute-done.13.a_ref = f32[1,896]{1,0:T(1,128)S(1)} collective-permute-done((f32[1,896]{1,0:T(1,128)S(1)}, f32[1,896]{1,0:T(1,128)S(1)}, u32[]{:S(2)}, u32[]{:S(2)}) %collective-permute-start.13) | collective-permute-done | bytes 3616 | tf_op jit(solution)/shard_map/ppermute | solution.py:328
  72.1 0.3 collective-permute-done.14.b_ref
  72.4 0.7 join.3
  73.1 3.8 %all-to-all-start.3 = ((f32[16,1,128]{2,1,0:T(1,128)}), f32[16,1,128]{2,1,0:T(1,128)S(1)}, u32[]{:S(2)}, u32[]{:S(2)}) async-start(f32[16,1,128]{2,1,0:T(1,128)} %bitcast.12), calls=%async_computation.3 | async-start | bytes 16384 | tf_op jit(solution)/shard_map/all_to_all | solution.py:338
  76.9 7.6 %all-to-all-done.3 = f32[16,1,128]{2,1,0:T(1,128)S(1)} async-done(((f32[16,1,128]{2,1,0:T(1,128)}), f32[16,1,128]{2,1,0:T(1,128)S(1)}, u32[]{:S(2)}, u32[]{:S(2)}) %all-to-all-start.3) | async-done | bytes 8224 | tf_op jit(solution)/shard_map/all_to_all | solution.py:338
  84.5 0.7 pick.3
  85.2 0.0 copy-done
  85.2 0.0 copy-done.9
  (1 shorter events, 0.0 us)
Async XLA Ops:
  26.2 40.1 %copy-start.1 = (bf16[16,32,1024]{2,1,0:T(8,128)(2,1)}, bf16[16,32,1024]{2,1,0:T(8,128)(2,1)S(1)}, u32[]{:S(2)}) copy-start(bf16[16,32,1024]{2,1,0:T(8,128)(2,1)S(1)} %all_to_all.19) | copy-start | bytes 3145732
  26.2 26.5 %collective-permute-start.8 = (bf16[512,1024]{1,0:T(8,128)(2,1)S(1)}, bf16[512,1024]{1,0:T(8,128)(2,1)S(1)}, u32[]{:S(2)}, u32[]{:S(2)}) collective-permute-start(bf16[512,1024]{1,0:T(8,128)(2,1)S(1)} %bitcast.22), channel_id=1, source_target_pairs={{6,0},{7,1},{1,2},{0,3},{3,4},{2,5},{5,6},{4,7},{14,8},{15,9},{9,1... | collective-permute-start | bytes 3145736 | tf_op jit(solution)/shard_map/ppermute | solution.py:328
  26.3 26.5 %collective-permute-start.7 = (bf16[512,1024]{1,0:T(8,128)(2,1)S(1)}, bf16[512,1024]{1,0:T(8,128)(2,1)S(1)}, u32[]{:S(2)}, u32[]{:S(2)}) collective-permute-start(bf16[512,1024]{1,0:T(8,128)(2,1)S(1)} %bitcast.23), channel_id=1, source_target_pairs={{2,0},{3,1},{4,2},{5,3},{6,4},{7,5},{1,6},{0,7},{10,8},{11,9},{12,... | collective-permute-start | bytes 3145736 | tf_op jit(solution)/shard_map/ppermute | solution.py:328
  28.4 24.4 %collective-permute-start.6 = (bf16[512,1024]{1,0:T(8,128)(2,1)S(1)}, bf16[512,1024]{1,0:T(8,128)(2,1)S(1)}, u32[]{:S(2)}, u32[]{:S(2)}) collective-permute-start(bf16[512,1024]{1,0:T(8,128)(2,1)S(1)} %bitcast.24), channel_id=1, source_target_pairs={{0,1},{1,0},{2,3},{3,2},{4,5},{5,4},{6,7},{7,6},{8,9},{9,8},{10,11... | collective-permute-start | bytes 3145736 | tf_op jit(solution)/shard_map/ppermute | solution.py:328
  52.8 13.6 %copy-start.3 = (bf16[512,1024]{1,0:T(8,128)(2,1)}, bf16[512,1024]{1,0:T(8,128)(2,1)S(1)}, u32[]{:S(2)}) copy-start(bf16[512,1024]{1,0:T(8,128)(2,1)S(1)} %collective-permute-done.8.refs_5_) | copy-start | bytes 3145732
  52.8 13.6 %copy-start.5 = (bf16[512,1024]{1,0:T(8,128)(2,1)}, bf16[512,1024]{1,0:T(8,128)(2,1)S(1)}, u32[]{:S(2)}) copy-start(bf16[512,1024]{1,0:T(8,128)(2,1)S(1)} %collective-permute-done.7.refs_4_) | copy-start | bytes 3145732
  52.8 13.6 %copy-start.7 = (bf16[512,1024]{1,0:T(8,128)(2,1)}, bf16[512,1024]{1,0:T(8,128)(2,1)S(1)}, u32[]{:S(2)}) copy-start(bf16[512,1024]{1,0:T(8,128)(2,1)S(1)} %collective-permute-done.6.refs_2_) | copy-start | bytes 3145732
  52.8 3.2 %collective-permute-start.9 = (bf16[208,1024]{1,0:T(8,128)(2,1)S(1)}, bf16[208,1024]{1,0:T(8,128)(2,1)S(1)}, u32[]{:S(2)}, u32[]{:S(2)}) collective-permute-start(bf16[208,1024]{1,0:T(8,128)(2,1)S(1)} %get-tuple-element.75.refs_1_), channel_id=1, source_target_pairs={{0,1},{1,0},{2,3},{3,2},{4,5},{5,4},{6,7},{7,6},{8,9},{9,8},{10,11... | collective-permute-start | bytes 1277960 | tf_op jit(solution)/shard_map/ppermute | solution.py:328
  52.9 13.4 %collective-permute-start.11 = (bf16[208,1024]{1,0:T(8,128)(2,1)S(1)}, bf16[208,1024]{1,0:T(8,128)(2,1)S(1)}, u32[]{:S(2)}, u32[]{:S(2)}) collective-permute-start(bf16[208,1024]{1,0:T(8,128)(2,1)S(1)} %get-tuple-element.75.refs_1_), channel_id=1, source_target_pairs={{6,0},{7,1},{1,2},{0,3},{3,4},{2,5},{5,6},{4,7},{14,8},{15,9},{9,1... | collective-permute-start | bytes 1277960 | tf_op jit(solution)/shard_map/ppermute | solution.py:328
  53.9 12.5 %collective-permute-start.10 = (bf16[208,1024]{1,0:T(8,128)(2,1)S(1)}, bf16[208,1024]{1,0:T(8,128)(2,1)S(1)}, u32[]{:S(2)}, u32[]{:S(2)}) collective-permute-start(bf16[208,1024]{1,0:T(8,128)(2,1)S(1)} %get-tuple-element.75.refs_1_), channel_id=1, source_target_pairs={{2,0},{3,1},{4,2},{5,3},{6,4},{7,5},{1,6},{0,7},{10,8},{11,9},{12,... | collective-permute-start | bytes 1277960 | tf_op jit(solution)/shard_map/ppermute | solution.py:328
  61.6 4.8 %collective-permute-start.12 = (f32[1,896]{1,0:T(1,128)S(1)}, f32[1,896]{1,0:T(1,128)S(1)}, u32[]{:S(2)}, u32[]{:S(2)}) collective-permute-start(f32[1,896]{1,0:T(1,128)S(1)} %get-tuple-element.80), channel_id=1, source_target_pairs={{0,1},{1,0},{2,3},{3,2},{4,5},{5,4},{6,7},{7,6},{8,9},{9,8},{10,11... | collective-permute-start | bytes 10760 | tf_op jit(solution)/shard_map/ppermute | solution.py:328
  66.4 18.8 %copy-start = (f32[512,1024]{1,0:T(8,128)S(1)}, f32[512,1024]{1,0:T(8,128)}, u32[]{:S(2)}) copy-start(f32[512,1024]{1,0:T(8,128)} %x_hbm.1) | copy-start | bytes 6291460
  66.4 18.8 %copy-start.9 = (s32[512]{0:T(512)S(1)}, s32[512]{0:T(512)}, u32[]{:S(2)}) copy-start(s32[512]{0:T(512)} %param.5) | copy-start | bytes 6148
  67.8 4.3 %collective-permute-start.13 = (f32[1,896]{1,0:T(1,128)S(1)}, f32[1,896]{1,0:T(1,128)S(1)}, u32[]{:S(2)}, u32[]{:S(2)}) collective-permute-start(f32[1,896]{1,0:T(1,128)S(1)} %get-tuple-element.84), channel_id=1, source_target_pairs={{0,2},{1,3},{2,4},{3,5},{4,6},{5,7},{6,1},{7,0},{8,10},{9,11},{10,... | collective-permute-start | bytes 10760 | tf_op jit(solution)/shard_map/ppermute | solution.py:328
  69.3 3.0 %collective-permute-start.14 = (f32[1,896]{1,0:T(1,128)S(1)}, f32[1,896]{1,0:T(1,128)S(1)}, u32[]{:S(2)}, u32[]{:S(2)}) collective-permute-start(f32[1,896]{1,0:T(1,128)S(1)} %get-tuple-element.85), channel_id=1, source_target_pairs={{0,6},{1,7},{2,1},{3,0},{4,3},{5,2},{6,5},{7,4},{8,14},{9,15},{10,... | collective-permute-start | bytes 10760 | tf_op jit(solution)/shard_map/ppermute | solution.py:328
  73.1 11.4 %all-to-all-start.3 = ((f32[16,1,128]{2,1,0:T(1,128)}), f32[16,1,128]{2,1,0:T(1,128)S(1)}, u32[]{:S(2)}, u32[]{:S(2)}) async-start(f32[16,1,128]{2,1,0:T(1,128)} %bitcast.12), calls=%async_computation.3 | async-start | bytes 16384 | tf_op jit(solution)/shard_map/all_to_all | solution.py:338

commit v7 on v6

--- a/solution.py
+++ b/solution.py
@@ -94,8 +94,7 @@
     )(embeddings, ids)
 
 
-def rest_kernel(unit_ref, meta_ref, second_ref, ranks_ref):
-    ranks_ref[...] = (iota(ranks_ref.shape, 0) == meta_ref[1:2, :]).astype(BF16)
+def rest_kernel(unit_ref, meta_ref, second_ref):
     place(1, unit_ref[...], meta_ref[0:1, :], meta_ref[1:2, :], second_ref)
 
 
@@ -103,31 +102,22 @@
     rows, width = unit.shape
     return pl.pallas_call(
         rest_kernel,
-        out_shape=(
-            jax.ShapeDtypeStruct((CHUNK, width), BF16),
-            jax.ShapeDtypeStruct((128, rows), BF16),
-        ),
+        out_shape=jax.ShapeDtypeStruct((CHUNK, width), BF16),
         compiler_params=params(),
         cost_estimate=cost(2 * CHUNK * rows * width, 4 * rows * width),
         name="rest",
     )(unit, meta)
 
 
-def pack_kernel(block_ref, packed_ref, source_ref, spread_ref):
+def pack_kernel(block_ref, packed_ref, spot_ref):
     rows = block_ref.shape[0]
     full = jnp.where(marked(block_ref[:, 0:128]), 0.0, 1.0)
     full = jnp.transpose(jnp.broadcast_to(full, (rows, 128)))[0:8, :]
     upto = (iota((rows, rows), 0) <= iota((rows, rows), 1)).astype(BF16)
     count = jnp.dot(full.astype(BF16), upto, preferred_element_type=F32)
     spot = jnp.where(full > 0.5, count - 1.0, -1.0).astype(jnp.int32)
-    wide = (iota((lanes(SHORT), rows), 0) == spot[0:1, :]).astype(BF16)
-    source = (iota((OWNERS, rows), 1) // HALF == iota((OWNERS, rows), 0)).astype(BF16)
-    source_ref[...] = lax.dot_general(
-        source, wide, (((1,), (1,)), ((), ())), preferred_element_type=F32
-    )
-    lane = (iota((rows, 128), 0) % HALF + HALF == iota((rows, 128), 1)).astype(BF16)
-    spread_ref[...] = jnp.dot(wide, lane, preferred_element_type=F32).astype(BF16)
-    onehot = wide[0:SHORT, :]
+    spot_ref[...] = spot
+    onehot = (iota((SHORT, rows), 0) == spot[0:1, :]).astype(BF16)
     moved = jnp.dot(onehot, block_ref[...], preferred_element_type=F32)
     taken = jnp.dot(onehot, jnp.ones((rows, 128), BF16), preferred_element_type=F32)
     packed_ref[...] = moved.astype(BF16)
@@ -141,17 +131,54 @@
         pack_kernel,
         out_shape=(
             jax.ShapeDtypeStruct((SHORT, width), BF16),
+            jax.ShapeDtypeStruct((8, rows), jnp.int32),
+        ),
+        compiler_params=params(),
+        cost_estimate=cost(2 * SHORT * rows * width, 4 * rows * width),
+        name="pack",
+    )(block)
+
+
+def lanes(rows):
+    return -(-rows // 128) * 128
+
+
+def moves_kernel(spot_ref, source_ref, spread_ref):
+    rows = spot_ref.shape[1]
+    onehot = (iota((lanes(SHORT), rows), 0) == spot_ref[0:1, :]).astype(BF16)
+    source = (iota((OWNERS, rows), 1) // HALF == iota((OWNERS, rows), 0)).astype(BF16)
+    source_ref[...] = lax.dot_general(
+        source, onehot, (((1,), (1,)), ((), ())), preferred_element_type=F32
+    )
+    lane = (iota((rows, 128), 0) % HALF + HALF == iota((rows, 128), 1)).astype(BF16)
+    spread_ref[...] = jnp.dot(onehot, lane, preferred_element_type=F32).astype(BF16)
+
+
+def moves_of(spot):
+    return pl.pallas_call(
+        moves_kernel,
+        out_shape=(
             jax.ShapeDtypeStruct((OWNERS, lanes(SHORT)), F32),
             jax.ShapeDtypeStruct((lanes(SHORT), 128), BF16),
         ),
         compiler_params=params(),
-        cost_estimate=cost(2 * SHORT * rows * width, 4 * rows * width),
-        name="pack",
-    )(block)
-
-
-def lanes(rows):
-    return -(-rows // 128) * 128
+        cost_estimate=cost(2 * lanes(SHORT) * spot.shape[1] * 256, 1 << 20),
+        name="moves",
+    )(spot)
+
+
+def ranks_kernel(meta_ref, ranks_ref):
+    ranks_ref[...] = (iota(ranks_ref.shape, 0) == meta_ref[1:2, :]).astype(BF16)
+
+
+def ranks_of(meta):
+    return pl.pallas_call(
+        ranks_kernel,
+        out_shape=jax.ShapeDtypeStruct((128, meta.shape[1]), BF16),
+        compiler_params=params(),
+        cost_estimate=cost(1 << 16, 1 << 17),
+        name="ranks",
+    )(meta)
 
 
 def pair_kernel(units, n_blocks, n_before, wanted, tails, *refs):
@@ -386,24 +413,22 @@
     own_a = to_owners(first)
     own_a, unit = lax.optimization_barrier((own_a, unit))
     a = neighbours(own_a)
-    second, ranks = rest(unit, meta)
-    return a, to_owners(second), (meta, ranks)
+    return a, to_owners(rest(unit, meta)), meta
 
 
 def whole(embeddings, ids, a, own_b):
-    _, unit, meta = prep(embeddings, ids)
-    _, ranks = rest(unit, meta)
+    _, _, meta = prep(embeddings, ids)
     best = match(a, neighbours(own_b), ())
-    return give_back(*best, (meta, ranks))[0]
+    return give_back(*best, (meta, ranks_of(meta)))[0]
 
 
 def per_device(embeddings, cluster_ids):
     ids = cluster_ids.reshape(1, -1)
-    a, own_b, own_rows = exchange(embeddings, ids)
-    packed, *moves = pack(own_b)
-    packed, *a = lax.optimization_barrier((packed, *a))
+    a, own_b, meta = exchange(embeddings, ids)
+    packed, spot = pack(own_b)
+    packed, spot, meta, *a = lax.optimization_barrier((packed, spot, meta, *a))
     best = match(a, neighbours(packed), (1, 3, 6, 7))
-    value, flag = give_back(*best, own_rows, *moves)
+    value, flag = give_back(*best, (meta, ranks_of(meta)), *moves_of(spot))
     return lax.cond(
         flag.reshape(()) != 0, lambda: whole(embeddings, ids, a, own_b), lambda: value
     ).reshape(-1)

time: 85.5 us -> 85.3 us (level)
  no operation moved by 1% of the time
where the time goes in v7:
time: 85.3 us; the launch traced here: 85.1 us
  blocking collectives  44.4 us (52%)
  starting transfers between devices  14.8 us (17%)
  waiting for transfers between devices  13 us (15%)
  Pallas kernels  12.7 us (15%)
    all_to_all x2, blocking collectives, to_owners(): lax.all_to_all(block, 'wide', split_axis=0, concat_axis=0, tiled=True)  44.4 us
    ppermute x9, starting transfers between devices, along_pair(): return lax.ppermute(block, 'pair', perm)  10.9 us
    all_to_all x1, waiting for transfers between devices, give_back(): lax.all_to_all(tiles.reshape(OWNERS, 1, 128), 'wide', split_axis=0, conca...  7.37 us
    pallas_call x2, Pallas kernels, pairs(): pl.pallas_call(functools.partial(pair_kernel, units, n, len(before), want...  6.95 us
    ppermute x9, waiting for transfers between devices, along_pair(): return lax.ppermute(block, 'pair', perm)  5.59 us
    all_to_all x1, starting transfers between devices, give_back(): lax.all_to_all(tiles.reshape(OWNERS, 1, 128), 'wide', split_axis=0, conca...  3.83 us
    pallas_call x1, Pallas kernels, prep(): pl.pallas_call(prep_kernel, in_specs=[pl.BlockSpec(memory_space=pltpu.HBM...  2.46 us
  transfers between devices with their start and end apart: 10, of which 4 were waited for; matrix products, arithmetic and copies ran while one was open for 0% of the time, Pallas kernels for 9%

profile of v7, /device:TPU:0, one launch (start us, length us, event | category | flops | bytes accessed | tf_op | source)
XLA Modules:
  0.0 85.1 jit_solution(11462691004425404108)
XLA Ops:
  0.0 2.5 %prep.3 = (bf16[512,1024]{1,0:T(8,128)(2,1)S(1)}, bf16[512,1024]{1,0:T(8,128)(2,1)S(1)}, s32[8,512]{1,0:T(8,128)S(1)}) custom-call(f32[512,1024]{1,0:T(8,128)} %x_hbm.1, s32[1,512]{1,0:T(1,128)} %bitcast.28), custom_call_target="tpu_custom_call" | custom-call | flops 536870912 | bytes 4194304 | tf_op jit(solution)/shard_map/prep/pallas_call | solution.py:78
  2.5 23.8 %all_to_all.19 = bf16[16,32,1024]{2,1,0:T(8,128)(2,1)S(1)} all-to-all(bf16[16,32,1024]{2,1,0:T(8,128)(2,1)S(1)} %bitcast.17), channel_id=1, replica_groups=mesh['wide'=16,'pair'=8] {'wide'}, dimensions={0} | all-to-all | bytes 2097152 | tf_op jit(solution)/shard_map/all_to_all | solution.py:351
  26.2 0.0 copy-start.1
  26.2 0.1 collective-permute-start.8
  26.3 2.1 %collective-permute-start.7 = (bf16[512,1024]{1,0:T(8,128)(2,1)S(1)}, bf16[512,1024]{1,0:T(8,128)(2,1)S(1)}, u32[]{:S(2)}, u32[]{:S(2)}) collective-permute-start(bf16[512,1024]{1,0:T(8,128)(2,1)S(1)} %bitcast.23), channel_id=1, source_target_pairs={{2,0},{3,1},{4,2},{5,3},{6,4},{7,5},{1,6},{0,7},{10,8},{11,9},{12,... | collective-permute-start | bytes 3145736 | tf_op jit(solution)/shard_map/ppermute | solution.py:355
  28.4 1.9 %collective-permute-start.6 = (bf16[512,1024]{1,0:T(8,128)(2,1)S(1)}, bf16[512,1024]{1,0:T(8,128)(2,1)S(1)}, u32[]{:S(2)}, u32[]{:S(2)}) collective-permute-start(bf16[512,1024]{1,0:T(8,128)(2,1)S(1)} %bitcast.24), channel_id=1, source_target_pairs={{0,1},{1,0},{2,3},{3,2},{4,5},{5,4},{6,7},{7,6},{8,9},{9,8},{10,11... | collective-permute-start | bytes 3145736 | tf_op jit(solution)/shard_map/ppermute | solution.py:355
  30.4 0.9 rest.1
  31.2 20.7 %all_to_all.20 = bf16[16,32,1024]{2,1,0:T(8,128)(2,1)S(1)} all-to-all(bf16[16,32,1024]{2,1,0:T(8,128)(2,1)S(1)} %bitcast.16), channel_id=1, replica_groups=mesh['wide'=16,'pair'=8] {'wide'}, dimensions={0} | all-to-all | bytes 2097152 | tf_op jit(solution)/shard_map/all_to_all | solution.py:351
  51.9 0.7 pack.1
  52.6 0.0 collective-permute-done.8.refs_5_
  52.6 0.0 copy-start.3
  52.6 0.0 collective-permute-done.7.refs_4_
  52.6 0.0 copy-start.5
  52.6 0.0 collective-permute-done.6.refs_2_
  52.7 0.0 copy-start.7
  52.7 0.1 collective-permute-start.9
  52.8 1.1 %collective-permute-start.11 = (bf16[208,1024]{1,0:T(8,128)(2,1)S(1)}, bf16[208,1024]{1,0:T(8,128)(2,1)S(1)}, u32[]{:S(2)}, u32[]{:S(2)}) collective-permute-start(bf16[208,1024]{1,0:T(8,128)(2,1)S(1)} %get-tuple-element.74.refs_1_), channel_id=1, source_target_pairs={{6,0},{7,1},{1,2},{0,3},{3,4},{2,5},{5,6},{4,7},{14,8},{15,9},{9,1... | collective-permute-start | bytes 1277960 | tf_op jit(solution)/shard_map/ppermute | solution.py:355
  53.9 2.0 %collective-permute-start.10 = (bf16[208,1024]{1,0:T(8,128)(2,1)S(1)}, bf16[208,1024]{1,0:T(8,128)(2,1)S(1)}, u32[]{:S(2)}, u32[]{:S(2)}) collective-permute-start(bf16[208,1024]{1,0:T(8,128)(2,1)S(1)} %get-tuple-element.74.refs_1_), channel_id=1, source_target_pairs={{2,0},{3,1},{4,2},{5,3},{6,4},{7,5},{1,6},{0,7},{10,8},{11,9},{12,... | collective-permute-start | bytes 1277960 | tf_op jit(solution)/shard_map/ppermute | solution.py:355
  55.9 0.0 collective-permute-done.9.refs_3_
  55.9 5.6 %early.3 = (f32[1,896]{1,0:T(1,128)S(1)}, f32[1,896]{1,0:T(1,128)S(1)}, f32[1,896]{1,0:T(1,128)S(1)}, f32[1,896]{1,0:T(1,128)S(1)}) custom-call(bf16[512,1024]{1,0:T(8,128)(2,1)S(1)} %bitcast.25, bf16[208,1024]{1,0:T(8,128)(2,1)S(1)} %get-tuple-element.74.refs_1_, bf16[512,1024]{1,0:T(8,128)(2,1)S(1)} %collective-permute-done.6.refs_2_, ...), custom_call_target="tpu_custom_call" | custom-call | flops 4388290560 | bytes 6291456 | tf_op jit(solution)/shard_map/early/pallas_call | solution.py:248
  61.5 0.4 collective-permute-start.12
  61.9 4.4 %collective-permute-done.11.refs_7_ = bf16[208,1024]{1,0:T(8,128)(2,1)S(1)} collective-permute-done((bf16[208,1024]{1,0:T(8,128)(2,1)S(1)}, bf16[208,1024]{1,0:T(8,128)(2,1)S(1)}, u32[]{:S(2)}, u32[]{:S(2)}) %collective-permute-start.11) | collective-permute-done | bytes 426016 | tf_op jit(solution)/shard_map/ppermute | solution.py:355
  66.3 0.0 collective-permute-done.10.refs_6_
  66.3 0.0 collective-permute-done.12.refs_9_
  66.3 0.0 copy-done.1
  66.3 0.0 copy-done.3
  66.3 0.0 copy-done.5
  66.3 0.0 copy-done.7
  66.3 0.0 copy-start
  66.3 0.0 copy-start.9
  66.3 1.3 %late.3 = (f32[1,896]{1,0:T(1,128)S(1)}, f32[1,896]{1,0:T(1,128)S(1)}, f32[1,896]{1,0:T(1,128)S(1)}) custom-call(bf16[512,1024]{1,0:T(8,128)(2,1)S(1)} %bitcast.26, bf16[208,1024]{1,0:T(8,128)(2,1)S(1)} %get-tuple-element.74.refs_1_, bf16[512,1024]{1,0:T(8,128)(2,1)S(1)} %collective-permute-done.6.refs_2_, ...), custom_call_target="tpu_custom_call" | custom-call | flops 702021632 | bytes 8388608 | tf_op jit(solution)/shard_map/late/pallas_call | solution.py:248
  67.7 1.7 %collective-permute-start.13 = (f32[1,896]{1,0:T(1,128)S(1)}, f32[1,896]{1,0:T(1,128)S(1)}, u32[]{:S(2)}, u32[]{:S(2)}) collective-permute-start(f32[1,896]{1,0:T(1,128)S(1)} %get-tuple-element.83), channel_id=1, source_target_pairs={{0,2},{1,3},{2,4},{3,5},{4,6},{5,7},{6,1},{7,0},{8,10},{9,11},{10,... | collective-permute-start | bytes 10760 | tf_op jit(solution)/shard_map/ppermute | solution.py:355
  69.3 1.5 %collective-permute-start.14 = (f32[1,896]{1,0:T(1,128)S(1)}, f32[1,896]{1,0:T(1,128)S(1)}, u32[]{:S(2)}, u32[]{:S(2)}) collective-permute-start(f32[1,896]{1,0:T(1,128)S(1)} %get-tuple-element.84), channel_id=1, source_target_pairs={{0,6},{1,7},{2,1},{3,0},{4,3},{5,2},{6,5},{7,4},{8,14},{9,15},{10,... | collective-permute-start | bytes 10760 | tf_op jit(solution)/shard_map/ppermute | solution.py:355
  70.8 0.3 moves.1
  71.1 0.8 collective-permute-done.13.a_ref
  72.0 0.4 collective-permute-done.14.b_ref
  72.3 0.7 join.3
  73.1 3.8 %all-to-all-start.3 = ((f32[16,1,128]{2,1,0:T(1,128)}), f32[16,1,128]{2,1,0:T(1,128)S(1)}, u32[]{:S(2)}, u32[]{:S(2)}) async-start(f32[16,1,128]{2,1,0:T(1,128)} %bitcast.12), calls=%async_computation.3 | async-start | bytes 16384 | tf_op jit(solution)/shard_map/all_to_all | solution.py:365
  77.0 7.4 %all-to-all-done.3 = f32[16,1,128]{2,1,0:T(1,128)S(1)} async-done(((f32[16,1,128]{2,1,0:T(1,128)}), f32[16,1,128]{2,1,0:T(1,128)S(1)}, u32[]{:S(2)}, u32[]{:S(2)}) %all-to-all-start.3) | async-done | bytes 8224 | tf_op jit(solution)/shard_map/all_to_all | solution.py:365
  84.3 0.7 pick.3
  85.1 0.0 copy-done
  85.1 0.0 copy-done.9
  (2 shorter events, 0.0 us)
Async XLA Ops:
  26.2 40.0 %copy-start.1 = (bf16[16,32,1024]{2,1,0:T(8,128)(2,1)}, bf16[16,32,1024]{2,1,0:T(8,128)(2,1)S(1)}, u32[]{:S(2)}) copy-start(bf16[16,32,1024]{2,1,0:T(8,128)(2,1)S(1)} %all_to_all.19) | copy-start | bytes 3145732
  26.2 26.4 %collective-permute-start.8 = (bf16[512,1024]{1,0:T(8,128)(2,1)S(1)}, bf16[512,1024]{1,0:T(8,128)(2,1)S(1)}, u32[]{:S(2)}, u32[]{:S(2)}) collective-permute-start(bf16[512,1024]{1,0:T(8,128)(2,1)S(1)} %bitcast.22), channel_id=1, source_target_pairs={{6,0},{7,1},{1,2},{0,3},{3,4},{2,5},{5,6},{4,7},{14,8},{15,9},{9,1... | collective-permute-start | bytes 3145736 | tf_op jit(solution)/shard_map/ppermute | solution.py:355
  26.3 26.3 %collective-permute-start.7 = (bf16[512,1024]{1,0:T(8,128)(2,1)S(1)}, bf16[512,1024]{1,0:T(8,128)(2,1)S(1)}, u32[]{:S(2)}, u32[]{:S(2)}) collective-permute-start(bf16[512,1024]{1,0:T(8,128)(2,1)S(1)} %bitcast.23), channel_id=1, source_target_pairs={{2,0},{3,1},{4,2},{5,3},{6,4},{7,5},{1,6},{0,7},{10,8},{11,9},{12,... | collective-permute-start | bytes 3145736 | tf_op jit(solution)/shard_map/ppermute | solution.py:355
  28.4 24.2 %collective-permute-start.6 = (bf16[512,1024]{1,0:T(8,128)(2,1)S(1)}, bf16[512,1024]{1,0:T(8,128)(2,1)S(1)}, u32[]{:S(2)}, u32[]{:S(2)}) collective-permute-start(bf16[512,1024]{1,0:T(8,128)(2,1)S(1)} %bitcast.24), channel_id=1, source_target_pairs={{0,1},{1,0},{2,3},{3,2},{4,5},{5,4},{6,7},{7,6},{8,9},{9,8},{10,11... | collective-permute-start | bytes 3145736 | tf_op jit(solution)/shard_map/ppermute | solution.py:355
  52.6 13.7 %copy-start.3 = (bf16[512,1024]{1,0:T(8,128)(2,1)}, bf16[512,1024]{1,0:T(8,128)(2,1)S(1)}, u32[]{:S(2)}) copy-start(bf16[512,1024]{1,0:T(8,128)(2,1)S(1)} %collective-permute-done.8.refs_5_) | copy-start | bytes 3145732
  52.6 13.6 %copy-start.5 = (bf16[512,1024]{1,0:T(8,128)(2,1)}, bf16[512,1024]{1,0:T(8,128)(2,1)S(1)}, u32[]{:S(2)}) copy-start(bf16[512,1024]{1,0:T(8,128)(2,1)S(1)} %collective-permute-done.7.refs_4_) | copy-start | bytes 3145732
  52.7 13.6 %copy-start.7 = (bf16[512,1024]{1,0:T(8,128)(2,1)}, bf16[512,1024]{1,0:T(8,128)(2,1)S(1)}, u32[]{:S(2)}) copy-start(bf16[512,1024]{1,0:T(8,128)(2,1)S(1)} %collective-permute-done.6.refs_2_) | copy-start | bytes 3145732
  52.7 3.2 %collective-permute-start.9 = (bf16[208,1024]{1,0:T(8,128)(2,1)S(1)}, bf16[208,1024]{1,0:T(8,128)(2,1)S(1)}, u32[]{:S(2)}, u32[]{:S(2)}) collective-permute-start(bf16[208,1024]{1,0:T(8,128)(2,1)S(1)} %get-tuple-element.74.refs_1_), channel_id=1, source_target_pairs={{0,1},{1,0},{2,3},{3,2},{4,5},{5,4},{6,7},{7,6},{8,9},{9,8},{10,11... | collective-permute-start | bytes 1277960 | tf_op jit(solution)/shard_map/ppermute | solution.py:355
  52.8 13.5 %collective-permute-start.11 = (bf16[208,1024]{1,0:T(8,128)(2,1)S(1)}, bf16[208,1024]{1,0:T(8,128)(2,1)S(1)}, u32[]{:S(2)}, u32[]{:S(2)}) collective-permute-start(bf16[208,1024]{1,0:T(8,128)(2,1)S(1)} %get-tuple-element.74.refs_1_), channel_id=1, source_target_pairs={{6,0},{7,1},{1,2},{0,3},{3,4},{2,5},{5,6},{4,7},{14,8},{15,9},{9,1... | collective-permute-start | bytes 1277960 | tf_op jit(solution)/shard_map/ppermute | solution.py:355
  53.9 12.4 %collective-permute-start.10 = (bf16[208,1024]{1,0:T(8,128)(2,1)S(1)}, bf16[208,1024]{1,0:T(8,128)(2,1)S(1)}, u32[]{:S(2)}, u32[]{:S(2)}) collective-permute-start(bf16[208,1024]{1,0:T(8,128)(2,1)S(1)} %get-tuple-element.74.refs_1_), channel_id=1, source_target_pairs={{2,0},{3,1},{4,2},{5,3},{6,4},{7,5},{1,6},{0,7},{10,8},{11,9},{12,... | collective-permute-start | bytes 1277960 | tf_op jit(solution)/shard_map/ppermute | solution.py:355
  61.5 4.8 %collective-permute-start.12 = (f32[1,896]{1,0:T(1,128)S(1)}, f32[1,896]{1,0:T(1,128)S(1)}, u32[]{:S(2)}, u32[]{:S(2)}) collective-permute-start(f32[1,896]{1,0:T(1,128)S(1)} %get-tuple-element.79), channel_id=1, source_target_pairs={{0,1},{1,0},{2,3},{3,2},{4,5},{5,4},{6,7},{7,6},{8,9},{9,8},{10,11... | collective-permute-start | bytes 10760 | tf_op jit(solution)/shard_map/ppermute | solution.py:355
  66.3 18.8 %copy-start = (f32[512,1024]{1,0:T(8,128)S(1)}, f32[512,1024]{1,0:T(8,128)}, u32[]{:S(2)}) copy-start(f32[512,1024]{1,0:T(8,128)} %x_hbm.1) | copy-start | bytes 6291460
  66.3 18.8 %copy-start.9 = (s32[512]{0:T(512)S(1)}, s32[512]{0:T(512)}, u32[]{:S(2)}) copy-start(s32[512]{0:T(512)} %param.5) | copy-start | bytes 6148
  67.7 4.3 %collective-permute-start.13 = (f32[1,896]{1,0:T(1,128)S(1)}, f32[1,896]{1,0:T(1,128)S(1)}, u32[]{:S(2)}, u32[]{:S(2)}) collective-permute-start(f32[1,896]{1,0:T(1,128)S(1)} %get-tuple-element.83), channel_id=1, source_target_pairs={{0,2},{1,3},{2,4},{3,5},{4,6},{5,7},{6,1},{7,0},{8,10},{9,11},{10,... | collective-permute-start | bytes 10760 | tf_op jit(solution)/shard_map/ppermute | solution.py:355
  69.3 3.0 %collective-permute-start.14 = (f32[1,896]{1,0:T(1,128)S(1)}, f32[1,896]{1,0:T(1,128)S(1)}, u32[]{:S(2)}, u32[]{:S(2)}) collective-permute-start(f32[1,896]{1,0:T(1,128)S(1)} %get-tuple-element.84), channel_id=1, source_target_pairs={{0,6},{1,7},{2,1},{3,0},{4,3},{5,2},{6,5},{7,4},{8,14},{9,15},{10,... | collective-permute-start | bytes 10760 | tf_op jit(solution)/shard_map/ppermute | solution.py:355
  73.1 11.2 %all-to-all-start.3 = ((f32[16,1,128]{2,1,0:T(1,128)}), f32[16,1,128]{2,1,0:T(1,128)S(1)}, u32[]{:S(2)}, u32[]{:S(2)}) async-start(f32[16,1,128]{2,1,0:T(1,128)} %bitcast.12), calls=%async_computation.3 | async-start | bytes 16384 | tf_op jit(solution)/shard_map/all_to_all | solution.py:365

commit v8 on v6

--- a/solution.py
+++ b/solution.py
@@ -49,7 +49,7 @@
 
 def prep_kernel(x_hbm, ids_hbm, first_ref, unit_ref, meta_ref, x_ref, ids_ref, sems):
     rows = x_ref.shape[0]
-    parts = 4
+    parts = 8
     step = rows // parts
     copies = [pltpu.make_async_copy(ids_hbm, ids_ref, sems.at[parts])]
     for i in range(parts):
@@ -64,9 +64,11 @@
     counts = jnp.dot(onehot.astype(BF16), upto, preferred_element_type=F32)
     rank = jnp.sum(jnp.where(onehot, counts, 0.0), axis=0, keepdims=True).astype(jnp.int32) - 1
     meta_ref[...] = jnp.where(iota((8, rows), 0) == 0, ids, rank)
-    for i in range(parts):
-        copies[i + 1].wait()
-        at = pl.ds(i * step, step)
+    groups = 2
+    for i in range(groups):
+        for j in range(parts // groups):
+            copies[1 + i * (parts // groups) + j].wait()
+        at = pl.ds(i * (rows // groups), rows // groups)
         x = x_ref[at, :]
         scale = lax.rsqrt(jnp.sum(x * x, axis=1, keepdims=True) + EPSILON)
         unit_ref[at, :] = (x * scale).astype(BF16)
@@ -86,7 +88,7 @@
         scratch_shapes=[
             pltpu.VMEM((rows, width), F32),
             pltpu.VMEM((1, rows), jnp.int32),
-            pltpu.SemaphoreType.DMA((5,)),
+            pltpu.SemaphoreType.DMA((9,)),
         ],
         compiler_params=params(),
         cost_estimate=cost(2 * CHUNK * rows * width, 8 * rows * width),

time: 85.5 us -> 85.5 us (level)
  no operation moved by 1% of the time
where the time goes in v8:
time: 85.5 us; the launch traced here: 85.3 us
  blocking collectives  44.4 us (52%)
  starting transfers between devices  14.8 us (17%)
  waiting for transfers between devices  13.3 us (16%)
  Pallas kernels  12.6 us (15%)
    all_to_all x2, blocking collectives, to_owners(): lax.all_to_all(block, 'wide', split_axis=0, concat_axis=0, tiled=True)  44.4 us
    ppermute x9, starting transfers between devices, along_pair(): return lax.ppermute(block, 'pair', perm)  10.9 us
    all_to_all x1, waiting for transfers between devices, give_back(): lax.all_to_all(tiles.reshape(OWNERS, 1, 128), 'wide', split_axis=0, conca...  7.56 us
    pallas_call x2, Pallas kernels, pairs(): pl.pallas_call(functools.partial(pair_kernel, units, n, len(before), want...  6.96 us
    ppermute x9, waiting for transfers between devices, along_pair(): return lax.ppermute(block, 'pair', perm)  5.71 us
    all_to_all x1, starting transfers between devices, give_back(): lax.all_to_all(tiles.reshape(OWNERS, 1, 128), 'wide', split_axis=0, conca...  3.84 us
    pallas_call x1, Pallas kernels, prep(): pl.pallas_call(prep_kernel, in_specs=[pl.BlockSpec(memory_space=pltpu.HBM...  2.5 us
  transfers between devices with their start and end apart: 10, of which 4 were waited for; matrix products, arithmetic and copies ran while one was open for 0% of the time, Pallas kernels for 9%

profile of v8, /device:TPU:0, one launch (start us, length us, event | category | flops | bytes accessed | tf_op | source)
XLA Modules:
  0.0 85.3 jit_solution(13268345560513576769)
XLA Ops:
  0.0 2.5 %prep.3 = (bf16[512,1024]{1,0:T(8,128)(2,1)S(1)}, bf16[512,1024]{1,0:T(8,128)(2,1)S(1)}, s32[8,512]{1,0:T(8,128)S(1)}) custom-call(f32[512,1024]{1,0:T(8,128)} %x_hbm.1, s32[1,512]{1,0:T(1,128)} %bitcast.28), custom_call_target="tpu_custom_call" | custom-call | flops 536870912 | bytes 4194304 | tf_op jit(solution)/shard_map/prep/pallas_call | solution.py:80
  2.5 23.8 %all_to_all.19 = bf16[16,32,1024]{2,1,0:T(8,128)(2,1)S(1)} all-to-all(bf16[16,32,1024]{2,1,0:T(8,128)(2,1)S(1)} %bitcast.16), channel_id=1, replica_groups=mesh['wide'=16,'pair'=8] {'wide'}, dimensions={0} | all-to-all | bytes 2097152 | tf_op jit(solution)/shard_map/all_to_all | solution.py:326
  26.3 0.0 copy-start.1
  26.3 0.1 collective-permute-start.8
  26.4 2.1 %collective-permute-start.7 = (bf16[512,1024]{1,0:T(8,128)(2,1)S(1)}, bf16[512,1024]{1,0:T(8,128)(2,1)S(1)}, u32[]{:S(2)}, u32[]{:S(2)}) collective-permute-start(bf16[512,1024]{1,0:T(8,128)(2,1)S(1)} %bitcast.23), channel_id=1, source_target_pairs={{2,0},{3,1},{4,2},{5,3},{6,4},{7,5},{1,6},{0,7},{10,8},{11,9},{12,... | collective-permute-start | bytes 3145736 | tf_op jit(solution)/shard_map/ppermute | solution.py:330
  28.5 1.9 %collective-permute-start.6 = (bf16[512,1024]{1,0:T(8,128)(2,1)S(1)}, bf16[512,1024]{1,0:T(8,128)(2,1)S(1)}, u32[]{:S(2)}, u32[]{:S(2)}) collective-permute-start(bf16[512,1024]{1,0:T(8,128)(2,1)S(1)} %bitcast.24), channel_id=1, source_target_pairs={{0,1},{1,0},{2,3},{3,2},{4,5},{5,4},{6,7},{7,6},{8,9},{9,8},{10,11... | collective-permute-start | bytes 3145736 | tf_op jit(solution)/shard_map/ppermute | solution.py:330
  30.4 0.9 %rest.3 = (bf16[512,1024]{1,0:T(8,128)(2,1)S(1)}, bf16[128,512]{1,0:T(8,128)(2,1)S(1)}) custom-call(bf16[512,1024]{1,0:T(8,128)(2,1)S(1)} %get-tuple-element.69.unit_ref, s32[8,512]{1,0:T(8,128)S(1)} %get-tuple-element.70.meta_ref), custom_call_target="tpu_custom_call" | custom-call | flops 536870912 | bytes 2097152 | tf_op jit(solution)/shard_map/rest/pallas_call | solution.py:106
  31.3 20.7 %all_to_all.20 = bf16[16,32,1024]{2,1,0:T(8,128)(2,1)S(1)} all-to-all(bf16[16,32,1024]{2,1,0:T(8,128)(2,1)S(1)} %bitcast.17), channel_id=1, replica_groups=mesh['wide'=16,'pair'=8] {'wide'}, dimensions={0} | all-to-all | bytes 2097152 | tf_op jit(solution)/shard_map/all_to_all | solution.py:326
  52.0 0.8 pack.1
  52.8 0.0 collective-permute-done.8.refs_5_
  52.8 0.0 copy-start.3
  52.8 0.0 collective-permute-done.7.refs_4_
  52.8 0.0 copy-start.5
  52.8 0.0 collective-permute-done.6.refs_2_
  52.9 0.0 copy-start.7
  52.9 0.1 collective-permute-start.9
  53.0 0.9 %collective-permute-start.11 = (bf16[208,1024]{1,0:T(8,128)(2,1)S(1)}, bf16[208,1024]{1,0:T(8,128)(2,1)S(1)}, u32[]{:S(2)}, u32[]{:S(2)}) collective-permute-start(bf16[208,1024]{1,0:T(8,128)(2,1)S(1)} %get-tuple-element.75.refs_1_), channel_id=1, source_target_pairs={{6,0},{7,1},{1,2},{0,3},{3,4},{2,5},{5,6},{4,7},{14,8},{15,9},{9,1... | collective-permute-start | bytes 1277960 | tf_op jit(solution)/shard_map/ppermute | solution.py:330
  53.9 2.1 %collective-permute-start.10 = (bf16[208,1024]{1,0:T(8,128)(2,1)S(1)}, bf16[208,1024]{1,0:T(8,128)(2,1)S(1)}, u32[]{:S(2)}, u32[]{:S(2)}) collective-permute-start(bf16[208,1024]{1,0:T(8,128)(2,1)S(1)} %get-tuple-element.75.refs_1_), channel_id=1, source_target_pairs={{2,0},{3,1},{4,2},{5,3},{6,4},{7,5},{1,6},{0,7},{10,8},{11,9},{12,... | collective-permute-start | bytes 1277960 | tf_op jit(solution)/shard_map/ppermute | solution.py:330
  56.0 0.0 collective-permute-done.9.refs_3_
  56.0 5.6 %early.3 = (f32[1,896]{1,0:T(1,128)S(1)}, f32[1,896]{1,0:T(1,128)S(1)}, f32[1,896]{1,0:T(1,128)S(1)}, f32[1,896]{1,0:T(1,128)S(1)}) custom-call(bf16[512,1024]{1,0:T(8,128)(2,1)S(1)} %bitcast.25, bf16[208,1024]{1,0:T(8,128)(2,1)S(1)} %get-tuple-element.75.refs_1_, bf16[512,1024]{1,0:T(8,128)(2,1)S(1)} %collective-permute-done.6.refs_2_, ...), custom_call_target="tpu_custom_call" | custom-call | flops 4388290560 | bytes 6291456 | tf_op jit(solution)/shard_map/early/pallas_call | solution.py:223
  61.6 0.4 collective-permute-start.12
  62.1 4.3 %collective-permute-done.11.refs_7_ = bf16[208,1024]{1,0:T(8,128)(2,1)S(1)} collective-permute-done((bf16[208,1024]{1,0:T(8,128)(2,1)S(1)}, bf16[208,1024]{1,0:T(8,128)(2,1)S(1)}, u32[]{:S(2)}, u32[]{:S(2)}) %collective-permute-start.11) | collective-permute-done | bytes 426016 | tf_op jit(solution)/shard_map/ppermute | solution.py:330
  66.4 0.0 collective-permute-done.10.refs_6_
  66.4 0.0 collective-permute-done.12.refs_9_
  66.4 0.0 copy-done.1
  66.4 0.0 copy-done.3
  66.4 0.0 copy-done.5
  66.4 0.0 copy-done.7
  66.4 0.0 copy-start
  66.5 0.0 copy-start.9
  66.5 1.4 %late.3 = (f32[1,896]{1,0:T(1,128)S(1)}, f32[1,896]{1,0:T(1,128)S(1)}, f32[1,896]{1,0:T(1,128)S(1)}) custom-call(bf16[512,1024]{1,0:T(8,128)(2,1)S(1)} %bitcast.26, bf16[208,1024]{1,0:T(8,128)(2,1)S(1)} %get-tuple-element.75.refs_1_, bf16[512,1024]{1,0:T(8,128)(2,1)S(1)} %collective-permute-done.6.refs_2_, ...), custom_call_target="tpu_custom_call" | custom-call | flops 702021632 | bytes 8388608 | tf_op jit(solution)/shard_map/late/pallas_call | solution.py:223
  67.8 1.5 %collective-permute-start.13 = (f32[1,896]{1,0:T(1,128)S(1)}, f32[1,896]{1,0:T(1,128)S(1)}, u32[]{:S(2)}, u32[]{:S(2)}) collective-permute-start(f32[1,896]{1,0:T(1,128)S(1)} %get-tuple-element.84), channel_id=1, source_target_pairs={{0,2},{1,3},{2,4},{3,5},{4,6},{5,7},{6,1},{7,0},{8,10},{9,11},{10,... | collective-permute-start | bytes 10760 | tf_op jit(solution)/shard_map/ppermute | solution.py:330
  69.4 1.7 %collective-permute-start.14 = (f32[1,896]{1,0:T(1,128)S(1)}, f32[1,896]{1,0:T(1,128)S(1)}, u32[]{:S(2)}, u32[]{:S(2)}) collective-permute-start(f32[1,896]{1,0:T(1,128)S(1)} %get-tuple-element.85), channel_id=1, source_target_pairs={{0,6},{1,7},{2,1},{3,0},{4,3},{5,2},{6,5},{7,4},{8,14},{9,15},{10,... | collective-permute-start | bytes 10760 | tf_op jit(solution)/shard_map/ppermute | solution.py:330
  71.0 1.1 %collective-permute-done.13.a_ref = f32[1,896]{1,0:T(1,128)S(1)} collective-permute-done((f32[1,896]{1,0:T(1,128)S(1)}, f32[1,896]{1,0:T(1,128)S(1)}, u32[]{:S(2)}, u32[]{:S(2)}) %collective-permute-start.13) | collective-permute-done | bytes 3616 | tf_op jit(solution)/shard_map/ppermute | solution.py:330
  72.1 0.3 collective-permute-done.14.b_ref
  72.4 0.7 join.3
  73.1 3.8 %all-to-all-start.3 = ((f32[16,1,128]{2,1,0:T(1,128)}), f32[16,1,128]{2,1,0:T(1,128)S(1)}, u32[]{:S(2)}, u32[]{:S(2)}) async-start(f32[16,1,128]{2,1,0:T(1,128)} %bitcast.12), calls=%async_computation.3 | async-start | bytes 16384 | tf_op jit(solution)/shard_map/all_to_all | solution.py:340
  77.0 7.6 %all-to-all-done.3 = f32[16,1,128]{2,1,0:T(1,128)S(1)} async-done(((f32[16,1,128]{2,1,0:T(1,128)}), f32[16,1,128]{2,1,0:T(1,128)S(1)}, u32[]{:S(2)}, u32[]{:S(2)}) %all-to-all-start.3) | async-done | bytes 8224 | tf_op jit(solution)/shard_map/all_to_all | solution.py:340
  84.5 0.7 pick.3
  85.3 0.0 copy-done
  85.3 0.0 copy-done.9
  (1 shorter events, 0.0 us)
Async XLA Ops:
  26.3 40.1 %copy-start.1 = (bf16[16,32,1024]{2,1,0:T(8,128)(2,1)}, bf16[16,32,1024]{2,1,0:T(8,128)(2,1)S(1)}, u32[]{:S(2)}) copy-start(bf16[16,32,1024]{2,1,0:T(8,128)(2,1)S(1)} %all_to_all.19) | copy-start | bytes 3145732
  26.3 26.5 %collective-permute-start.8 = (bf16[512,1024]{1,0:T(8,128)(2,1)S(1)}, bf16[512,1024]{1,0:T(8,128)(2,1)S(1)}, u32[]{:S(2)}, u32[]{:S(2)}) collective-permute-start(bf16[512,1024]{1,0:T(8,128)(2,1)S(1)} %bitcast.22), channel_id=1, source_target_pairs={{6,0},{7,1},{1,2},{0,3},{3,4},{2,5},{5,6},{4,7},{14,8},{15,9},{9,1... | collective-permute-start | bytes 3145736 | tf_op jit(solution)/shard_map/ppermute | solution.py:330
  26.4 26.5 %collective-permute-start.7 = (bf16[512,1024]{1,0:T(8,128)(2,1)S(1)}, bf16[512,1024]{1,0:T(8,128)(2,1)S(1)}, u32[]{:S(2)}, u32[]{:S(2)}) collective-permute-start(bf16[512,1024]{1,0:T(8,128)(2,1)S(1)} %bitcast.23), channel_id=1, source_target_pairs={{2,0},{3,1},{4,2},{5,3},{6,4},{7,5},{1,6},{0,7},{10,8},{11,9},{12,... | collective-permute-start | bytes 3145736 | tf_op jit(solution)/shard_map/ppermute | solution.py:330
  28.5 24.4 %collective-permute-start.6 = (bf16[512,1024]{1,0:T(8,128)(2,1)S(1)}, bf16[512,1024]{1,0:T(8,128)(2,1)S(1)}, u32[]{:S(2)}, u32[]{:S(2)}) collective-permute-start(bf16[512,1024]{1,0:T(8,128)(2,1)S(1)} %bitcast.24), channel_id=1, source_target_pairs={{0,1},{1,0},{2,3},{3,2},{4,5},{5,4},{6,7},{7,6},{8,9},{9,8},{10,11... | collective-permute-start | bytes 3145736 | tf_op jit(solution)/shard_map/ppermute | solution.py:330
  52.8 13.6 %copy-start.3 = (bf16[512,1024]{1,0:T(8,128)(2,1)}, bf16[512,1024]{1,0:T(8,128)(2,1)S(1)}, u32[]{:S(2)}) copy-start(bf16[512,1024]{1,0:T(8,128)(2,1)S(1)} %collective-permute-done.8.refs_5_) | copy-start | bytes 3145732
  52.8 13.6 %copy-start.5 = (bf16[512,1024]{1,0:T(8,128)(2,1)}, bf16[512,1024]{1,0:T(8,128)(2,1)S(1)}, u32[]{:S(2)}) copy-start(bf16[512,1024]{1,0:T(8,128)(2,1)S(1)} %collective-permute-done.7.refs_4_) | copy-start | bytes 3145732
  52.9 13.6 %copy-start.7 = (bf16[512,1024]{1,0:T(8,128)(2,1)}, bf16[512,1024]{1,0:T(8,128)(2,1)S(1)}, u32[]{:S(2)}) copy-start(bf16[512,1024]{1,0:T(8,128)(2,1)S(1)} %collective-permute-done.6.refs_2_) | copy-start | bytes 3145732
  52.9 3.2 %collective-permute-start.9 = (bf16[208,1024]{1,0:T(8,128)(2,1)S(1)}, bf16[208,1024]{1,0:T(8,128)(2,1)S(1)}, u32[]{:S(2)}, u32[]{:S(2)}) collective-permute-start(bf16[208,1024]{1,0:T(8,128)(2,1)S(1)} %get-tuple-element.75.refs_1_), channel_id=1, source_target_pairs={{0,1},{1,0},{2,3},{3,2},{4,5},{5,4},{6,7},{7,6},{8,9},{9,8},{10,11... | collective-permute-start | bytes 1277960 | tf_op jit(solution)/shard_map/ppermute | solution.py:330
  53.0 13.4 %collective-permute-start.11 = (bf16[208,1024]{1,0:T(8,128)(2,1)S(1)}, bf16[208,1024]{1,0:T(8,128)(2,1)S(1)}, u32[]{:S(2)}, u32[]{:S(2)}) collective-permute-start(bf16[208,1024]{1,0:T(8,128)(2,1)S(1)} %get-tuple-element.75.refs_1_), channel_id=1, source_target_pairs={{6,0},{7,1},{1,2},{0,3},{3,4},{2,5},{5,6},{4,7},{14,8},{15,9},{9,1... | collective-permute-start | bytes 1277960 | tf_op jit(solution)/shard_map/ppermute | solution.py:330
  53.9 12.5 %collective-permute-start.10 = (bf16[208,1024]{1,0:T(8,128)(2,1)S(1)}, bf16[208,1024]{1,0:T(8,128)(2,1)S(1)}, u32[]{:S(2)}, u32[]{:S(2)}) collective-permute-start(bf16[208,1024]{1,0:T(8,128)(2,1)S(1)} %get-tuple-element.75.refs_1_), channel_id=1, source_target_pairs={{2,0},{3,1},{4,2},{5,3},{6,4},{7,5},{1,6},{0,7},{10,8},{11,9},{12,... | collective-permute-start | bytes 1277960 | tf_op jit(solution)/shard_map/ppermute | solution.py:330
  61.6 4.8 %collective-permute-start.12 = (f32[1,896]{1,0:T(1,128)S(1)}, f32[1,896]{1,0:T(1,128)S(1)}, u32[]{:S(2)}, u32[]{:S(2)}) collective-permute-start(f32[1,896]{1,0:T(1,128)S(1)} %get-tuple-element.80), channel_id=1, source_target_pairs={{0,1},{1,0},{2,3},{3,2},{4,5},{5,4},{6,7},{7,6},{8,9},{9,8},{10,11... | collective-permute-start | bytes 10760 | tf_op jit(solution)/shard_map/ppermute | solution.py:330
  66.4 18.8 %copy-start = (f32[512,1024]{1,0:T(8,128)S(1)}, f32[512,1024]{1,0:T(8,128)}, u32[]{:S(2)}) copy-start(f32[512,1024]{1,0:T(8,128)} %x_hbm.1) | copy-start | bytes 6291460
  66.5 18.8 %copy-start.9 = (s32[512]{0:T(512)S(1)}, s32[512]{0:T(512)}, u32[]{:S(2)}) copy-start(s32[512]{0:T(512)} %param.5) | copy-start | bytes 6148
  67.8 4.3 %collective-permute-start.13 = (f32[1,896]{1,0:T(1,128)S(1)}, f32[1,896]{1,0:T(1,128)S(1)}, u32[]{:S(2)}, u32[]{:S(2)}) collective-permute-start(f32[1,896]{1,0:T(1,128)S(1)} %get-tuple-element.84), channel_id=1, source_target_pairs={{0,2},{1,3},{2,4},{3,5},{4,6},{5,7},{6,1},{7,0},{8,10},{9,11},{10,... | collective-permute-start | bytes 10760 | tf_op jit(solution)/shard_map/ppermute | solution.py:330
  69.4 3.0 %collective-permute-start.14 = (f32[1,896]{1,0:T(1,128)S(1)}, f32[1,896]{1,0:T(1,128)S(1)}, u32[]{:S(2)}, u32[]{:S(2)}) collective-permute-start(f32[1,896]{1,0:T(1,128)S(1)} %get-tuple-element.85), channel_id=1, source_target_pairs={{0,6},{1,7},{2,1},{3,0},{4,3},{5,2},{6,5},{7,4},{8,14},{9,15},{10,... | collective-permute-start | bytes 10760 | tf_op jit(solution)/shard_map/ppermute | solution.py:330
  73.1 11.4 %all-to-all-start.3 = ((f32[16,1,128]{2,1,0:T(1,128)}), f32[16,1,128]{2,1,0:T(1,128)S(1)}, u32[]{:S(2)}, u32[]{:S(2)}) async-start(f32[16,1,128]{2,1,0:T(1,128)} %bitcast.12), calls=%async_computation.3 | async-start | bytes 16384 | tf_op jit(solution)/shard_map/all_to_all | solution.py:340
